TPU v7x, 256 devices: a whole 4x4x8 slice. The times are simulated.
256 devices in a mesh: clip: 16 (over x, y_lo, core), copy: 16 (over z, y_hi).
Axes of the slice: x: 4, y: 4 (y_hi: 2, y_lo: 2; y = y_hi * 2 + y_lo), z: 8, core: 2. Of those that a mesh axis runs over, the one named last changes fastest.
Arguments:
- frames: bfloat16 [16, 256, 1024], P('clip', 'copy'), may hold values from -6 to 6
- targets: bfloat16 [16, 256, 1024], P('clip', 'copy'), may hold values from -6 to 6
- kept_index: int32 [16, 16, 128], P('clip', 'copy'), may hold values from 0 to 255, as said below
- kept_count: int32 [16, 16], P('clip', 'copy'), may hold values from 64 to 128, as said below
- fill_slot: int32 [16, 16, 256], P('clip', 'copy'), may hold values from 0 to 128, as said below
- norm_gain: float32 [1024], replicated, may hold values from 0.5 to 1.5
- w_qkv: bfloat16 [1024, 3072], P('clip'), may hold values from -8 to 8
- w_out: bfloat16 [1024, 1024], P('clip'), may hold values from -0.1875 to 0.1875
- mask_embed: bfloat16 [1024], replicated, may hold values from -4 to 4
- dec_kernel: float32 [7, 1024], replicated, may hold values from -2 to 2
Outputs:
- encoded: bfloat16 [16, 16, 128, 1024], P('clip', 'copy')
- grad_qkv: float32 [1024, 3072], P('clip', 'copy')
- grad_out: float32 [1024, 1024], P('clip', 'copy')
Inputs may be any that keep to these rules, and one draw needn't show every extreme that they name: `kept_count`: some copy of every clip keeps exactly 128 frames. `kept_index`: for each copy the first kept_count entries are the kept frame positions in rising order, the rest are other frames of the clip in rising order; no position repeats. `fill_slot`: a kept frame holds its row among the first kept_count entries of kept_index, every other frame holds 128.
All inputs are finite; a program needn't handle non-finite values.
Results may differ from a plain program's by a relative error of at most 0.017.
Values may be sent and summed in bfloat16 or wider, within the bound.
No kernel may reach another device: no remote copies, remote signals or barrier semaphores. Data moves between devices by JAX's collectives and lax.ppermute only.
A program may use at most 64 MiB of HBM per device.

v0:
```python
import jax
import jax.numpy as jnp
from jax import lax
from jax.sharding import PartitionSpec as P

HS = 64


NORM_EPSILON = 1e-05
MASKED_SCORE = -1e30


def layer_norm_rows(row_block, norm_gain):
    values = row_block.astype(jnp.float32)
    center = values - jnp.mean(values, axis=1, keepdims=True)
    spread = jnp.mean(center * center, axis=1, keepdims=True)
    return (center * lax.rsqrt(spread + NORM_EPSILON) * norm_gain[None, :]).astype(jnp.bfloat16)


def depthwise(field, dec_kernel, flipped):
    reach = dec_kernel.shape[0] // 2
    length = field.shape[0]
    padded = jnp.pad(field, ((reach, reach), (0, 0)))
    total = jnp.zeros_like(field)
    for tap_index in range(dec_kernel.shape[0]):
        begin = 2 * reach - tap_index if flipped else tap_index
        total = total + dec_kernel[tap_index][None, :] * padded[begin : begin + length]
    return total


def head_blocks(matrix, head_count, group_size):
    row_total = matrix.shape[0]
    return jnp.moveaxis(matrix.reshape(row_total, head_count // group_size, group_size, -1), 1, 0)


def head_rows(blocks):
    moved = jnp.moveaxis(blocks, 0, 1)
    return moved.reshape(moved.shape[0], -1)


def softmax_probs(query_block, key_block, live_keys, score_scale):
    scores = (
        jnp.einsum("qhd,khd->hqk", query_block, key_block, preferred_element_type=jnp.float32)
        * score_scale
    )
    scores = jnp.where(live_keys[None, None, :], scores, MASKED_SCORE)
    highest = jnp.max(scores, axis=-1, keepdims=True)
    raised = jnp.exp(scores - highest)
    return raised / jnp.sum(raised, axis=-1, keepdims=True)


def inner_rows(left, right):
    return lax.dot_general(
        left, right, (((0,), (0,)), ((), ())), preferred_element_type=jnp.float32
    )


def per_device(
    frames,
    targets,
    kept_index,
    kept_count,
    fill_slot,
    norm_gain,
    w_qkv,
    w_out,
    mask_embed,
    dec_kernel,
):
    clip_devices = lax.axis_size("clip")
    copy_devices = lax.axis_size("copy")
    kept_most = kept_index.shape[2]
    inner_width = w_out.shape[0] * clip_devices
    head_count = inner_width // HS
    group_size = 4
    score_scale = HS ** (-0.5)
    loss_scale = (kept_most * clip_devices * copy_devices) ** (-0.5)
    gathered_frames, gathered_targets = (
        lax.all_gather(frames, "copy", axis=1, tiled=True),
        lax.all_gather(targets, "copy", axis=1, tiled=True),
    )
    clip_targets = gathered_targets[0]
    clip_frames = gathered_frames[0]
    w_qkv_all, w_out_all = (
        lax.all_gather(w_qkv, "clip", axis=0, tiled=True),
        lax.all_gather(w_out, "clip", axis=0, tiled=True),
    )
    positions = kept_index[0, 0]
    kept_total = kept_count[0, 0]
    slot_map = fill_slot[0, 0]
    live_keys = jnp.arange(kept_most) < kept_total
    inputs = jnp.take(clip_frames, positions, axis=0)
    normed = layer_norm_rows(inputs, norm_gain)
    projected = jnp.dot(normed, w_qkv_all, preferred_element_type=jnp.float32).astype(jnp.bfloat16)
    query_blocks = head_blocks(projected[:, :inner_width], head_count, group_size)
    key_blocks = head_blocks(projected[:, inner_width : 2 * inner_width], head_count, group_size)
    value_blocks = head_blocks(projected[:, 2 * inner_width :], head_count, group_size)

    def forward_group(blocks):
        probs = softmax_probs(blocks[0], blocks[1], live_keys, score_scale)
        return jnp.einsum(
            "hqk,khd->qhd",
            probs.astype(jnp.bfloat16),
            blocks[2],
            preferred_element_type=jnp.float32,
        ).astype(jnp.bfloat16)

    context = head_rows(lax.map(forward_group, (query_blocks, key_blocks, value_blocks)))
    mixed = inputs.astype(jnp.float32) + jnp.dot(
        context, w_out_all, preferred_element_type=jnp.float32
    )
    encoded = jnp.where(live_keys[:, None], mixed, 0.0).astype(jnp.bfloat16)
    table = jnp.concatenate([encoded, mask_embed[None, :]], axis=0)
    filled = jnp.take(table, slot_map, axis=0)
    predicted = depthwise(filled.astype(jnp.float32), dec_kernel, False)
    masked_frames = slot_map == kept_most
    residue = predicted - clip_targets.astype(jnp.float32)
    error = jnp.where(masked_frames[:, None], residue, 0.0) * loss_scale
    dfilled = depthwise(error, dec_kernel, True)
    dencoded = jnp.where(live_keys[:, None], jnp.take(dfilled, positions, axis=0), 0.0).astype(
        jnp.bfloat16
    )
    dcontext = lax.dot_general(
        dencoded, w_out_all, (((1,), (1,)), ((), ())), preferred_element_type=jnp.float32
    ).astype(jnp.bfloat16)
    dcontext_blocks = head_blocks(dcontext, head_count, group_size)

    def backward_group(blocks):
        query_block, key_block, value_block, dcontext_block = blocks
        probs = softmax_probs(query_block, key_block, live_keys, score_scale)
        probs_low = probs.astype(jnp.bfloat16)
        dprobs = jnp.einsum(
            "qhd,khd->hqk", dcontext_block, value_block, preferred_element_type=jnp.float32
        )
        dvalues = jnp.einsum(
            "hqk,qhd->khd", probs_low, dcontext_block, preferred_element_type=jnp.float32
        )
        dscores = probs * (dprobs - jnp.sum(probs * dprobs, axis=-1, keepdims=True)) * score_scale
        dscores = dscores.astype(jnp.bfloat16)
        dqueries = jnp.einsum(
            "hqk,khd->qhd", dscores, key_block, preferred_element_type=jnp.float32
        )
        dkeys = jnp.einsum("hqk,qhd->khd", dscores, query_block, preferred_element_type=jnp.float32)
        return (dqueries, dkeys, dvalues)

    dquery_blocks, dkey_blocks, dvalue_blocks = lax.map(
        backward_group, (query_blocks, key_blocks, value_blocks, dcontext_blocks)
    )
    dprojected = jnp.concatenate(
        [head_rows(dquery_blocks), head_rows(dkey_blocks), head_rows(dvalue_blocks)], axis=1
    ).astype(jnp.bfloat16)
    output_part = lax.psum_scatter(
        inner_rows(context, dencoded).astype(jnp.bfloat16), "clip", scatter_dimension=0, tiled=True
    )
    project_part = lax.psum_scatter(
        inner_rows(normed, dprojected).astype(jnp.bfloat16), "clip", scatter_dimension=0, tiled=True
    )
    grad_qkv, grad_out = (
        lax.psum_scatter(project_part, "copy", scatter_dimension=1, tiled=True).astype(jnp.float32),
        lax.psum_scatter(output_part, "copy", scatter_dimension=1, tiled=True).astype(jnp.float32),
    )
    return (encoded[None, None], grad_qkv, grad_out)


def solution(mesh):
    in_specs = (
        P("clip", "copy", None),
        P("clip", "copy", None),
        P("clip", "copy", None),
        P("clip", "copy"),
        P("clip", "copy", None),
        P(),
        P("clip", None),
        P("clip", None),
        P(),
        P(),
    )
    out_specs = (P("clip", "copy", None, None), P("clip", "copy"), P("clip", "copy"))
    return jax.shard_map(
        per_device, mesh=mesh, in_specs=in_specs, out_specs=out_specs, check_vma=False
    )
```

profile of v0, /device:TPU:32, one launch (start us, length us, event | category | flops | bytes accessed | tf_op | source)
XLA Modules:
  0.0 683.5 jit_solution(8953151238436781517)
XLA Ops:
  8.0 0.7 all-gather.5.cloned.1.call-update
  10.1 45.6 %all_gather.12 = bf16[1,256,1024]{2,1,0:T(8,128)(2,1)S(1)} all-gather(bf16[1,16,1024]{2,1,0:T(8,128)(2,1)} %param.14), channel_id=1, replica_groups=mesh['clip'=16,'copy'=16] {'copy'}, dimensions={1}, use_global_device_ids=true | all-gather | bytes 557056 | tf_op jit(solution)/shard_map/all_gather | solution.py:79
  55.7 0.9 gather_fusion
  57.8 38.8 %all_gather.15 = bf16[1,256,1024]{2,1,0:T(8,128)(2,1)S(1)} all-gather(bf16[1,16,1024]{2,1,0:T(8,128)(2,1)S(1)} %copy-done.11), channel_id=1, replica_groups=mesh['clip'=16,'copy'=16] {'copy'}, dimensions={1}, use_global_device_ids=true | all-gather | bytes 557056 | tf_op jit(solution)/shard_map/all_gather | solution.py:80
  96.6 3.9 convolution_convert_fusion.2
  101.2 5.7 while.26
  107.6 2.1 fusion.112
  110.4 1.2 gather_fusion.1
  111.8 1.0 broadcast_multiply_fusion
  112.8 0.9 multiply_add_fusion
  113.7 0.9 gather_fusion.2
  114.5 3.1 convolution_convert_fusion.3
  117.6 1.6 convolution_convert_fusion.4
  119.2 1.2 copy.36
  120.5 8.7 %while.27 = (s32[]{:T(128)}, bf16[4,128,4,64]{1,3,2,0:T(8,128)(2,1)S(1)}, bf16[4,128,4,64]{1,3,2,0:T(8,128)(2,1)S(1)}, bf16[4,128,4,64]{1,3,2,0:T(8,128)(2,1)S(1...) while((s32[]{:T(128)}, ...), condition=%wide.region_10.11_spmd.clone, body=%wide.region_6.10_spmd.clone.sunk | while | flops 51841152 | bytes 3624169 | solution.py:146
  129.3 4.6 convolution_convert_fusion.1
  134.0 53.0 %reduce-scatter.11.cloned.1.call-done = bf16[64,1024]{1,0:T(8,128)(2,1)} async-done(((bf16[1024,1024]{1,0:T(8,128)(2,1)}), bf16[64,1024]{1,0:T(8,128)(2,1)}) %reduce-scatter.11.cloned.1.call-update) | async-done | bytes 131088 | tf_op jit(solution)/shard_map/reduce_scatter | solution.py:152
  186.9 1.7 copy.43
  188.8 76.8 %reduce-scatter.9.cloned.1.call-done = bf16[64,3072]{1,0:T(8,128)(2,1)} async-done(((bf16[1024,3072]{1,0:T(8,128)(2,1)}), bf16[64,3072]{1,0:T(8,128)(2,1)}) %reduce-scatter.9.cloned.1.call-update) | async-done | bytes 393232 | tf_op jit(solution)/shard_map/reduce_scatter | solution.py:155
  265.6 2.1 copy.41
  267.8 202.5 %reduce-scatter.15.cloned.1.call-done = bf16[64,64]{1,0:T(8,128)(2,1)} async-done(((bf16[1024,64]{1,0:T(8,128)(2,1)}), bf16[64,64]{1,0:T(8,128)(2,1)}) %reduce-scatter.15.cloned.1.call-update) | async-done | bytes 8208
  470.3 0.8 copy.44
  471.7 203.3 %reduce-scatter.13.cloned.1.call-done = bf16[192,64]{1,0:T(8,128)(2,1)} async-done(((bf16[3072,64]{1,0:T(8,128)(2,1)}), bf16[192,64]{1,0:T(8,128)(2,1)}) %reduce-scatter.13.cloned.1.call-update) | async-done | bytes 24592
  675.1 0.9 copy.42
  (105 shorter events, 20.4 us)
Async XLA Ops:
  7.2 50.2 %copy-start.14 = (bf16[1024]{0:T(1024)(128)(2,1)S(1)}, bf16[1024]{0:T(1024)(128)(2,1)}, u32[]{:S(2)}) copy-start(bf16[1024]{0:T(1024)(128)(2,1)} %param.22) | copy-start | bytes 6148
  7.2 50.2 %copy-start.13 = (s32[1,1,256]{2,1,0:T(1,128)S(1)}, s32[1,1,256]{2,1,0:T(1,128)}, u32[]{:S(2)}) copy-start(s32[1,1,256]{2,1,0:T(1,128)} %param.18) | copy-start | bytes 3076
  7.2 50.5 %copy-start.12 = (f32[7,1024]{1,0:T(8,128)S(1)}, f32[7,1024]{1,0:T(8,128)}, u32[]{:S(2)}) copy-start(f32[7,1024]{1,0:T(8,128)} %param.23) | copy-start | bytes 86020
  7.2 50.6 %copy-start.11 = (bf16[1,16,1024]{2,1,0:T(8,128)(2,1)S(1)}, bf16[1,16,1024]{2,1,0:T(8,128)(2,1)}, u32[]{:S(2)}) copy-start(bf16[1,16,1024]{2,1,0:T(8,128)(2,1)} %param.15) | copy-start | bytes 98308
  7.2 89.4 %all-gather.3.cloned.1.call-start = ((), (), s32[]{:S(2)}) async-start(), calls=%async_computation.4 | async-start | bytes 6684672 | tf_op jit(solution)/shard_map/all_gather | solution.py:85
  7.9 88.7 %copy-start.3 = (f32[1024]{0:T(1024)S(1)}, f32[1024]{0:T(1024)}, u32[]{:S(2)}) copy-start(f32[1024]{0:T(1024)} %param.19) | copy-start | bytes 12292
  8.0 98.9 %all-gather.5.cloned.1.call-start = ((), (), s32[]{:S(2)}) async-start(), calls=%async_computation.5 | async-start | bytes 2228224 | tf_op jit(solution)/shard_map/all_gather | solution.py:86
  8.7 178.2 %reduce-scatter.11.cloned.1.call-start = ((), (), s32[]{:S(2)}) async-start(), calls=%async_computation.7 | async-start | bytes 2228224 | tf_op jit(solution)/shard_map/reduce_scatter | solution.py:152
  106.8 0.7 copy-start.1
  106.8 0.8 copy-start.7
  106.8 2.9 copy-start.9
  109.7 0.7 copy-start.2
  113.7 4.0 copy-start
  117.6 2.9 copy-start.4
  117.6 2.9 copy-start.5
  119.2 1.3 copy-start.6
  119.2 1.3 copy-start.8
  119.2 1.3 copy-start.10
  120.4 145.2 %reduce-scatter.9.cloned.1.call-start = ((), (), s32[]{:S(2)}) async-start(), calls=%async_computation.6 | async-start | bytes 6684672 | tf_op jit(solution)/shard_map/reduce_scatter | solution.py:155
  133.9 336.4 %reduce-scatter.15.cloned.1.call-start = ((), (), s32[]{:S(2)}) async-start(), calls=%async_computation.9 | async-start | bytes 278528
  188.7 486.4 %reduce-scatter.13.cloned.1.call-start = ((), (), s32[]{:S(2)}) async-start(), calls=%async_computation.8 | async-start | bytes 835584
Sparse Core Ops, SparseCore 0:
  9.9 57.2 all-gather.2
  69.0 37.6 all-gather.4
  120.5 66.3 reduce-scatter.10
  189.3 76.2 reduce-scatter.8
  269.2 201.0 reduce-scatter.14
  474.5 200.5 reduce-scatter.12
where the time goes:
time: 685 us; the launch traced here: 683 us
  waiting for transfers between devices  537 us (78%)
  blocking collectives  84.4 us (12%)
  matrix products  24.1 us (4%)
  between operations  15.1 us (2%)
  local copies, waits for them, and re-layouts  11.8 us (2%)
  other arithmetic  10.3 us (2%)
    unnamed x8, waiting for transfers between devices  407 us
    reduce_scatter x1, waiting for transfers between devices, per_device(): lax.psum_scatter(inner_rows(normed, dprojected).astype(jnp.bfloat16), 'cl...  76.8 us
    reduce_scatter x1, waiting for transfers between devices, per_device(): lax.psum_scatter(inner_rows(context, dencoded).astype(jnp.bfloat16), 'cli...  53 us
    all_gather x1, blocking collectives, per_device(): lax.all_gather(frames, 'copy', axis=1, tiled=True)  45.6 us
    all_gather x1, blocking collectives, per_device(): lax.all_gather(targets, 'copy', axis=1, tiled=True)  38.8 us
  transfers between devices with their start and end apart: 6, of which 4 were waited for; matrix products, arithmetic and copies ran while one was open for 5% of the time, Pallas kernels for 0%

commit v1 on v0

v1 whole, which is shorter than its diff:
```python
import jax
import jax.numpy as jnp
from jax import lax
from jax.experimental import pallas as pl
from jax.experimental.pallas import tpu as pltpu
from jax.sharding import Mesh
from jax.sharding import PartitionSpec as P


D = 1024
H = 16
HS = 64
L = 256
KMAX = 128
KW = 7
CLIPS = 16
COPIES = 16
QALL = COPIES * KMAX
NORM_EPSILON = 1e-05
MASKED_SCORE = -1e30
SCORE_SCALE = HS**-0.5
LOSS_SCALE = (KMAX * CLIPS * COPIES) ** -0.5
PAD = 8
LANES = 256
VMEM_LIMIT = 48 * 1024 * 1024

CLIP = ("x", "y_lo", "core")
COPY = ("z", "y_hi")
F32 = jnp.float32
BF16 = jnp.bfloat16


def mm(left, right):
    return jnp.dot(left, right, preferred_element_type=F32)


def mm_nt(left, right):
    return lax.dot_general(left, right, (((1,), (1,)), ((), ())), preferred_element_type=F32)


def whole(count):
    return [pl.BlockSpec(memory_space=pltpu.VMEM)] * count


def params():
    return pltpu.CompilerParams(vmem_limit_bytes=VMEM_LIMIT)


def forward_kernel(
    got_ref, w_ref, gain_ref, ctx_ref, probs_ref, pick_ref, query_ref, key_ref, value_ref, normed_ref, wv_ref
):
    values = got_ref[:, :D].astype(F32)
    center = values - jnp.mean(values, axis=1, keepdims=True)
    spread = jnp.mean(center * center, axis=1, keepdims=True)
    normed = (center * lax.rsqrt(spread + NORM_EPSILON) * gain_ref[...]).astype(BF16)
    normed_ref[...] = normed.T
    for c in range(CLIPS):
        wv_ref[c * HS : c * HS + HS // 2, :] = w_ref[c, HS:, :HS]
        wv_ref[c * HS + HS // 2 : (c + 1) * HS, :] = w_ref[c, HS:, HS:]
    qk = mm(normed, w_ref[:, :HS, :].reshape(D, 2 * HS)).astype(BF16)
    v = mm(normed, wv_ref[...]).astype(BF16)
    qk_t = qk.astype(F32).T
    query_t = (qk_t[:HS] * SCORE_SCALE).astype(BF16)
    key = qk[:, HS:]
    key_ref[...] = qk_t[HS:].astype(BF16)
    value_ref[...] = v
    value_t = v.astype(F32).T.astype(BF16)
    rows = lax.broadcasted_iota(jnp.int32, (L, KMAX), 0).astype(F32)
    for m in range(COPIES):
        lanes = slice(m * KMAX, (m + 1) * KMAX)
        index = got_ref[m * 16 : (m + 1) * 16, D:].astype(F32)[:1]
        hit = jnp.where(rows == index, 1.0, 0.0)
        pick = hit.astype(BF16)
        pick_ref[:, lanes] = pick
        queries = mm(query_t, pick).astype(BF16)
        query_ref[:, lanes] = queries
        kept = jnp.sum(hit, axis=1, keepdims=True)
        scores = jnp.where(kept > 0.5, mm(key, queries), MASKED_SCORE)
        raised = jnp.exp(scores - jnp.max(scores, axis=0, keepdims=True))
        probs = raised / jnp.sum(raised, axis=0, keepdims=True)
        probs_ref[:, lanes] = probs
        ctx_ref[m] = mm(value_t, probs.astype(BF16)).astype(BF16)


def forward(got, weights, gain):
    return pl.pallas_call(
        forward_kernel,
        out_shape=[
            jax.ShapeDtypeStruct((COPIES, HS, KMAX), BF16),
            jax.ShapeDtypeStruct((L, QALL), F32),
            jax.ShapeDtypeStruct((L, QALL), BF16),
            jax.ShapeDtypeStruct((HS, QALL), BF16),
            jax.ShapeDtypeStruct((HS, L), BF16),
            jax.ShapeDtypeStruct((L, HS), BF16),
            jax.ShapeDtypeStruct((D, L), BF16),
        ],
        in_specs=whole(3),
        out_specs=whole(7),
        scratch_shapes=[pltpu.VMEM((D, HS), BF16)],
        compiler_params=params(),
        name="forward",
    )(got, weights, gain)


def decoder_kernel(
    count_ref, ctx_ref, got_ref, w_ref, targets_ref, index_ref, embed_ref, taps_ref, encoded_ref, dctx_ref, denc_ref, field_ref
):
    live = lax.broadcasted_iota(jnp.int32, (KMAX, 1), 0) < count_ref[0]
    rows = lax.broadcasted_iota(jnp.int32, (L, KMAX), 0).astype(F32)
    hit = jnp.where(rows == index_ref[:1].astype(F32), 1.0, 0.0)
    masked = 1.0 - jnp.sum(hit, axis=1, keepdims=True)
    place = hit.astype(BF16)
    pick = hit.T.astype(BF16)
    ctx = ctx_ref[...].T
    reach = KW // 2
    field_ref[:PAD] = jnp.zeros((PAD, LANES), F32)
    field_ref[PAD + L :] = jnp.zeros((PAD, LANES), F32)
    for c in range(D // LANES):
        lanes = slice(c * LANES, (c + 1) * LANES)
        mixed = mm(pick, got_ref[:, lanes]) + mm(ctx, w_ref[:, lanes])
        encoded = jnp.where(live, mixed, 0.0).astype(BF16)
        encoded_ref[:, lanes] = encoded
        field_ref[PAD : PAD + L] = mm(place, encoded) + masked * embed_ref[:, lanes].astype(F32)
        predicted = taps_ref[:1, lanes] * field_ref[PAD - reach : PAD - reach + L]
        for t in range(1, KW):
            begin = PAD - reach + t
            predicted = predicted + taps_ref[t : t + 1, lanes] * field_ref[begin : begin + L]
        error = masked * (predicted - targets_ref[:, lanes].astype(F32)) * LOSS_SCALE
        field_ref[PAD : PAD + L] = error
        dfilled = taps_ref[:1, lanes] * field_ref[PAD + reach : PAD + reach + L]
        for t in range(1, KW):
            begin = PAD + reach - t
            dfilled = dfilled + taps_ref[t : t + 1, lanes] * field_ref[begin : begin + L]
        denc_ref[:, lanes] = mm(pick, dfilled.astype(BF16)).astype(BF16)
    dctx_ref[...] = mm_nt(w_ref[...], denc_ref[...]).astype(BF16)


def decoder(count, ctx, got, w_out, targets, index, embed, taps):
    return pl.pallas_call(
        decoder_kernel,
        out_shape=[
            jax.ShapeDtypeStruct((KMAX, D), BF16),
            jax.ShapeDtypeStruct((D, KMAX), BF16),
            jax.ShapeDtypeStruct((KMAX, D), BF16),
        ],
        in_specs=[pl.BlockSpec(memory_space=pltpu.SMEM)] + whole(7),
        out_specs=whole(3),
        scratch_shapes=[pltpu.VMEM((L + 2 * PAD, LANES), F32)],
        compiler_params=params(),
        name="decoder",
    )(count, ctx, got, w_out, targets, index, embed, taps)


def out_grad_kernel(core_ref, ctx_ref, denc_ref, out_ref):
    half_rows = HS // 2
    for c in range(CLIPS):
        half = jnp.where(core_ref[0] == c % 2, 0, 1)
        block = mm(ctx_ref[c * HS : (c + 1) * HS, :], denc_ref[...])
        upper, lower = block[:half_rows], block[half_rows:]
        for a in range(D // 128):
            lanes = slice(a * 128, (a + 1) * 128)
            first, second = upper[:, lanes], lower[:, lanes]
            even = jnp.concatenate([first[:, :HS], second[:, :HS]], axis=1)
            odd = jnp.concatenate([first[:, HS:], second[:, HS:]], axis=1)
            out_ref[half, c // 2, 2 * a] = even.astype(BF16)
            out_ref[half, c // 2, 2 * a + 1] = odd.astype(BF16)


def out_grad(core, ctx, denc):
    return pl.pallas_call(
        out_grad_kernel,
        out_shape=jax.ShapeDtypeStruct((2, CLIPS // 2, COPIES, HS // 2, 2 * HS), BF16),
        in_specs=[pl.BlockSpec(memory_space=pltpu.SMEM)] + whole(2),
        out_specs=pl.BlockSpec(memory_space=pltpu.VMEM),
        compiler_params=params(),
        name="out_grad",
    )(core, ctx, denc)


def backward_kernel(
    dctx_ref, probs_ref, pick_ref, query_ref, key_ref, value_ref, normed_ref, out_ref, dctx_all, low_all, ds_all, dq_all
):
    key_t = key_ref[...]
    value = value_ref[...]
    for m in range(COPIES):
        lanes = slice(m * KMAX, (m + 1) * KMAX)
        dctx = dctx_ref[m]
        dctx_all[:, lanes] = dctx
        probs = probs_ref[:, lanes]
        low_all[:, lanes] = probs.astype(BF16)
        dprobs = mm(value, dctx)
        dscores = probs * (dprobs - jnp.sum(probs * dprobs, axis=0, keepdims=True))
        dscores = dscores.astype(BF16)
        ds_all[:, lanes] = dscores
        dq_all[:, lanes] = (mm(key_t, dscores) * SCORE_SCALE).astype(BF16)
    dvalue = mm_nt(dctx_all[...], low_all[...]).astype(BF16)
    dkey = mm_nt(query_ref[...], ds_all[...]).astype(BF16)
    dquery = mm_nt(dq_all[...], pick_ref[...]).astype(BF16)
    normed_t = normed_ref[...]
    grad_qk = mm_nt(normed_t, jnp.concatenate([dquery, dkey], axis=0)).astype(BF16)
    grad_v = mm_nt(normed_t, dvalue).astype(BF16)
    for c in range(CLIPS):
        out_ref[c, :HS, :] = grad_qk[c * HS : (c + 1) * HS]
        out_ref[c, HS:, :HS] = grad_v[c * HS : c * HS + HS // 2]
        out_ref[c, HS:, HS:] = grad_v[c * HS + HS // 2 : (c + 1) * HS]


def backward(dctx, probs, pick, query, key, value, normed):
    return pl.pallas_call(
        backward_kernel,
        out_shape=jax.ShapeDtypeStruct((CLIPS, HS + HS // 2, 2 * HS), BF16),
        in_specs=whole(7),
        out_specs=pl.BlockSpec(memory_space=pltpu.VMEM),
        scratch_shapes=[
            pltpu.VMEM((HS, QALL), BF16),
            pltpu.VMEM((L, QALL), BF16),
            pltpu.VMEM((L, QALL), BF16),
            pltpu.VMEM((HS, QALL), BF16),
        ],
        compiler_params=params(),
        name="backward",
    )(dctx, probs, pick, query, key, value, normed)


def swap(array, axes):
    return lax.all_to_all(array, axes, 0, 0, tiled=True)


def side_by_side(block):
    half = block.shape[0] // 2
    return jnp.concatenate([block[:half], block[half:]], axis=1)


def stacked(block):
    half = block.shape[-1] // 2
    return jnp.concatenate([block[..., :half], block[..., half:]], axis=-2)


def per_device(
    frames,
    targets,
    kept_index,
    kept_count,
    fill_slot,
    norm_gain,
    w_qkv,
    w_out,
    mask_embed,
    dec_kernel,
):
    copy_at = lax.axis_index(COPY)
    core = lax.axis_index("core")
    count = kept_count[0]
    live = jnp.arange(KMAX)[None, :] < count[0]
    index = jnp.broadcast_to(jnp.where(live, kept_index[0], L).astype(BF16), (16, KMAX))

    packed = jnp.concatenate([frames[0], index], axis=1)
    got = swap(jnp.broadcast_to(packed[None], (COPIES,) + packed.shape), COPY).reshape(L, D + KMAX)

    wq, wk, wv = [
        lax.dynamic_slice(w_qkv, (0, part * D + copy_at * HS), (HS, HS)) for part in range(3)
    ]
    weights = jnp.concatenate([jnp.concatenate([wq, wk], axis=1), side_by_side(wv)], axis=0)
    weights = lax.all_gather(weights, CLIP, axis=0)
    w_out_all = lax.all_gather(w_out, CLIP, axis=0, tiled=True)
    targets_all = lax.all_gather(lax.all_gather(targets[0], "y_hi", axis=0), "z", axis=0)
    targets_all = targets_all.reshape(L, D)

    ctx, probs, pick, query, key, value, normed = forward(got, weights, norm_gain[None, :])
    ctx = swap(ctx, COPY).reshape(D, KMAX)
    encoded, dctx, denc = decoder(
        count, ctx, got, w_out_all, targets_all, index, mask_embed[None, :], dec_kernel
    )
    dctx = swap(dctx.reshape(H, HS, KMAX), COPY)

    out_term = out_grad(core.reshape(1), ctx, denc)
    other = lax.ppermute(out_term[1], "core", [(0, 1), (1, 0)])
    out_term = (out_term[0].astype(F32) + other.astype(F32)).astype(BF16)
    out_term = swap(out_term, ("x", "y_lo"))
    out_term = jnp.sum(out_term.astype(F32), axis=0).astype(BF16)

    term = swap(backward(dctx, probs, pick, query, key, value, normed), CLIP)
    term = jnp.sum(term.astype(F32), axis=0).astype(BF16)
    to = jnp.arange(COPIES)[:, None, None]
    zero = jnp.zeros((HS // 2, 2 * HS), BF16)
    pieces = (side_by_side(term[:HS, :HS]), side_by_side(term[:HS, HS:]), term[HS:])
    sent = zero[None]
    for part, piece in enumerate(pieces):
        sent = jnp.where(to == (part * H + copy_at) // 3, piece[None], sent)
    last = swap(jnp.concatenate([out_term, sent], axis=1), COPY)
    grad_out = stacked(jnp.sum(last[:, : HS // 2].astype(F32), axis=0))
    blocks = [
        stacked(lax.dynamic_index_in_dim(last, (3 * copy_at + i) % COPIES, 0, False)[HS // 2 :])
        for i in range(3)
    ]
    grad_qkv = jnp.concatenate(blocks, axis=1).astype(F32)
    return (encoded[None, None], grad_qkv, grad_out)


def solution(mesh):
    fine = Mesh(mesh.devices.reshape(4, 2, 2, 8, 2), ("x", "y_lo", "core", "z", "y_hi"))
    in_specs = (
        P(CLIP, COPY, None),
        P(CLIP, COPY, None),
        P(CLIP, COPY, None),
        P(CLIP, COPY),
        P(CLIP, COPY, None),
        P(),
        P(CLIP, None),
        P(CLIP, None),
        P(),
        P(),
    )
    out_specs = (P(CLIP, COPY, None, None), P(CLIP, COPY), P(CLIP, COPY))
    return jax.shard_map(
        per_device, mesh=fine, in_specs=in_specs, out_specs=out_specs, check_vma=False
    )
```

time: 685 us -> 198 us (0.29)
  waiting for transfers between devices: 537 us -> 34.7 us
  starting transfers between devices: 0.24 us -> 33.7 us
  matrix products: 24.1 us -> 0 us
  Pallas kernels: 0 us -> 19.9 us
    unnamed x8 -> x1, waiting for transfers between devices: 407 us -> 0.68 us
    reduce_scatter x2 -> x0, waiting for transfers between devices: 130 us -> none  [the longest x1 76.8 us: per_device(): lax.psum_scatter(inner_rows(normed, dprojected).astype(jnp.bfloat16), 'cl...]
    all_to_all x0 -> x5, waiting for transfers between devices: none -> 34 us  [swap(): return lax.all_to_all(array, axes, 0, 0, tiled=True)]
    all_to_all x0 -> x5, starting transfers between devices: none -> 33.7 us  [swap(): return lax.all_to_all(array, axes, 0, 0, tiled=True)]
    all_gather x2 -> x3, blocking collectives: 84.4 us -> 55.6 us  [the longest x1 25.7 us: per_device(): lax.all_gather(lax.all_gather(targets[0], 'y_hi', axis=0), 'z', axis=0)]
    all_to_all x0 -> x1, blocking collectives: none -> 22.7 us  [swap(): return lax.all_to_all(array, axes, 0, 0, tiled=True)]
    dot_general x25 -> x0, matrix products: 21.6 us -> none  [the longest x2 7.72 us: inner_rows(): lax.dot_general(left, right, (((0,), (0,)), ((), ())), preferred_element_...]
    pallas_call x0 -> x4, Pallas kernels: none -> 19.9 us  [the longest x1 7.69 us: forward(): pl.pallas_call(forward_kernel, out_shape=[jax.ShapeDtypeStruct((COPIES, H...]
  transfers between devices with their start and end apart: 6 -> 7, of which waited for: 4 -> 3; matrix products, arithmetic and copies ran while one was open for 5% -> 3% of each run, Pallas kernels for 0% -> 7%
where the time goes in v1:
time: 198 us; the launch traced here: 196 us
  blocking collectives  78.2 us (39%)
  waiting for transfers between devices  34.7 us (18%)
  starting transfers between devices  33.7 us (17%)
  Pallas kernels  19.9 us (10%)
  between operations  14.9 us (8%)
  local copies, waits for them, and re-layouts  8.39 us (4%)
  other arithmetic  6.51 us (3%)
    all_to_all x5, waiting for transfers between devices, swap(): return lax.all_to_all(array, axes, 0, 0, tiled=True)  34 us
    all_to_all x5, starting transfers between devices, swap(): return lax.all_to_all(array, axes, 0, 0, tiled=True)  33.7 us
    all_gather x1, blocking collectives, per_device(): lax.all_gather(lax.all_gather(targets[0], 'y_hi', axis=0), 'z', axis=0)  25.7 us
    all_gather x1, blocking collectives, per_device(): weights = lax.all_gather(weights, CLIP, axis=0)  23.6 us
    all_to_all x1, blocking collectives, swap(): return lax.all_to_all(array, axes, 0, 0, tiled=True)  22.7 us
    pallas_call x1, Pallas kernels, forward(): pl.pallas_call(forward_kernel, out_shape=[jax.ShapeDtypeStruct((COPIES, H...  7.69 us
    all_gather x1, blocking collectives, per_device(): lax.all_gather(targets[0], 'y_hi', axis=0)  6.26 us
    pallas_call x1, Pallas kernels, backward(): pl.pallas_call(backward_kernel, out_shape=jax.ShapeDtypeStruct((CLIPS, HS...  5.93 us
  transfers between devices with their start and end apart: 7, of which 3 were waited for; matrix products, arithmetic and copies ran while one was open for 3% of the time, Pallas kernels for 7%

profile of v1, /device:TPU:32, one launch (start us, length us, event | category | flops | bytes accessed | tf_op | source)
XLA Modules:
  0.0 196.3 jit_solution(18185539771332900331)
XLA Ops:
  10.0 0.9 broadcast_in_dim.81
  10.9 11.3 %all-to-all-start = ((bf16[16,16,1152]{2,1,0:T(8,128)(2,1)}), bf16[16,16,1152]{2,1,0:T(8,128)(2,1)S(1)}, u32[]{:S(2)}, u32[]{:S(2)}) async-start(bf16[16,16,1152]{2,1,0:T(8,128)(2,1)} %broadcast_in_dim.81), calls=%async_computation | async-start | bytes 1179648 | tf_op jit(solution)/shard_map/all_to_all | solution.py:226
  22.2 0.8 constant_dynamic-slice_fusion
  23.0 0.8 constant_dynamic-slice_fusion.2
  23.9 23.6 %all-gather = bf16[1536,128]{1,0:T(8,128)(2,1)S(1)} all-gather(bf16[96,128]{1,0:T(8,128)(2,1)S(1)} %maximum_maximum_fusion), channel_id=2, replica_groups=mesh['x'=4,'y_lo'=2,'core'=2,'z'=8,'y_hi'=2] {'x','y_lo','core'}, dimensions={0}, use_global_device_ids=true | all-gather | bytes 417792 | tf_op jit(solution)/shard_map/all_gather | solution.py:264
  47.6 7.7 %forward.1 = (bf16[16,64,128]{2,1,0:T(8,128)(2,1)}, f32[256,2048]{1,0:T(8,128)S(1)}, bf16[256,2048]{1,0:T(8,128)(2,1)S(1)}, bf16[64,2048]{1,0:T(8,128)(2,1)S(1)}...) custom-call(bf16[256,1152]{1,0:T(8,128)(2,1)S(1)} %bitcast.28, ...), custom_call_target="tpu_custom_call" | custom-call | tf_op jit(solution)/shard_map/forward/pallas_call | solution.py:86
  55.3 1.3 copy-done.1
  56.6 0.8 copy-done.3
  58.1 9.9 %all-to-all-start.1 = ((bf16[16,64,128]{2,1,0:T(8,128)(2,1)}), bf16[16,64,128]{2,1,0:T(8,128)(2,1)S(1)}, u32[]{:S(2)}, u32[]{:S(2)}) async-start(bf16[16,64,128]{2,1,0:T(8,128)(2,1)} %get-tuple-element.13), calls=%async_computation.1 | async-start | bytes 524288 | tf_op jit(solution)/shard_map/all_to_all | solution.py:226
  68.1 6.3 %all_gather.21 = bf16[2,16,1024]{2,1,0:T(8,128)(2,1)S(1)} all-gather(bf16[1,16,1024]{2,1,0:T(8,128)(2,1)S(1)} %copy-done.9), channel_id=1, replica_groups=mesh['x'=4,'y_lo'=2,'core'=2,'z'=8,'y_hi'=2] {'y_hi'}, dimensions={0}, use_global_device_ids=true | all-gather | bytes 98304 | tf_op jit(solution)/shard_map/all_gather | solution.py:266
  74.3 25.7 %all-gather.1 = bf16[16,16,1024]{2,1,0:T(8,128)(2,1)S(1)} all-gather(bf16[2,16,1024]{2,1,0:T(8,128)(2,1)S(1)} %all_gather.21), channel_id=3, replica_groups=mesh['x'=4,'y_lo'=2,'core'=2,'z'=8,'y_hi'=2] {'z'}, dimensions={0}, use_global_device_ids=true | all-gather | bytes 589824 | tf_op jit(solution)/shard_map/all_gather | solution.py:266
  100.0 1.6 copy-done
  101.6 5.4 %decoder.1 = (bf16[128,1024]{1,0:T(8,128)(2,1)}, bf16[1024,128]{1,0:T(8,128)(2,1)S(1)}, bf16[128,1024]{1,0:T(8,128)(2,1)S(1)}) custom-call(s32[1]{0:T(128)} %bitcast.26.count_ref, bf16[1024,128]{1,0:T(8,128)(2,1)S(1)} %bitcast.30, bf16[256,1152]{1,0:T(8,128)(2,1)S(1)} %bitcast.29, bf16[1024,1024]{1,0:T(8,128)(2,1)S(1)} %copy-done, ...), custom_call_target="tpu_custom_call" | custom-call | tf_op jit(solution)/shard_map/decoder/pallas_call | solution.py:139
  107.0 0.9 out_grad.1
  107.9 1.1 slice_bitcast_fusion
  109.0 22.7 %all_to_all.30.dctx_ref = bf16[16,64,128]{2,1,0:T(8,128)(2,1)S(1)} all-to-all(bf16[16,64,128]{2,1,0:T(8,128)(2,1)S(1)} %bitcast.34), channel_id=1, replica_groups=mesh['x'=4,'y_lo'=2,'core'=2,'z'=8,'y_hi'=2] {'z','y_hi'}, dimensions={0} | all-to-all | bytes 524288 | tf_op jit(solution)/shard_map/all_to_all | solution.py:226
  131.6 5.9 %backward.1 = bf16[16,96,128]{2,1,0:T(8,128)(2,1)} custom-call(bf16[16,64,128]{2,1,0:T(8,128)(2,1)S(1)} %all_to_all.30.dctx_ref, f32[256,2048]{1,0:T(8,128)S(1)} %copy-done.2, bf16[256,2048]{1,0:T(8,128)(2,1)S(1)} %get-tuple-element.18.pick_ref, bf16[64,2048]{1,0:T(8,128)(2,1)S(1)} %copy-done.6, bf16[64,256]{1,0:T(8,128)(2,1)S(1)} %get-tuple-element.20.key_ref, ...), custom_call_target="tpu_custom_call" | custom-call | tf_op jit(solution)/shard_map/backward/pallas_call | solution.py:209
  137.6 3.6 %all-to-all-start.4 = ((bf16[16,96,128]{2,1,0:T(8,128)(2,1)}), bf16[16,96,128]{2,1,0:T(8,128)(2,1)S(1)}, u32[]{:S(2)}, u32[]{:S(2)}) async-start(bf16[16,96,128]{2,1,0:T(8,128)(2,1)} %backward.1), calls=%async_computation.4 | async-start | bytes 786432 | tf_op jit(solution)/shard_map/all_to_all | solution.py:226
  141.1 2.5 %fusion = bf16[8,16,32,128]{3,2,1,0:T(8,128)(2,1)} fusion(bf16[8,16,32,128]{3,2,1,0:T(8,128)(2,1)} %collective-permute-done, bf16[2,8,16,32,128]{4,3,2,1,0:T(8,128)(2,1)S(1)} %out_grad.1), kind=kLoop, calls=%fused_computation.1 | loop fusion | flops 2097152 | bytes 3145728 | tf_op jit(solution)/shard_map/convert_element_type | solution.py:278
  143.6 6.7 %all-to-all-done.4 = bf16[16,96,128]{2,1,0:T(8,128)(2,1)S(1)} async-done(((bf16[16,96,128]{2,1,0:T(8,128)(2,1)}), bf16[16,96,128]{2,1,0:T(8,128)(2,1)S(1)}, u32[]{:S(2)}, u32[]{:S(2)}) %all-to-all-start.4) | async-done | bytes 393248 | tf_op jit(solution)/shard_map/all_to_all | solution.py:226
  150.3 3.6 %all-to-all-start.2 = ((bf16[8,16,32,128]{3,2,1,0:T(8,128)(2,1)}), bf16[8,16,32,128]{3,2,1,0:T(8,128)(2,1)S(1)}, u32[]{:S(2)}, u32[]{:S(2)}) async-start(bf16[8,16,32,128]{3,2,1,0:T(8,128)(2,1)} %fusion), calls=%async_computation.2 | async-start | bytes 2097152 | tf_op jit(solution)/shard_map/all_to_all | solution.py:226
  154.3 15.7 %all-to-all-done.2 = bf16[8,16,32,128]{3,2,1,0:T(8,128)(2,1)S(1)} async-done(((bf16[8,16,32,128]{3,2,1,0:T(8,128)(2,1)}), bf16[8,16,32,128]{3,2,1,0:T(8,128)(2,1)S(1)}, u32[]{:S(2)}, u32[]{:S(2)}) %all-to-all-start.2) | async-done | bytes 1048608 | tf_op jit(solution)/shard_map/all_to_all | solution.py:226
  170.9 5.3 %all-to-all-start.5 = ((bf16[16,64,128]{2,1,0:T(8,128)(2,1)}), bf16[16,64,128]{2,1,0:T(8,128)(2,1)S(1)}, u32[]{:S(2)}, u32[]{:S(2)}) async-start(bf16[16,64,128]{2,1,0:T(8,128)(2,1)} %pad_maximum_fusion), calls=%async_computation.5 | async-start | bytes 524288 | tf_op jit(solution)/shard_map/all_to_all | solution.py:226
  176.2 11.6 %all-to-all-done.5 = bf16[16,64,128]{2,1,0:T(8,128)(2,1)S(1)} async-done(((bf16[16,64,128]{2,1,0:T(8,128)(2,1)}), bf16[16,64,128]{2,1,0:T(8,128)(2,1)S(1)}, u32[]{:S(2)}, u32[]{:S(2)}) %all-to-all-start.5) | async-done | bytes 262176 | tf_op jit(solution)/shard_map/all_to_all | solution.py:226
  (48 shorter events, 5.9 us)
Async XLA Ops:
  7.2 40.4 %copy-start.8 = (f32[1024]{0:T(1024)S(1)}, f32[1024]{0:T(1024)}, u32[]{:S(2)}) copy-start(f32[1024]{0:T(1024)} %param.14) | copy-start | bytes 12292
  7.2 60.9 %copy-start.10 = (bf16[1024]{0:T(1024)(128)(2,1)S(1)}, bf16[1024]{0:T(1024)(128)(2,1)}, u32[]{:S(2)}) copy-start(bf16[1024]{0:T(1024)(128)(2,1)} %param.17) | copy-start | bytes 6148
  7.2 60.9 %copy-start.9 = (bf16[1,16,1024]{2,1,0:T(8,128)(2,1)S(1)}, bf16[1,16,1024]{2,1,0:T(8,128)(2,1)}, u32[]{:S(2)}) copy-start(bf16[1,16,1024]{2,1,0:T(8,128)(2,1)} %param.11) | copy-start | bytes 98308
  7.2 92.8 %all-gather.4.cloned.1.call-start = ((), (), s32[]{:S(2)}) async-start(), calls=%async_computation.6 | async-start | bytes 2228224 | tf_op jit(solution)/shard_map/all_gather | solution.py:265
  10.9 89.1 %copy-start.7 = (f32[7,1024]{1,0:T(8,128)S(1)}, f32[7,1024]{1,0:T(8,128)}, u32[]{:S(2)}) copy-start(f32[7,1024]{1,0:T(8,128)} %taps_ref.1) | copy-start | bytes 86020
  10.9 36.7 %all-to-all-start = ((bf16[16,16,1152]{2,1,0:T(8,128)(2,1)}), bf16[16,16,1152]{2,1,0:T(8,128)(2,1)S(1)}, u32[]{:S(2)}, u32[]{:S(2)}) async-start(bf16[16,16,1152]{2,1,0:T(8,128)(2,1)} %broadcast_in_dim.81), calls=%async_computation | async-start | bytes 1179648 | tf_op jit(solution)/shard_map/all_to_all | solution.py:226
  55.3 1.3 copy-start.1
  56.6 0.8 copy-start.3
  57.4 0.7 copy-start.5
  58.1 41.9 %all-to-all-start.1 = ((bf16[16,64,128]{2,1,0:T(8,128)(2,1)}), bf16[16,64,128]{2,1,0:T(8,128)(2,1)S(1)}, u32[]{:S(2)}, u32[]{:S(2)}) async-start(bf16[16,64,128]{2,1,0:T(8,128)(2,1)} %get-tuple-element.13), calls=%async_computation.1 | async-start | bytes 524288 | tf_op jit(solution)/shard_map/all_to_all | solution.py:226
  100.0 1.6 copy-start
  107.0 24.6 %copy-start.2 = (f32[256,2048]{1,0:T(8,128)S(1)}, f32[256,2048]{1,0:T(8,128)}, u32[]{:S(2)}) copy-start(f32[256,2048]{1,0:T(8,128)} %copy-done.1) | copy-start | bytes 6291460
  107.0 24.6 %copy-start.4 = (bf16[1024,256]{1,0:T(8,128)(2,1)S(1)}, bf16[1024,256]{1,0:T(8,128)(2,1)}, u32[]{:S(2)}) copy-start(bf16[1024,256]{1,0:T(8,128)(2,1)} %copy-done.3) | copy-start | bytes 1572868
  107.0 24.6 %copy-start.6 = (bf16[64,2048]{1,0:T(8,128)(2,1)S(1)}, bf16[64,2048]{1,0:T(8,128)(2,1)}, u32[]{:S(2)}) copy-start(bf16[64,2048]{1,0:T(8,128)(2,1)} %copy-done.5) | copy-start | bytes 786436
  109.0 32.2 %collective-permute-start = (bf16[8,16,32,128]{3,2,1,0:T(8,128)(2,1)}, bf16[8,16,32,128]{3,2,1,0:T(8,128)(2,1)}, u32[]{:S(2)}, u32[]{:S(2)}) collective-permute-start(bf16[8,16,32,128]{3,2,1,0:T(8,128)(2,1)} %slice_bitcast_fusion), channel_id=1, source_target_pairs={{0,16},{16,0},{1,17},{17,1},{2,18},{18,2},{3,19},{19,3},{4,20},{20... | collective-permute-start | bytes 3145736 | tf_op jit(solution)/shard_map/ppermute | solution.py:277
  137.6 12.8 %all-to-all-start.4 = ((bf16[16,96,128]{2,1,0:T(8,128)(2,1)}), bf16[16,96,128]{2,1,0:T(8,128)(2,1)S(1)}, u32[]{:S(2)}, u32[]{:S(2)}) async-start(bf16[16,96,128]{2,1,0:T(8,128)(2,1)} %backward.1), calls=%async_computation.4 | async-start | bytes 786432 | tf_op jit(solution)/shard_map/all_to_all | solution.py:226
  150.3 19.7 %all-to-all-start.2 = ((bf16[8,16,32,128]{3,2,1,0:T(8,128)(2,1)}), bf16[8,16,32,128]{3,2,1,0:T(8,128)(2,1)S(1)}, u32[]{:S(2)}, u32[]{:S(2)}) async-start(bf16[8,16,32,128]{3,2,1,0:T(8,128)(2,1)} %fusion), calls=%async_computation.2 | async-start | bytes 2097152 | tf_op jit(solution)/shard_map/all_to_all | solution.py:226
  170.9 16.9 %all-to-all-start.5 = ((bf16[16,64,128]{2,1,0:T(8,128)(2,1)}), bf16[16,64,128]{2,1,0:T(8,128)(2,1)S(1)}, u32[]{:S(2)}, u32[]{:S(2)}) async-start(bf16[16,64,128]{2,1,0:T(8,128)(2,1)} %pad_maximum_fusion), calls=%async_computation.5 | async-start | bytes 524288 | tf_op jit(solution)/shard_map/all_to_all | solution.py:226
Sparse Core Ops, SparseCore 0:
  9.9 43.8 all-gather.3

commit v2 on v1

v2 whole, which is shorter than its diff:
```python
import jax
import jax.numpy as jnp
from jax import lax
from jax.experimental import pallas as pl
from jax.experimental.pallas import tpu as pltpu
from jax.sharding import Mesh
from jax.sharding import PartitionSpec as P


D = 1024
H = 16
HS = 64
HALF = HS // 2
L = 256
KMAX = 128
KW = 7
CLIPS = 16
COPIES = 16
ROWS = L // COPIES
QALL = COPIES * KMAX
NORM_EPSILON = 1e-05
MASKED_SCORE = -1e30
SCORE_SCALE = HS**-0.5
LOSS_SCALE = (KMAX * CLIPS * COPIES) ** -0.5
PAD = 8
LANES = 256
BLOCK = 128
VMEM_LIMIT = 20 * 1024 * 1024

XS, YS = 4, 2
CLIP = ("x", "y_lo", "core")
COPY = ("z", "y_hi")
F32 = jnp.float32
BF16 = jnp.bfloat16

VMEM = pl.BlockSpec(memory_space=pltpu.VMEM)
SMEM = pl.BlockSpec(memory_space=pltpu.SMEM)
HBM = pl.BlockSpec(memory_space=pltpu.HBM)


def mm(left, right):
    return jnp.dot(left, right, preferred_element_type=F32)


def mm_nt(left, right):
    return lax.dot_general(left, right, (((1,), (1,)), ((), ())), preferred_element_type=F32)


def call(kernel, name, microseconds, out_shape, in_specs, out_specs, scratch=()):
    return pl.pallas_call(
        kernel,
        out_shape=[
            pltpu.HBM(shape, dtype) if spec is HBM else jax.ShapeDtypeStruct(shape, dtype)
            for (shape, dtype), spec in zip(out_shape, out_specs)
        ],
        in_specs=in_specs,
        out_specs=out_specs,
        scratch_shapes=list(scratch),
        compiler_params=pltpu.CompilerParams(vmem_limit_bytes=VMEM_LIMIT),
        cost_estimate=pl.CostEstimate(
            flops=int(microseconds * 1e9), bytes_accessed=1024, transcendentals=0
        ),
        name=name,
    )


def pack_kernel(place_ref, count_ref, frames_ref, index_ref, w_ref, sent_ref, index_out, weights_ref, w_buf, sems):
    head = place_ref[0]
    copies = []
    for part in range(3):
        begin = pl.multiple_of(part * D + (head // 2) * BLOCK, BLOCK)
        copies.append(
            pltpu.make_async_copy(w_ref.at[:, pl.ds(begin, BLOCK)], w_buf.at[part], sems.at[part])
        )
        copies[part].start()
    lanes = lax.broadcasted_iota(jnp.int32, (ROWS, KMAX), 1)
    index = jnp.broadcast_to(index_ref[0], (ROWS, KMAX))
    index = jnp.where(lanes < count_ref[0, 0], index, L).astype(F32).astype(BF16)
    index_out[...] = index
    for m in range(COPIES):
        sent_ref[m, :, :D] = frames_ref[0]
        sent_ref[m, :, D:] = index
    odd = head % 2 == 1
    for part in range(3):
        copies[part].wait()
    q, k, v = [
        jnp.where(odd, w_buf[part, :, HS:].astype(F32), w_buf[part, :, :HS].astype(F32)) for part in range(3)
    ]
    weights_ref[:HS, :] = jnp.concatenate([q, k], axis=1).astype(BF16)
    weights_ref[HS:, :] = jnp.concatenate([v[:HALF], v[HALF:]], axis=1).astype(BF16)


def pack(place, count, frames, index, w_qkv):
    return call(
        pack_kernel,
        "pack",
        1,
        [((COPIES, ROWS, D + KMAX), BF16), ((ROWS, KMAX), BF16), ((HS + HALF, BLOCK), BF16)],
        [SMEM, SMEM, VMEM, VMEM, HBM],
        [VMEM, VMEM, VMEM],
        [pltpu.VMEM((3, HS, BLOCK), BF16), pltpu.SemaphoreType.DMA((3,))],
    )(place, count, frames, index, pltpu.with_memory_space_constraint(w_qkv, pltpu.HBM))


def normalize(got_ref, gain_ref):
    values = got_ref[:, :D].astype(F32)
    center = values - jnp.mean(values, axis=1, keepdims=True)
    spread = jnp.mean(center * center, axis=1, keepdims=True)
    return (center * lax.rsqrt(spread + NORM_EPSILON) * gain_ref[...]).astype(BF16)


def forward_kernel(
    got_ref, w_ref, gain_ref, targets_ref, out_ref, probs_out, pick_out, query_out, key_out, value_out,
    probs_ref, pick_ref, query_ref, wv_ref, sems,
):
    for m in range(COPIES):
        for a in range(D // BLOCK):
            rows = slice(HS + a * ROWS, HS + (a + 1) * ROWS)
            out_ref[m, rows, :] = targets_ref[0, :, a * BLOCK : (a + 1) * BLOCK]
    normed = normalize(got_ref, gain_ref)
    for c in range(CLIPS):
        wv_ref[c * HS : c * HS + HALF, :] = w_ref[c, HS:, :HS]
        wv_ref[c * HS + HALF : (c + 1) * HS, :] = w_ref[c, HS:, HS:]
    qk = mm(normed, w_ref[:, :HS, :].reshape(D, 2 * HS)).astype(BF16)
    v = mm(normed, wv_ref[...]).astype(BF16)
    qk_t = qk.astype(F32).T
    query_t = (qk_t[:HS] * SCORE_SCALE).astype(BF16)
    key = qk[:, HS:]
    key_out[...] = qk_t[HS:].astype(BF16)
    value_out[...] = v
    value_t = v.astype(F32).T.astype(BF16)
    rows = lax.broadcasted_iota(jnp.int32, (L, KMAX), 0).astype(F32)
    ones = jnp.ones((KMAX, KMAX), BF16)
    saves = []
    for m in range(COPIES):
        lanes = slice(m * KMAX, (m + 1) * KMAX)
        index = got_ref[m * ROWS : (m + 1) * ROWS, D:].astype(F32)[:1]
        pick = jnp.where(rows == index, 1.0, 0.0).astype(BF16)
        pick_ref[:, lanes] = pick
        queries = mm(query_t, pick).astype(BF16)
        query_ref[:, lanes] = queries
        scores = jnp.where(mm(pick, ones) > 0.5, mm(key, queries), MASKED_SCORE)
        raised = jnp.exp(scores - jnp.max(scores, axis=0, keepdims=True))
        probs = raised * (1.0 / jnp.sum(raised, axis=0, keepdims=True))
        probs_ref[m] = probs
        save = pltpu.make_async_copy(probs_ref.at[m], probs_out.at[m], sems.at[m])
        save.start()
        saves.append(save)
        out_ref[m, :HS, :] = mm(value_t, probs.astype(BF16)).astype(BF16)
    for here, there, at in ((pick_ref, pick_out, COPIES), (query_ref, query_out, COPIES + 1)):
        save = pltpu.make_async_copy(here, there, sems.at[at])
        save.start()
        saves.append(save)
    for save in saves:
        save.wait()


def forward(got, weights, gain, targets):
    return call(
        forward_kernel,
        "forward",
        6,
        [
            ((COPIES, HS + KMAX, KMAX), BF16),
            ((COPIES, L, KMAX), F32),
            ((L, QALL), BF16),
            ((HS, QALL), BF16),
            ((HS, L), BF16),
            ((L, HS), BF16),
        ],
        [VMEM] * 4,
        [VMEM, HBM, HBM, HBM, VMEM, VMEM],
        [
            pltpu.VMEM((COPIES, L, KMAX), F32),
            pltpu.VMEM((L, QALL), BF16),
            pltpu.VMEM((HS, QALL), BF16),
            pltpu.VMEM((D, HS), BF16),
            pltpu.SemaphoreType.DMA((COPIES + 2,)),
        ],
    )(got, weights, gain, targets)


def prepare_kernel(got_ref, gain_ref, out_ref, buf, sem):
    buf[...] = normalize(got_ref, gain_ref).T
    save = pltpu.make_async_copy(buf, out_ref, sem)
    save.start()
    save.wait()


def prepare(got, gain):
    return call(
        prepare_kernel,
        "prepare",
        2,
        [((D, L), BF16)],
        [VMEM] * 2,
        [HBM],
        [pltpu.VMEM((D, L), BF16), pltpu.SemaphoreType.DMA(())],
    )(got, gain)[0]


def decoder_kernel(
    place_ref, count_ref, recv_ref, got_ref, w_hbm, index_ref, embed_ref, taps_ref,
    encoded_ref, dctx_ref, ctx_ref, denc_ref, share_ref,
    w_ref, field_ref, sems,
):
    chunks = D // LANES
    copies = []
    for c in range(chunks):
        lanes = pl.ds(c * LANES, LANES)
        copies.append(pltpu.make_async_copy(w_hbm.at[:, lanes], w_ref.at[:, lanes], sems.at[c]))
        copies[c].start()
    core = place_ref[1]
    live = lax.broadcasted_iota(jnp.int32, (KMAX, 1), 0) < count_ref[0, 0]
    rows = lax.broadcasted_iota(jnp.int32, (L, KMAX), 0).astype(F32)
    hit = jnp.where(rows == index_ref[...].astype(F32)[:1], 1.0, 0.0)
    masked = 1.0 - jnp.sum(hit, axis=1, keepdims=True)
    place = hit.astype(BF16)
    pick = hit.T.astype(BF16)
    ctx_t = recv_ref[:, :HS, :]
    ctx_ref[...] = ctx_t
    ctx = ctx_t.reshape(D, KMAX).T
    for i in range(CLIPS // 2):
        share_ref[i, :HS, :] = ctx_ref[2 * i + 1 - core]
    reach = KW // 2
    field_ref[:PAD] = jnp.zeros((PAD, LANES), F32)
    field_ref[PAD + L :] = jnp.zeros((PAD, LANES), F32)
    for c in range(chunks):
        lanes = slice(c * LANES, (c + 1) * LANES)
        copies[c].wait()
        mixed = mm(pick, got_ref[:, lanes]) + mm(ctx, w_ref[:, lanes])
        encoded = jnp.where(live, mixed, 0.0).astype(BF16)
        encoded_ref[:, lanes] = encoded
        field_ref[PAD : PAD + L] = mm(place, encoded) + masked * embed_ref[:, lanes].astype(F32)
        predicted = taps_ref[:1, lanes] * field_ref[PAD - reach : PAD - reach + L]
        for t in range(1, KW):
            begin = PAD - reach + t
            predicted = predicted + taps_ref[t : t + 1, lanes] * field_ref[begin : begin + L]
        wanted = []
        for a in range(c * LANES // BLOCK, (c + 1) * LANES // BLOCK):
            block = recv_ref[:, HS + a * ROWS : HS + (a + 1) * ROWS, :]
            wanted.append(block.reshape(L, BLOCK))
        wanted = jnp.concatenate(wanted, axis=1).astype(F32)
        field_ref[PAD : PAD + L] = masked * (predicted - wanted) * LOSS_SCALE
        dfilled = taps_ref[:1, lanes] * field_ref[PAD + reach : PAD + reach + L]
        for t in range(1, KW):
            begin = PAD + reach - t
            dfilled = dfilled + taps_ref[t : t + 1, lanes] * field_ref[begin : begin + L]
        denc = mm(pick, dfilled.astype(BF16)).astype(BF16)
        denc_ref[:, lanes] = denc
        for a in range(c * LANES // BLOCK, (c + 1) * LANES // BLOCK):
            begin = a * BLOCK - c * LANES
            share_ref[a, HS:, :] = denc[:, begin : begin + BLOCK]
    dctx_ref[...] = mm_nt(w_ref[...], denc_ref[...]).astype(BF16)


def decoder(place, count, recv, got, w_out, index, embed, taps):
    return call(
        decoder_kernel,
        "decoder",
        5,
        [
            ((KMAX, D), BF16),
            ((D, KMAX), BF16),
            ((H, HS, KMAX), BF16),
            ((KMAX, D), BF16),
            ((CLIPS // 2, HS + KMAX, KMAX), BF16),
        ],
        [SMEM, SMEM, VMEM, VMEM, HBM, VMEM, VMEM, VMEM],
        [VMEM] * 5,
        [
            pltpu.VMEM((D, D), BF16),
            pltpu.VMEM((L + 2 * PAD, LANES), F32),
            pltpu.SemaphoreType.DMA((D // LANES,)),
        ],
    )(place, count, recv, got, pltpu.with_memory_space_constraint(w_out, pltpu.HBM), index, embed, taps)


def out_grad_kernel(place_ref, ctx_ref, denc_ref, share_ref, *refs):
    outs, both_ref = refs[:XS], refs[XS]
    core, x, y = place_ref[1], place_ref[2], place_ref[3]
    for a in range(D // BLOCK):
        lanes = slice(a * BLOCK, (a + 1) * BLOCK)
        both_ref[:KMAX, lanes] = denc_ref[:, lanes]
        both_ref[KMAX:, lanes] = share_ref[a, HS:, :]
    for r in range(XS):
        for s in range(YS):
            chip = YS * lax.rem(x + r, XS) + lax.rem(y + s, YS)
            left = jnp.concatenate([ctx_ref[2 * chip + core], share_ref[chip, :HS, :]], axis=1)
            block = mm(left, both_ref[...])
            upper, lower = block[:HALF], block[HALF:]
            for a in range(D // BLOCK):
                lanes = slice(a * BLOCK, (a + 1) * BLOCK)
                first, second = upper[:, lanes], lower[:, lanes]
                even = jnp.concatenate([first[:, :HS], second[:, :HS]], axis=1)
                odd = jnp.concatenate([first[:, HS:], second[:, HS:]], axis=1)
                outs[r][s, 2 * a] = even.astype(BF16)
                outs[r][s, 2 * a + 1] = odd.astype(BF16)


def out_grad(place, ctx, denc, share):
    return call(
        out_grad_kernel,
        "out_grad",
        1,
        [((YS, COPIES, HALF, BLOCK), BF16)] * XS,
        [SMEM] + [VMEM] * 3,
        [VMEM] * XS,
        [pltpu.VMEM((2 * KMAX, D), BF16)],
    )(place, ctx, denc, share)


def backward_kernel(
    dctx_ref, probs_ref, pick_ref, query_ref, key_ref, value_ref, normed_ref, out_ref, dctx_all, low_all, ds_all, dq_all
):
    key_t = key_ref[...]
    value = value_ref[...]
    for m in range(COPIES):
        lanes = slice(m * KMAX, (m + 1) * KMAX)
        dctx = dctx_ref[m]
        dctx_all[:, lanes] = dctx
        probs = probs_ref[m]
        low_all[:, lanes] = probs.astype(BF16)
        dprobs = mm(value, dctx)
        dscores = probs * (dprobs - jnp.sum(probs * dprobs, axis=0, keepdims=True))
        dscores = dscores.astype(BF16)
        ds_all[:, lanes] = dscores
        dq_all[:, lanes] = (mm(key_t, dscores) * SCORE_SCALE).astype(BF16)
    dvalue = mm_nt(dctx_all[...], low_all[...]).astype(BF16)
    dkey = mm_nt(query_ref[...], ds_all[...]).astype(BF16)
    dquery = mm_nt(dq_all[...], pick_ref[...]).astype(BF16)
    normed_t = normed_ref[...]
    grad_qk = mm_nt(normed_t, jnp.concatenate([dquery, dkey], axis=0)).astype(BF16)
    grad_v = mm_nt(normed_t, dvalue).astype(BF16)
    for c in range(CLIPS):
        out_ref[c, :HS, :] = grad_qk[c * HS : (c + 1) * HS]
        out_ref[c, HS:, :HS] = grad_v[c * HS : c * HS + HALF]
        out_ref[c, HS:, HS:] = grad_v[c * HS + HALF : (c + 1) * HS]


def backward(dctx, probs, pick, query, key, value, normed):
    return call(
        backward_kernel,
        "backward",
        5,
        [((CLIPS, HS + HALF, BLOCK), BF16)],
        [VMEM] * 7,
        [VMEM],
        [
            pltpu.VMEM((HS, QALL), BF16),
            pltpu.VMEM((L, QALL), BF16),
            pltpu.VMEM((L, QALL), BF16),
            pltpu.VMEM((HS, QALL), BF16),
        ],
    )(dctx, probs, pick, query, key, value, normed)[0]


def collect_kernel(place_ref, terms_ref, mine_ref, other_ref, out_ref):
    head = place_ref[0]
    out_ref[:, :HALF, :] = (mine_ref[...].astype(F32) + other_ref[...].astype(F32)).astype(BF16)
    out_ref[:, HALF:, :] = jnp.zeros((COPIES, HALF, BLOCK), BF16)
    term = jnp.sum(terms_ref[...].astype(F32), axis=0)
    upper, lower = term[:HALF], term[HALF:HS]
    query = jnp.concatenate([upper[:, :HS], lower[:, :HS]], axis=1)
    key = jnp.concatenate([upper[:, HS:], lower[:, HS:]], axis=1)
    for part, piece in enumerate((query, key, term[HS:])):
        out_ref[(part * H + head) // 3, HALF:, :] = piece.astype(BF16)


def collect(place, terms, mine, other):
    return call(
        collect_kernel,
        "collect",
        1,
        [((COPIES, HS, BLOCK), BF16)],
        [SMEM] + [VMEM] * 3,
        [VMEM],
    )(place, terms, mine, other)[0]


def finish_kernel(place_ref, last_ref, qkv_ref, out_ref):
    total = jnp.sum(last_ref[:, :HALF, :].astype(F32), axis=0)
    out_ref[:HALF, :] = total[:, :HS]
    out_ref[HALF:, :] = total[:, HS:]
    for i in range(3):
        block = last_ref[lax.rem(3 * place_ref[0] + i, COPIES), HALF:, :].astype(F32)
        qkv_ref[:HALF, i * HS : (i + 1) * HS] = block[:, :HS]
        qkv_ref[HALF:, i * HS : (i + 1) * HS] = block[:, HS:]


def finish(place, last):
    return call(
        finish_kernel,
        "finish",
        1,
        [((HS, 3 * HS), F32), ((HS, HS), F32)],
        [SMEM, VMEM],
        [VMEM] * 2,
    )(place, last)


def swap(array, axes):
    return lax.all_to_all(array, axes, 0, 0, tiled=True)


def total(*parts):
    result = parts[0].astype(F32)
    for part in parts[1:]:
        result = result + part.astype(F32)
    return result.astype(BF16)


def per_device(
    frames,
    targets,
    kept_index,
    kept_count,
    fill_slot,
    norm_gain,
    w_qkv,
    w_out,
    mask_embed,
    dec_kernel,
):
    place = jnp.stack(
        [lax.axis_index(COPY), lax.axis_index("core"), lax.axis_index("x"), lax.axis_index("y_lo")]
    )
    gain = norm_gain[None, :]
    sent, index, weights = pack(place, kept_count, frames, kept_index, w_qkv)
    got = swap(sent, COPY).reshape(L, D + KMAX)
    for axis in ("core", "y_lo", "x"):
        weights = lax.all_gather(weights, axis, axis=0)
    weights = weights.reshape(CLIPS, HS + HALF, BLOCK)
    w_out_all = lax.all_gather(w_out, CLIP, axis=0, tiled=True)

    sent, probs, pick, query, key, value = forward(got, weights, gain, targets)
    normed = prepare(got, gain)
    recv = swap(sent, COPY)
    encoded, dctx, ctx, denc, share = decoder(
        place, kept_count, recv, got, w_out_all, index, mask_embed[None, :], dec_kernel
    )
    dctx = swap(dctx.reshape(H, HS, KMAX), COPY)

    share = lax.ppermute(share, "core", [(0, 1), (1, 0)])
    parts = list(out_grad(place, ctx, denc, share))
    for r in range(1, XS):
        parts[r] = lax.ppermute(parts[r], "x", [(i, (i + r) % XS) for i in range(XS)])
    mine = total(*[part[0] for part in parts])
    other = total(*[part[1] for part in parts])
    other = lax.ppermute(other, "y_lo", [(0, 1), (1, 0)])

    terms = swap(backward(dctx, probs, pick, query, key, value, normed), CLIP)
    grad_qkv, grad_out = finish(place, swap(collect(place, terms, mine, other), COPY))
    return (encoded[None, None], grad_qkv, grad_out)


def solution(mesh):
    fine = Mesh(mesh.devices.reshape(XS, YS, 2, 8, 2), ("x", "y_lo", "core", "z", "y_hi"))
    in_specs = (
        P(CLIP, COPY, None),
        P(CLIP, COPY, None),
        P(CLIP, COPY, None),
        P(CLIP, COPY),
        P(CLIP, COPY, None),
        P(),
        P(CLIP, None),
        P(CLIP, None),
        P(),
        P(),
    )
    out_specs = (P(CLIP, COPY, None, None), P(CLIP, COPY), P(CLIP, COPY))
    return jax.shard_map(
        per_device, mesh=fine, in_specs=in_specs, out_specs=out_specs, check_vma=False
    )
```

time: 198 us -> 157 us (0.79)
  blocking collectives: 78.2 us -> 38.9 us
  Pallas kernels: 19.9 us -> 27.9 us
  other arithmetic: 6.51 us -> 0.22 us
  waiting for transfers between devices: 34.7 us -> 30.3 us
  starting transfers between devices: 33.7 us -> 38.1 us
  local copies, waits for them, and re-layouts: 8.39 us -> 4.26 us
    all_gather x3, blocking collectives: 55.6 us -> 20.8 us  [per_device(): weights = lax.all_gather(weights, axis, axis=0)]
    all_to_all x5 -> x4, waiting for transfers between devices: 34 us -> 21.2 us  [swap(): return lax.all_to_all(array, axes, 0, 0, tiled=True)]
    ppermute x1 -> x5, waiting for transfers between devices: 0.01 us -> 8.37 us  [the longest x1 7.96 us: per_device(): other = lax.ppermute(other, 'y_lo', [(0, 1), (1, 0)])]
    pallas_call x4 -> x8, Pallas kernels: 19.9 us -> 27.9 us  [the longest x1 7.96 us: decoder(): call(decoder_kernel, 'decoder', 5, [((KMAX, D), BF16), ((D, KMAX), BF16),...]
    ppermute x1 -> x5, starting transfers between devices: 0.01 us -> 7.55 us  [the longest x3 5.54 us: per_device(): lax.ppermute(parts[r], 'x', [(i, (i + r) % XS) for i in range(XS)])]
    all_to_all x1, blocking collectives: 22.7 us -> 18 us  [swap(): return lax.all_to_all(array, axes, 0, 0, tiled=True)]
    convert_element_type x3 -> x0, other arithmetic: 3.84 us -> none  [the longest x1 2.47 us: per_device(): out_term = (out_term[0].astype(F32) + other.astype(F32)).astype(BF16)]
    all_to_all x5 -> x4, starting transfers between devices: 33.7 us -> 30.5 us  [swap(): return lax.all_to_all(array, axes, 0, 0, tiled=True)]
  transfers between devices with their start and end apart: 7 -> 10, of which waited for: 3 -> 4; matrix products, arithmetic and copies ran while one was open for 3% -> 0% of each run, Pallas kernels for 7% -> 12%
where the time goes in v2:
time: 157 us; the launch traced here: 154 us
  blocking collectives  38.9 us (25%)
  starting transfers between devices  38.1 us (24%)
  waiting for transfers between devices  30.3 us (19%)
  Pallas kernels  27.9 us (18%)
  between operations  14.8 us (9%)
  local copies, waits for them, and re-layouts  4.26 us (3%)
    all_to_all x4, starting transfers between devices, swap(): return lax.all_to_all(array, axes, 0, 0, tiled=True)  30.5 us
    all_to_all x4, waiting for transfers between devices, swap(): return lax.all_to_all(array, axes, 0, 0, tiled=True)  21.2 us
    all_gather x3, blocking collectives, per_device(): weights = lax.all_gather(weights, axis, axis=0)  20.8 us
    all_to_all x1, blocking collectives, swap(): return lax.all_to_all(array, axes, 0, 0, tiled=True)  18 us
    pallas_call x1, Pallas kernels, decoder(): call(decoder_kernel, 'decoder', 5, [((KMAX, D), BF16), ((D, KMAX), BF16),...  7.96 us
    ppermute x1, waiting for transfers between devices, per_device(): other = lax.ppermute(other, 'y_lo', [(0, 1), (1, 0)])  7.96 us
    pallas_call x1, Pallas kernels, forward(): call(forward_kernel, 'forward', 6, [((COPIES, HS + KMAX, KMAX), BF16), ((...  7.04 us
    pallas_call x1, Pallas kernels, backward(): call(backward_kernel, 'backward', 5, [((CLIPS, HS + HALF, BLOCK), BF16)],...  5.96 us
  transfers between devices with their start and end apart: 10, of which 4 were waited for; matrix products, arithmetic and copies ran while one was open for 0% of the time, Pallas kernels for 12%

profile of v2, /device:TPU:32, one launch (start us, length us, event | category | flops | bytes accessed | tf_op | source)
XLA Modules:
  0.0 154.4 jit_solution(9434518839883086956)
XLA Ops:
  10.1 2.2 %pack.1 = (bf16[16,16,1152]{2,1,0:T(8,128)(2,1)}, bf16[16,128]{1,0:T(8,128)(2,1)S(1)}, bf16[96,128]{1,0:T(8,128)(2,1)S(1)}) custom-call(s32[4]{0:T(128)S(1)} %pad_add_fusion.place_ref, s32[1,1]{1,0:T(1,128)S(6)} %copy.12.count_ref, bf16[1,16,1024]{2,1,0:T(8,128)(2,1)S(1)} %copy-done, s32[1,1,128]{2,1,0:T(1,128)S(1)} %copy-done.4, bf16[64,3072]{1,0:T(8,128)(2,1)} %w_ref.1), custom_call_target="tpu_custom_call" | custom-call | flops 1000000000 | bytes 1024 | tf_op jit(solution)/shard_map/pack/pallas_call | solution.py:94
  12.2 11.2 %all-to-all-start = ((bf16[16,16,1152]{2,1,0:T(8,128)(2,1)}), bf16[16,16,1152]{2,1,0:T(8,128)(2,1)S(1)}, u32[]{:S(2)}, u32[]{:S(2)}) async-start(bf16[16,16,1152]{2,1,0:T(8,128)(2,1)} %get-tuple-element.23), calls=%async_computation | async-start | bytes 1179648 | tf_op jit(solution)/shard_map/all_to_all | solution.py:403
  23.5 1.8 %all-gather = bf16[192,128]{1,0:T(8,128)(2,1)S(1)} all-gather(bf16[96,128]{1,0:T(8,128)(2,1)S(1)} %get-tuple-element.24), channel_id=2, replica_groups=mesh['x'=4,'y_lo'=2,'core'=2,'z'=8,'y_hi'=2] {'core'}, dimensions={0}, use_global_device_ids=true | all-gather | bytes 73728 | tf_op jit(solution)/shard_map/all_gather | solution.py:432
  25.3 6.3 %all-gather.1 = bf16[4,96,128]{2,1,0:T(8,128)(2,1)S(1)} all-gather(bf16[2,96,128]{2,1,0:T(8,128)(2,1)S(1)} %bitcast.22), channel_id=3, replica_groups=mesh['x'=4,'y_lo'=2,'core'=2,'z'=8,'y_hi'=2] {'y_lo'}, dimensions={0}, use_global_device_ids=true | all-gather | bytes 147456 | tf_op jit(solution)/shard_map/all_gather | solution.py:432
  31.6 12.7 %all-gather.2 = bf16[8,2,96,128]{3,2,1,0:T(8,128)(2,1)S(1)} all-gather(bf16[2,2,96,128]{3,2,1,0:T(8,128)(2,1)S(1)} %bitcast.21), channel_id=4, replica_groups=mesh['x'=4,'y_lo'=2,'core'=2,'z'=8,'y_hi'=2] {'x'}, dimensions={0}, use_global_device_ids=true | all-gather | bytes 491520 | tf_op jit(solution)/shard_map/all_gather | solution.py:432
  44.3 7.0 %forward.1 = (bf16[16,192,128]{2,1,0:T(8,128)(2,1)}, f32[16,256,128]{2,1,0:T(8,128)}, bf16[256,2048]{1,0:T(8,128)(2,1)}, bf16[64,2048]{1,0:T(8,128)(2,1)}, bf16[...) custom-call(bf16[256,1152]{1,0:T(8,128)(2,1)S(1)} %bitcast.15, bf16[16,96,128]{2,1,0:T(8,128)(2,1)S(1)} %bitcast.18, ...), custom_call_target="tpu_custom_call" | custom-call | flops 6000000000 | bytes 1024 | tf_op jit(solution)/shard_map/forward/pallas_call | solution.py:159
  51.4 9.1 %all-to-all-start.1 = ((bf16[16,192,128]{2,1,0:T(8,128)(2,1)}), bf16[16,192,128]{2,1,0:T(8,128)(2,1)S(1)}, u32[]{:S(2)}, u32[]{:S(2)}) async-start(bf16[16,192,128]{2,1,0:T(8,128)(2,1)} %get-tuple-element.25), calls=%async_computation.1 | async-start | bytes 1572864 | tf_op jit(solution)/shard_map/all_to_all | solution.py:403
  60.5 19.1 %all-to-all-done.1.recv_ref = bf16[16,192,128]{2,1,0:T(8,128)(2,1)S(1)} async-done(((bf16[16,192,128]{2,1,0:T(8,128)(2,1)}), bf16[16,192,128]{2,1,0:T(8,128)(2,1)S(1)}, u32[]{:S(2)}, u32[]{:S(2)}) %all-to-all-start.1) | async-done | bytes 786464 | tf_op jit(solution)/shard_map/all_to_all | solution.py:403
  79.6 8.0 %decoder.1 = (bf16[128,1024]{1,0:T(8,128)(2,1)}, bf16[1024,128]{1,0:T(8,128)(2,1)}, bf16[16,64,128]{2,1,0:T(8,128)(2,1)S(1)}, bf16[128,1024]{1,0:T(8,128)(2,1)S(1)}, bf16[8,192,128]{2,1,0:T(8,128)(2,1)S(1)}) custom-call(s32[4]{0:T(128)S(1)} %pad_add_fusion.place_ref, s32[1,1]{1,0:T(1,128)S(6)} %copy.12.count_ref, ...), custom_call_target="tpu_custom_call" | custom-call | flops 5000000000 | bytes 1024 | tf_op jit(solution)/shard_map/decoder/pallas_call | solution.py:258
  87.6 4.8 %all-to-all-start.2 = ((bf16[16,64,128]{2,1,0:T(8,128)(2,1)}), bf16[16,64,128]{2,1,0:T(8,128)(2,1)S(1)}, u32[]{:S(2)}, u32[]{:S(2)}) async-start(bf16[16,64,128]{2,1,0:T(8,128)(2,1)} %bitcast.10), calls=%async_computation.2 | async-start | bytes 524288 | tf_op jit(solution)/shard_map/all_to_all | solution.py:403
  92.4 1.3 prepare.1.normed_ref
  94.2 1.5 out_grad.1
  95.7 2.6 %collective-permute-start.1 = (bf16[2,16,32,128]{3,2,1,0:T(8,128)(2,1)S(1)}, bf16[2,16,32,128]{3,2,1,0:T(8,128)(2,1)S(1)}, u32[]{:S(2)}, u32[]{:S(2)}) collective-permute-start(bf16[2,16,32,128]{3,2,1,0:T(8,128)(2,1)S(1)} %get-tuple-element.38), channel_id=1, source_target_pairs={{0,64},{64,128},{128,192},{192,0},{1,65},{65,129},{129,193},{193,1... | collective-permute-start | bytes 786440 | tf_op jit(solution)/shard_map/ppermute | solution.py:447
  98.3 1.7 %collective-permute-start.2 = (bf16[2,16,32,128]{3,2,1,0:T(8,128)(2,1)S(1)}, bf16[2,16,32,128]{3,2,1,0:T(8,128)(2,1)S(1)}, u32[]{:S(2)}, u32[]{:S(2)}) collective-permute-start(bf16[2,16,32,128]{3,2,1,0:T(8,128)(2,1)S(1)} %get-tuple-element.39), channel_id=1, source_target_pairs={{0,128},{64,192},{128,0},{192,64},{1,129},{65,193},{129,1},{193,65... | collective-permute-start | bytes 786440 | tf_op jit(solution)/shard_map/ppermute | solution.py:447
  100.0 1.2 collective-permute-start.3
  101.2 2.1 %all-to-all-done.2.dctx_ref = bf16[16,64,128]{2,1,0:T(8,128)(2,1)S(1)} async-done(((bf16[16,64,128]{2,1,0:T(8,128)(2,1)}), bf16[16,64,128]{2,1,0:T(8,128)(2,1)S(1)}, u32[]{:S(2)}, u32[]{:S(2)}) %all-to-all-start.2) | async-done | bytes 262176 | tf_op jit(solution)/shard_map/all_to_all | solution.py:403
  103.3 1.6 %copy-done.6 = f32[16,256,128]{2,1,0:T(8,128)S(1)} copy-done((f32[16,256,128]{2,1,0:T(8,128)S(1)}, f32[16,256,128]{2,1,0:T(8,128)}, u32[]{:S(2)}) %copy-start.6) | copy-done | bytes 2097176
  104.9 1.2 copy-done.7
  106.1 6.0 %backward.1 = bf16[16,96,128]{2,1,0:T(8,128)(2,1)} custom-call(bf16[16,64,128]{2,1,0:T(8,128)(2,1)S(1)} %all-to-all-done.2.dctx_ref, f32[16,256,128]{2,1,0:T(8,128)S(1)} %copy-done.6, bf16[256,2048]{1,0:T(8,128)(2,1)S(1)} %copy-done.7, bf16[64,2048]{1,0:T(8,128)(2,1)S(1)} %copy-done.8, bf16[64,256]{1,0:T(8,128)(2,1)S(1)} %get-tuple-element.32.key_ref, ...), custom_call_target="tpu_custom_call" | custom-call | flops 5000000000 | bytes 1024 | tf_op jit(solution)/shard_map/backward/pallas_call | solution.py:342
  112.1 5.3 %all-to-all-start.3 = ((bf16[16,96,128]{2,1,0:T(8,128)(2,1)}), bf16[16,96,128]{2,1,0:T(8,128)(2,1)S(1)}, u32[]{:S(2)}, u32[]{:S(2)}) async-start(bf16[16,96,128]{2,1,0:T(8,128)(2,1)} %backward.1), calls=%async_computation.3 | async-start | bytes 786432 | tf_op jit(solution)/shard_map/all_to_all | solution.py:403
  117.6 2.0 %collective-permute-start.4 = (bf16[16,32,128]{2,1,0:T(8,128)(2,1)S(1)}, bf16[16,32,128]{2,1,0:T(8,128)(2,1)S(1)}, u32[]{:S(2)}, u32[]{:S(2)}) collective-permute-start(bf16[16,32,128]{2,1,0:T(8,128)(2,1)S(1)} %get-tuple-element.43), channel_id=1, source_target_pairs={{0,32},{32,0},{1,33},{33,1},{2,34},{34,2},{3,35},{35,3},{4,36},{36... | collective-permute-start | bytes 393224 | tf_op jit(solution)/shard_map/ppermute | solution.py:450
  119.6 8.0 %collective-permute-done.4.other_ref = bf16[16,32,128]{2,1,0:T(8,128)(2,1)S(1)} collective-permute-done((bf16[16,32,128]{2,1,0:T(8,128)(2,1)S(1)}, bf16[16,32,128]{2,1,0:T(8,128)(2,1)S(1)}, u32[]{:S(2)}, u32[]{:S(2)}) %collective-permute-start.4) | collective-permute-done | bytes 131104 | tf_op jit(solution)/shard_map/ppermute | solution.py:450
  128.3 18.0 %all_to_all.25.last_ref = bf16[16,64,128]{2,1,0:T(8,128)(2,1)S(1)} all-to-all(bf16[16,64,128]{2,1,0:T(8,128)(2,1)S(1)} %collect.1), channel_id=1, replica_groups=mesh['x'=4,'y_lo'=2,'core'=2,'z'=8,'y_hi'=2] {'z','y_hi'}, dimensions={0} | all-to-all | bytes 524288 | tf_op jit(solution)/shard_map/all_to_all | solution.py:403
  146.3 1.3 finish.1
  (32 shorter events, 3.5 us)
Async XLA Ops:
  7.2 72.5 %all-gather.5.cloned.1.call-start = ((), (), s32[]{:S(2)}) async-start(), calls=%async_computation.5 | async-start | bytes 2228224 | tf_op jit(solution)/shard_map/all_gather | solution.py:434
  8.6 0.8 copy-start
  9.4 0.7 copy-start.4
  10.0 34.3 %copy-start.1 = (bf16[1,16,1024]{2,1,0:T(8,128)(2,1)S(1)}, bf16[1,16,1024]{2,1,0:T(8,128)(2,1)}, u32[]{:S(2)}) copy-start(bf16[1,16,1024]{2,1,0:T(8,128)(2,1)} %targets_ref.1) | copy-start | bytes 98308
  10.0 34.3 %copy-start.3 = (f32[1024]{0:T(1024)S(1)}, f32[1024]{0:T(1024)}, u32[]{:S(2)}) copy-start(f32[1024]{0:T(1024)} %param.14) | copy-start | bytes 12292
  12.2 32.1 %all-to-all-start = ((bf16[16,16,1152]{2,1,0:T(8,128)(2,1)}), bf16[16,16,1152]{2,1,0:T(8,128)(2,1)S(1)}, u32[]{:S(2)}, u32[]{:S(2)}) async-start(bf16[16,16,1152]{2,1,0:T(8,128)(2,1)} %get-tuple-element.23), calls=%async_computation | async-start | bytes 1179648 | tf_op jit(solution)/shard_map/all_to_all | solution.py:403
  44.3 16.2 %copy-start.9 = (bf16[1024]{0:T(1024)(128)(2,1)S(1)}, bf16[1024]{0:T(1024)(128)(2,1)}, u32[]{:S(2)}) copy-start(bf16[1024]{0:T(1024)(128)(2,1)} %param.17) | copy-start | bytes 6148
  44.3 35.3 %copy-start.2 = (f32[7,1024]{1,0:T(8,128)S(1)}, f32[7,1024]{1,0:T(8,128)}, u32[]{:S(2)}) copy-start(f32[7,1024]{1,0:T(8,128)} %taps_ref.1) | copy-start | bytes 86020
  51.4 28.3 %all-to-all-start.1 = ((bf16[16,192,128]{2,1,0:T(8,128)(2,1)}), bf16[16,192,128]{2,1,0:T(8,128)(2,1)S(1)}, u32[]{:S(2)}, u32[]{:S(2)}) async-start(bf16[16,192,128]{2,1,0:T(8,128)(2,1)} %get-tuple-element.25), calls=%async_computation.1 | async-start | bytes 1572864 | tf_op jit(solution)/shard_map/all_to_all | solution.py:403
  87.6 15.7 %all-to-all-start.2 = ((bf16[16,64,128]{2,1,0:T(8,128)(2,1)}), bf16[16,64,128]{2,1,0:T(8,128)(2,1)S(1)}, u32[]{:S(2)}, u32[]{:S(2)}) async-start(bf16[16,64,128]{2,1,0:T(8,128)(2,1)} %bitcast.10), calls=%async_computation.2 | async-start | bytes 524288 | tf_op jit(solution)/shard_map/all_to_all | solution.py:403
  92.4 1.7 %collective-permute-start = (bf16[8,192,128]{2,1,0:T(8,128)(2,1)S(1)}, bf16[8,192,128]{2,1,0:T(8,128)(2,1)S(1)}, u32[]{:S(2)}, u32[]{:S(2)}) collective-permute-start(bf16[8,192,128]{2,1,0:T(8,128)(2,1)S(1)} %get-tuple-element.36), channel_id=1, source_target_pairs={{0,16},{16,0},{1,17},{17,1},{2,18},{18,2},{3,19},{19,3},{4,20},{20... | collective-permute-start | bytes 1179656 | tf_op jit(solution)/shard_map/ppermute | solution.py:444
  93.7 9.6 %copy-start.5 = (bf16[1024,256]{1,0:T(8,128)(2,1)S(1)}, bf16[1024,256]{1,0:T(8,128)(2,1)}, u32[]{:S(2)}) copy-start(bf16[1024,256]{1,0:T(8,128)(2,1)} %prepare.1.normed_ref) | copy-start | bytes 1572868
  93.7 9.6 %copy-start.8 = (bf16[64,2048]{1,0:T(8,128)(2,1)S(1)}, bf16[64,2048]{1,0:T(8,128)(2,1)}, u32[]{:S(2)}) copy-start(bf16[64,2048]{1,0:T(8,128)(2,1)} %get-tuple-element.31.query_ref) | copy-start | bytes 786436
  95.7 21.8 %collective-permute-start.1 = (bf16[2,16,32,128]{3,2,1,0:T(8,128)(2,1)S(1)}, bf16[2,16,32,128]{3,2,1,0:T(8,128)(2,1)S(1)}, u32[]{:S(2)}, u32[]{:S(2)}) collective-permute-start(bf16[2,16,32,128]{3,2,1,0:T(8,128)(2,1)S(1)} %get-tuple-element.38), channel_id=1, source_target_pairs={{0,64},{64,128},{128,192},{192,0},{1,65},{65,129},{129,193},{193,1... | collective-permute-start | bytes 786440 | tf_op jit(solution)/shard_map/ppermute | solution.py:447
  98.3 19.2 %collective-permute-start.2 = (bf16[2,16,32,128]{3,2,1,0:T(8,128)(2,1)S(1)}, bf16[2,16,32,128]{3,2,1,0:T(8,128)(2,1)S(1)}, u32[]{:S(2)}, u32[]{:S(2)}) collective-permute-start(bf16[2,16,32,128]{3,2,1,0:T(8,128)(2,1)S(1)} %get-tuple-element.39), channel_id=1, source_target_pairs={{0,128},{64,192},{128,0},{192,64},{1,129},{65,193},{129,1},{193,65... | collective-permute-start | bytes 786440 | tf_op jit(solution)/shard_map/ppermute | solution.py:447
  100.0 17.4 %collective-permute-start.3 = (bf16[2,16,32,128]{3,2,1,0:T(8,128)(2,1)S(1)}, bf16[2,16,32,128]{3,2,1,0:T(8,128)(2,1)S(1)}, u32[]{:S(2)}, u32[]{:S(2)}) collective-permute-start(bf16[2,16,32,128]{3,2,1,0:T(8,128)(2,1)S(1)} %get-tuple-element.40), channel_id=1, source_target_pairs={{0,192},{64,0},{128,64},{192,128},{1,193},{65,1},{129,65},{193,129... | collective-permute-start | bytes 786440 | tf_op jit(solution)/shard_map/ppermute | solution.py:447
  103.3 1.6 %copy-start.6 = (f32[16,256,128]{2,1,0:T(8,128)S(1)}, f32[16,256,128]{2,1,0:T(8,128)}, u32[]{:S(2)}) copy-start(f32[16,256,128]{2,1,0:T(8,128)} %get-tuple-element.29.probs_ref) | copy-start | bytes 6291460
  104.9 1.2 copy-start.7
  112.1 15.5 %all-to-all-start.3 = ((bf16[16,96,128]{2,1,0:T(8,128)(2,1)}), bf16[16,96,128]{2,1,0:T(8,128)(2,1)S(1)}, u32[]{:S(2)}, u32[]{:S(2)}) async-start(bf16[16,96,128]{2,1,0:T(8,128)(2,1)} %backward.1), calls=%async_computation.3 | async-start | bytes 786432 | tf_op jit(solution)/shard_map/all_to_all | solution.py:403
  117.6 10.0 %collective-permute-start.4 = (bf16[16,32,128]{2,1,0:T(8,128)(2,1)S(1)}, bf16[16,32,128]{2,1,0:T(8,128)(2,1)S(1)}, u32[]{:S(2)}, u32[]{:S(2)}) collective-permute-start(bf16[16,32,128]{2,1,0:T(8,128)(2,1)S(1)} %get-tuple-element.43), channel_id=1, source_target_pairs={{0,32},{32,0},{1,33},{33,1},{2,34},{34,2},{3,35},{35,3},{4,36},{36... | collective-permute-start | bytes 393224 | tf_op jit(solution)/shard_map/ppermute | solution.py:450
Sparse Core Ops, SparseCore 0:
  9.8 42.8 all-gather.4

commit v3 on v2

v3 whole, which is shorter than its diff:
```python
import jax
import jax.numpy as jnp
from jax import lax
from jax.experimental import pallas as pl
from jax.experimental.pallas import tpu as pltpu
from jax.sharding import Mesh
from jax.sharding import PartitionSpec as P


D = 1024
H = 16
HS = 64
HALF = HS // 2
L = 256
KMAX = 128
KW = 7
CLIPS = 16
COPIES = 16
QALL = COPIES * KMAX
NORM_EPSILON = 1e-05
MASKED_SCORE = -1e30
SCORE_SCALE = HS**-0.5
ROWS = L // COPIES
LOSS_SCALE = (KMAX * CLIPS * COPIES) ** -0.5
PAD = 8
LANES = 256
BLOCK = 128
EARLY = D // 2
LATE = (D - EARLY) // BLOCK * ROWS
QKV = HS + HALF
EXTRA = 16
GROUP = 8
VMEM_LIMIT = 20 * 1024 * 1024

XS, YS = 4, 2
CLIP = ("x", "y_lo", "core")
COPY = ("z", "y_hi")
F32 = jnp.float32
BF16 = jnp.bfloat16

VMEM = pl.BlockSpec(memory_space=pltpu.VMEM)
SMEM = pl.BlockSpec(memory_space=pltpu.SMEM)
HBM = pl.BlockSpec(memory_space=pltpu.HBM)


def mm(left, right):
    return jnp.dot(left, right, preferred_element_type=F32)


def mm_nt(left, right):
    return lax.dot_general(left, right, (((1,), (1,)), ((), ())), preferred_element_type=F32)


def call(kernel, name, microseconds, out_shape, in_specs, out_specs, scratch=()):
    return pl.pallas_call(
        kernel,
        out_shape=[
            pltpu.HBM(shape, dtype) if spec is HBM else jax.ShapeDtypeStruct(shape, dtype)
            for (shape, dtype), spec in zip(out_shape, out_specs)
        ],
        in_specs=in_specs,
        out_specs=out_specs,
        scratch_shapes=list(scratch),
        compiler_params=pltpu.CompilerParams(vmem_limit_bytes=VMEM_LIMIT),
        cost_estimate=pl.CostEstimate(
            flops=int(microseconds * 1e9), bytes_accessed=1024, transcendentals=0
        ),
        name=name,
    )


def in_hbm(array):
    return pltpu.with_memory_space_constraint(array, pltpu.HBM)


def pack_kernel(
    place_ref, count_ref, frames_hbm, targets_hbm, index_hbm, w_ref, wo_hbm,
    sent_ref, index_out, weights_ref, w_buf, wo_buf, frames_ref, targets_ref, index_ref, sems,
):
    head = place_ref[0]
    copies = []
    load_index = pltpu.make_async_copy(index_hbm.at[0], index_ref, sems.at[3])
    load_index.start()
    load_frames = pltpu.make_async_copy(frames_hbm.at[0], frames_ref, sems.at[4])
    load_frames.start()
    load_targets = pltpu.make_async_copy(targets_hbm.at[0, :, :EARLY], targets_ref, sems.at[6])
    load_targets.start()
    load_out = pltpu.make_async_copy(wo_hbm, wo_buf, sems.at[5])
    load_out.start()
    for part in range(3):
        begin = pl.multiple_of(part * D + (head // 2) * BLOCK, BLOCK)
        copies.append(
            pltpu.make_async_copy(w_ref.at[:, pl.ds(begin, BLOCK)], w_buf.at[part], sems.at[part])
        )
        copies[part].start()
    lanes = lax.broadcasted_iota(jnp.int32, (ROWS, KMAX), 1)
    load_index.wait()
    index = jnp.broadcast_to(index_ref[...], (ROWS, KMAX))
    index = jnp.where(lanes < count_ref[0, 0], index, L).astype(F32).astype(BF16)
    index_out[...] = index
    load_frames.wait()
    load_targets.wait()
    for m in range(COPIES):
        sent_ref[m, :, :D] = frames_ref[...]
        sent_ref[m, :, D : D + KMAX] = index
        sent_ref[m, :, D + KMAX :] = targets_ref[...]
    odd = head % 2 == 1
    for part in range(3):
        copies[part].wait()
    q, k, v = [
        jnp.where(odd, w_buf[part, :, HS:].astype(F32), w_buf[part, :, :HS].astype(F32)) for part in range(3)
    ]
    weights_ref[:HS, :] = jnp.concatenate([q, k], axis=1).astype(BF16)
    weights_ref[HS:QKV, :] = jnp.concatenate([v[:HALF], v[HALF:]], axis=1).astype(BF16)
    load_out.wait()
    for a in range(D // BLOCK):
        weights_ref[QKV + a * HS : QKV + (a + 1) * HS, :] = wo_buf[:, a * BLOCK : (a + 1) * BLOCK]


def pack(place, count, frames, targets, index, w_qkv, w_out):
    return call(
        pack_kernel,
        "pack",
        1,
        [((COPIES, ROWS, D + KMAX + EARLY), BF16), ((ROWS, KMAX), BF16), ((QKV + HS * D // BLOCK, BLOCK), BF16)],
        [SMEM, SMEM] + [HBM] * 5,
        [VMEM, VMEM, VMEM],
        [
            pltpu.VMEM((3, HS, BLOCK), BF16),
            pltpu.VMEM((HS, D), BF16),
            pltpu.VMEM((ROWS, D), BF16),
            pltpu.VMEM((ROWS, EARLY), BF16),
            pltpu.VMEM((1, KMAX), jnp.int32),
            pltpu.SemaphoreType.DMA((7,)),
        ],
    )(place, count, in_hbm(frames), in_hbm(targets), in_hbm(index), in_hbm(w_qkv), in_hbm(w_out))


def normalize(got_ref, gain_hbm, gain_ref, sem):
    load = pltpu.make_async_copy(gain_hbm, gain_ref, sem)
    load.start()
    values = got_ref[:, :D].astype(F32)
    center = values - jnp.mean(values, axis=1, keepdims=True)
    spread = jnp.mean(center * center, axis=1, keepdims=True)
    load.wait()
    return (center * lax.rsqrt(spread + NORM_EPSILON) * gain_ref[...]).astype(BF16)


def forward_kernel(
    got_ref, w_ref, gain_hbm, targets_ref, out_ref, probs_out, pick_out, qkv_out,
    probs_ref, pick_ref, qkv_ref, wqk_ref, wv_ref, gain_ref, sems,
):
    for m in range(COPIES):
        for a in range((D - EARLY) // BLOCK):
            lanes = slice(EARLY + a * BLOCK, EARLY + (a + 1) * BLOCK)
            out_ref[m, HS + a * ROWS : HS + (a + 1) * ROWS, :] = targets_ref[0, :, lanes]
    normed = normalize(got_ref, gain_hbm, gain_ref, sems.at[3 * COPIES // GROUP])
    for c in range(CLIPS):
        block = w_ref[c % 2, c // (2 * YS), c // 2 % YS]
        wqk_ref[c * HS : (c + 1) * HS, :] = block[:HS]
        wv_ref[c * HS : c * HS + HALF, :] = block[HS:, :HS]
        wv_ref[c * HS + HALF : (c + 1) * HS, :] = block[HS:, HS:]
    qk = mm(normed, wqk_ref[...]).astype(BF16).astype(F32)
    v = mm(normed, wv_ref[...]).astype(BF16).astype(F32)
    qk_t = qk.T
    qkv_t = jnp.concatenate([qk_t[:HS] * SCORE_SCALE, qk_t[HS:], v.T], axis=0).astype(BF16)
    rows = lax.broadcasted_iota(jnp.int32, (L, KMAX), 0).astype(F32)
    first = lax.broadcasted_iota(jnp.int32, (EXTRA, KMAX), 0) == 0
    one_row = jnp.where(first, 1.0, 0.0).astype(BF16)
    saves = []
    for begin in range(0, COPIES, GROUP):
        group = range(begin, begin + GROUP)
        index = [got_ref[m * ROWS : (m + 1) * ROWS, D : D + KMAX].astype(F32)[:1] for m in group]
        pick = [jnp.where(rows == i, 1.0, 0.0).astype(BF16) for i in index]
        for m, p in zip(group, pick):
            pick_ref[:, m * KMAX : (m + 1) * KMAX] = p
        qkv = [mm(qkv_t, p).astype(BF16) for p in pick]
        for m, a in zip(group, qkv):
            qkv_ref[m] = a
        bias = [jnp.where(first & (i > L - 0.5), MASKED_SCORE, 0.0).astype(BF16) for i in index]
        queries = [jnp.concatenate([a[:HS], one_row], axis=0) for a in qkv]
        keys = [jnp.concatenate([a[HS : 2 * HS], e], axis=0).T for a, e in zip(qkv, bias)]
        scores = [mm(k, q) for k, q in zip(keys, queries)]
        raised = [jnp.exp(a - jnp.max(a, axis=0, keepdims=True)) for a in scores]
        probs = [a * (1.0 / jnp.sum(a, axis=0, keepdims=True)) for a in raised]
        for m, p in zip(group, probs):
            probs_ref[m] = p
        ctx = [mm(a[2 * HS :], p.astype(BF16)) for a, p in zip(qkv, probs)]
        for m, a in zip(group, ctx):
            out_ref[m, :HS, :] = a.astype(BF16)
        part = pl.ds(begin, GROUP)
        lanes = pl.ds(begin * KMAX, GROUP * KMAX)
        for here, there in (
            (probs_ref.at[part], probs_out.at[part]),
            (qkv_ref.at[part], qkv_out.at[part]),
            (pick_ref.at[:, lanes], pick_out.at[:, lanes]),
        ):
            saves.append(pltpu.make_async_copy(here, there, sems.at[len(saves)]))
            saves[-1].start()
    for save in saves:
        save.wait()


def forward(got, weights, gain, targets):
    return call(
        forward_kernel,
        "forward",
        0.1,
        [
            ((COPIES, HS + LATE, KMAX), BF16),
            ((COPIES, KMAX, KMAX), F32),
            ((L, QALL), BF16),
            ((COPIES, 3 * HS, KMAX), BF16),
        ],
        [VMEM, VMEM, HBM, VMEM],
        [VMEM, HBM, HBM, HBM],
        [
            pltpu.VMEM((COPIES, KMAX, KMAX), F32),
            pltpu.VMEM((L, QALL), BF16),
            pltpu.VMEM((COPIES, 3 * HS, KMAX), BF16),
            pltpu.VMEM((D, 2 * HS), BF16),
            pltpu.VMEM((D, HS), BF16),
            pltpu.VMEM((1, D), F32),
            pltpu.SemaphoreType.DMA((3 * COPIES // GROUP + 1,)),
        ],
    )(got, weights, in_hbm(gain), targets)


def prepare_kernel(got_ref, gain_hbm, out_ref, buf, gain_ref, sems):
    buf[...] = normalize(got_ref, gain_hbm, gain_ref, sems.at[1]).T
    save = pltpu.make_async_copy(buf, out_ref, sems.at[0])
    save.start()
    save.wait()


def prepare(got, gain):
    return call(
        prepare_kernel,
        "prepare",
        2,
        [((D, L), BF16)],
        [VMEM, HBM],
        [HBM],
        [pltpu.VMEM((D, L), BF16), pltpu.VMEM((1, D), F32), pltpu.SemaphoreType.DMA((2,))],
    )(got, in_hbm(gain))[0]


def decoder_kernel(
    place_ref, count_ref, recv_ref, got_ref, index_ref, embed_ref, taps_ref, *refs
):
    w_refs = refs[: 2 * XS]
    encoded_ref, dctx_ref, ctx_out, denc_out, share_out = refs[2 * XS : 2 * XS + 5]
    ctx_ref, denc_ref, share_ref, field_ref, error_ref, dfilled_ref, sems = refs[2 * XS + 5 :]
    chunks = D // LANES
    core, x = place_ref[1], place_ref[2]
    parts = []
    for s in range(XS):
        chip = YS * lax.rem(x + XS - s, XS)
        clips = [2 * (chip + t) + side for side in (core, 1 - core) for t in range(YS)]
        weights = [
            jnp.concatenate(
                [w_refs[s][:, a].reshape(YS * HS, BLOCK), w_refs[XS + s][:, a].reshape(YS * HS, BLOCK)], axis=0
            )
            for a in range(D // BLOCK)
        ]
        parts.append((clips, weights))
    live = lax.broadcasted_iota(jnp.int32, (KMAX, 1), 0) < count_ref[0, 0]
    rows = lax.broadcasted_iota(jnp.int32, (L, KMAX), 0).astype(F32)
    hit = jnp.where(rows == index_ref[...].astype(F32)[:1], 1.0, 0.0)
    masked = 1.0 - jnp.sum(hit, axis=1, keepdims=True)
    place = hit.astype(BF16)
    pick = hit.T.astype(BF16)
    ctx_ref[...] = recv_ref[:, :HS, :]
    saves = [
        pltpu.make_async_copy(here, there, sems.at[at])
        for at, (here, there) in enumerate(
            ((ctx_ref, ctx_out), (denc_ref, denc_out), (share_ref, share_out))
        )
    ]
    saves[0].start()
    ctx = [
        jnp.concatenate([ctx_ref[clip] for clip in clips], axis=0).T for clips, weights in parts
    ]
    for i in range(CLIPS // 2):
        share_ref[i, :HS, :] = ctx_ref[2 * i + 1 - core]
    reach = KW // 2
    blocks = D // BLOCK
    for ref in (field_ref, error_ref):
        ref[:PAD] = jnp.zeros((PAD, D), F32)
        ref[PAD + L :] = jnp.zeros((PAD, D), F32)
    inside = slice(PAD, PAD + L)
    columns = [slice(c * LANES, (c + 1) * LANES) for c in range(chunks)]
    inputs = [mm(pick, got_ref[:, lanes]) for lanes in columns]
    per = LANES // BLOCK
    mixed = inputs
    for left, (clips, weights) in zip(ctx, parts):
        wide = [
            jnp.concatenate(weights[c * per : (c + 1) * per], axis=1) for c in range(chunks)
        ]
        mixed = [m + mm(left, w) for m, w in zip(mixed, wide)]
    encoded = [jnp.where(live, m, 0.0).astype(BF16) for m in mixed]
    for lanes, e in zip(columns, encoded):
        encoded_ref[:, lanes] = e
    for lanes, e in zip(columns, encoded):
        field_ref[inside, lanes] = mm(place, e) + masked * embed_ref[:, lanes].astype(F32)
    for a in range(blocks):
        lanes = slice(a * BLOCK, (a + 1) * BLOCK)
        predicted = taps_ref[:1, lanes] * field_ref[PAD - reach : PAD - reach + L, lanes]
        for t in range(1, KW):
            begin = PAD - reach + t
            predicted = predicted + taps_ref[t : t + 1, lanes] * field_ref[begin : begin + L, lanes]
        if (a + 1) * BLOCK <= EARLY:
            begin = D + KMAX + a * BLOCK
            wanted = got_ref[:, begin : begin + BLOCK]
        else:
            begin = HS + (a * BLOCK - EARLY) // BLOCK * ROWS
            wanted = recv_ref[:, begin : begin + ROWS, :].reshape(L, BLOCK)
        error_ref[inside, lanes] = masked * (predicted - wanted.astype(F32)) * LOSS_SCALE
    for a in range(blocks):
        lanes = slice(a * BLOCK, (a + 1) * BLOCK)
        dfilled = taps_ref[:1, lanes] * error_ref[PAD + reach : PAD + reach + L, lanes]
        for t in range(1, KW):
            begin = PAD + reach - t
            dfilled = dfilled + taps_ref[t : t + 1, lanes] * error_ref[begin : begin + L, lanes]
        dfilled_ref[:, lanes] = dfilled.astype(BF16)
    denc = [mm(pick, dfilled_ref[:, lanes]).astype(BF16) for lanes in columns]
    for c in range(chunks):
        denc_ref[:, columns[c]] = denc[c]
        for i in range(per):
            share_ref[c * per + i, HS:, :] = denc[c][:, i * BLOCK : (i + 1) * BLOCK]
    saves[1].start()
    saves[2].start()
    denc = denc_ref[...]
    for clips, weights in parts:
        dctx = mm_nt(jnp.concatenate(weights, axis=1), denc).astype(BF16)
        for r, clip in enumerate(clips):
            dctx_ref[clip] = dctx[r * HS : (r + 1) * HS]
    for save in saves:
        save.wait()


def decoder(place, count, recv, got, w_out, index, embed, taps):
    return call(
        decoder_kernel,
        "decoder",
        5,
        [
            ((KMAX, D), BF16),
            ((H, HS, KMAX), BF16),
            ((H, HS, KMAX), BF16),
            ((KMAX, D), BF16),
            ((CLIPS // 2, HS + KMAX, KMAX), BF16),
        ],
        [SMEM, SMEM] + [VMEM] * (5 + 2 * XS),
        [VMEM] * 2 + [HBM] * 3,
        [
            pltpu.VMEM((H, HS, KMAX), BF16),
            pltpu.VMEM((KMAX, D), BF16),
            pltpu.VMEM((CLIPS // 2, HS + KMAX, KMAX), BF16),
            pltpu.VMEM((L + 2 * PAD, D), F32),
            pltpu.VMEM((L + 2 * PAD, D), F32),
            pltpu.VMEM((L, D), BF16),
            pltpu.SemaphoreType.DMA((3,)),
        ],
    )(place, count, recv, got, index, embed, taps, *w_out)


def out_grad_kernel(place_ref, ctx_ref, denc_ref, share_ref, *refs):
    outs, both_ref = refs[:XS], refs[XS]
    core, x, y = place_ref[1], place_ref[2], place_ref[3]
    for a in range(D // BLOCK):
        lanes = slice(a * BLOCK, (a + 1) * BLOCK)
        both_ref[:KMAX, lanes] = denc_ref[:, lanes]
        both_ref[KMAX:, lanes] = share_ref[a, HS:, :]
    for r in range(XS):
        for s in range(YS):
            chip = YS * lax.rem(x + r, XS) + lax.rem(y + s, YS)
            left = jnp.concatenate([ctx_ref[2 * chip + core], share_ref[chip, :HS, :]], axis=1)
            block = mm(left, both_ref[...])
            upper, lower = block[:HALF], block[HALF:]
            for a in range(D // BLOCK):
                lanes = slice(a * BLOCK, (a + 1) * BLOCK)
                first, second = upper[:, lanes], lower[:, lanes]
                even = jnp.concatenate([first[:, :HS], second[:, :HS]], axis=1)
                odd = jnp.concatenate([first[:, HS:], second[:, HS:]], axis=1)
                outs[r][s, 2 * a] = even.astype(BF16)
                outs[r][s, 2 * a + 1] = odd.astype(BF16)


def out_grad(place, ctx, denc, share):
    return call(
        out_grad_kernel,
        "out_grad",
        1,
        [((YS, COPIES, HALF, BLOCK), BF16)] * XS,
        [SMEM] + [VMEM] * 3,
        [VMEM] * XS,
        [pltpu.VMEM((2 * KMAX, D), BF16)],
    )(place, ctx, denc, share)


def backward_kernel(
    dctx_ref, probs_hbm, pick_hbm, qkv_hbm, normed_hbm, out_ref,
    probs_ref, pick_ref, qkv_ref, normed_ref, dqkv_ref, sems,
):
    loads = []
    for at, (there, here) in enumerate(
        ((qkv_hbm, qkv_ref), (probs_hbm, probs_ref), (pick_hbm, pick_ref), (normed_hbm, normed_ref))
    ):
        loads.append(pltpu.make_async_copy(there, here, sems.at[at]))
        loads[at].start()
    loads[0].wait()
    loads[1].wait()
    for begin in range(0, COPIES, GROUP):
        group = range(begin, begin + GROUP)
        dctx = [dctx_ref[m] for m in group]
        qkv = [qkv_ref[m] for m in group]
        probs = [probs_ref[m] for m in group]
        dprobs = [mm(a[2 * HS :].T, d) for a, d in zip(qkv, dctx)]
        along = [jnp.sum(p * d, axis=0, keepdims=True) for p, d in zip(probs, dprobs)]
        dscores = [(p * (d - a)).astype(BF16) for p, d, a in zip(probs, dprobs, along)]
        dvalue = [mm(p.astype(BF16), d.T) for p, d in zip(probs, dctx)]
        dkey = [mm(d, a[:HS].T) for d, a in zip(dscores, qkv)]
        dquery = [(mm(a[HS : 2 * HS], d) * SCORE_SCALE).T for a, d in zip(qkv, dscores)]
        for m, q, k, v in zip(group, dquery, dkey, dvalue):
            dqkv = jnp.concatenate([q, k, v], axis=1)
            dqkv_ref[m * KMAX : (m + 1) * KMAX, :] = dqkv.astype(BF16)
    loads[2].wait()
    loads[3].wait()
    total = mm(pick_ref[...], dqkv_ref[...]).astype(BF16)
    grad = mm(normed_ref[...], total).astype(BF16)
    for c in range(CLIPS):
        block = grad[c * HS : (c + 1) * HS]
        out_ref[c, :HS, :] = block[:, : 2 * HS]
        out_ref[c, HS:, :HS] = block[:HALF, 2 * HS :]
        out_ref[c, HS:, HS:] = block[HALF:, 2 * HS :]


def backward(dctx, probs, pick, qkv, normed):
    return call(
        backward_kernel,
        "backward",
        5,
        [((CLIPS, HS + HALF, BLOCK), BF16)],
        [VMEM] + [HBM] * 4,
        [VMEM],
        [
            pltpu.VMEM((COPIES, KMAX, KMAX), F32),
            pltpu.VMEM((L, QALL), BF16),
            pltpu.VMEM((COPIES, 3 * HS, KMAX), BF16),
            pltpu.VMEM((D, L), BF16),
            pltpu.VMEM((QALL, 3 * HS), BF16),
            pltpu.SemaphoreType.DMA((4,)),
        ],
    )(dctx, in_hbm(probs), in_hbm(pick), in_hbm(qkv), in_hbm(normed))[0]


def collect_kernel(place_ref, terms_ref, mine_ref, other_ref, out_ref):
    head = place_ref[0]
    out_ref[:, :HALF, :] = (mine_ref[...].astype(F32) + other_ref[...].astype(F32)).astype(BF16)
    out_ref[:, HALF:, :] = jnp.zeros((COPIES, HALF, BLOCK), BF16)
    term = jnp.sum(terms_ref[...].astype(F32), axis=0)
    upper, lower = term[:HALF], term[HALF:HS]
    query = jnp.concatenate([upper[:, :HS], lower[:, :HS]], axis=1)
    key = jnp.concatenate([upper[:, HS:], lower[:, HS:]], axis=1)
    for part, piece in enumerate((query, key, term[HS:])):
        out_ref[(part * H + head) // 3, HALF:, :] = piece.astype(BF16)


def collect(place, terms, mine, other):
    return call(
        collect_kernel,
        "collect",
        1,
        [((COPIES, HS, BLOCK), BF16)],
        [SMEM] + [VMEM] * 3,
        [VMEM],
    )(place, terms, mine, other)[0]


def finish_kernel(place_ref, last_ref, qkv_ref, out_ref):
    total = jnp.sum(last_ref[:, :HALF, :].astype(F32), axis=0)
    out_ref[:HALF, :] = total[:, :HS]
    out_ref[HALF:, :] = total[:, HS:]
    for i in range(3):
        block = last_ref[lax.rem(3 * place_ref[0] + i, COPIES), HALF:, :].astype(F32)
        qkv_ref[:HALF, i * HS : (i + 1) * HS] = block[:, :HS]
        qkv_ref[HALF:, i * HS : (i + 1) * HS] = block[:, HS:]


def finish(place, last):
    return call(
        finish_kernel,
        "finish",
        1,
        [((HS, 3 * HS), F32), ((HS, HS), F32)],
        [SMEM, VMEM],
        [VMEM] * 2,
    )(place, last)


def swap(array, axes):
    return lax.all_to_all(array, axes, 0, 0, tiled=True)


def total(*parts):
    result = parts[0].astype(F32)
    for part in parts[1:]:
        result = result + part.astype(F32)
    return result.astype(BF16)


def per_device(
    frames,
    targets,
    kept_index,
    kept_count,
    fill_slot,
    norm_gain,
    w_qkv,
    w_out,
    mask_embed,
    dec_kernel,
):
    place = jnp.stack(
        [lax.axis_index(COPY), lax.axis_index("core"), lax.axis_index("x"), lax.axis_index("y_lo")]
    )
    gain = norm_gain[None, :]
    sent, index, weights = pack(place, kept_count, frames, targets, kept_index, w_qkv, w_out)
    got = swap(sent, COPY).reshape(L, D + KMAX + EARLY)
    weights = lax.all_gather(weights, "y_lo", axis=0)
    near = weights[:, QKV:].reshape(YS, D // BLOCK, HS, BLOCK)
    weights = weights[:, :QKV]
    for axis in ("x", "core"):
        weights = lax.all_gather(weights, axis, axis=0)

    sent, probs, pick, qkv = forward(got, weights, gain, targets)
    normed = prepare(got, gain)
    recv = swap(sent, COPY)
    near, sent = lax.optimization_barrier((near, sent))
    w_out = [near]
    for r in range(1, XS):
        w_out.append(lax.ppermute(near, "x", [(i, (i + r) % XS) for i in range(XS)]))
    w_out += [lax.ppermute(part, "core", [(0, 1), (1, 0)]) for part in w_out]
    encoded, dctx, ctx, denc, share = decoder(
        place, kept_count, recv, got, w_out, index, mask_embed[None, :], dec_kernel
    )
    dctx = swap(dctx, COPY)

    share = lax.ppermute(share, "core", [(0, 1), (1, 0)])
    parts = list(out_grad(place, ctx, denc, share))
    for r in range(1, XS):
        parts[r] = lax.ppermute(parts[r], "x", [(i, (i + r) % XS) for i in range(XS)])
    mine = total(*[part[0] for part in parts])
    other = total(*[part[1] for part in parts])
    other = lax.ppermute(other, "y_lo", [(0, 1), (1, 0)])

    terms = swap(backward(dctx, probs, pick, qkv, normed), CLIP)
    grad_qkv, grad_out = finish(place, swap(collect(place, terms, mine, other), COPY))
    return (encoded[None, None], grad_qkv, grad_out)


def solution(mesh):
    fine = Mesh(mesh.devices.reshape(XS, YS, 2, 8, 2), ("x", "y_lo", "core", "z", "y_hi"))
    in_specs = (
        P(CLIP, COPY, None),
        P(CLIP, COPY, None),
        P(CLIP, COPY, None),
        P(CLIP, COPY),
        P(CLIP, COPY, None),
        P(),
        P(CLIP, None),
        P(CLIP, None),
        P(),
        P(),
    )
    out_specs = (P(CLIP, COPY, None, None), P(CLIP, COPY), P(CLIP, COPY))
    return jax.shard_map(
        per_device, mesh=fine, in_specs=in_specs, out_specs=out_specs, check_vma=False
    )
```

time: 157 us -> 137 us (0.87)
  between operations: 14.8 us -> 1.47 us
  starting transfers between devices: 38.1 us -> 43.2 us
  Pallas kernels: 27.9 us -> 22.9 us
  local copies, waits for them, and re-layouts: 4.26 us -> 0.05 us
  waiting for transfers between devices: 30.3 us -> 27.2 us
    all_to_all x4, waiting for transfers between devices: 21.2 us -> 5.83 us  [swap(): return lax.all_to_all(array, axes, 0, 0, tiled=True)]
    ppermute x0 -> x7, waiting for transfers between devices: none -> 12.5 us  [the longest x3 11.2 us: per_device(): lax.ppermute(near, 'x', [(i, (i + r) % XS) for i in range(XS)])]
    all_gather x0 -> x1, blocking collectives: none -> 6.9 us  [per_device(): weights = lax.all_gather(weights, 'y_lo', axis=0)]
    all_gather x3 -> x2, blocking collectives: 20.8 us -> 14.7 us  [per_device(): weights = lax.all_gather(weights, axis, axis=0)]
    ppermute x0 -> x7, starting transfers between devices: none -> 4.69 us  [the longest x3 4.17 us: per_device(): lax.ppermute(near, 'x', [(i, (i + r) % XS) for i in range(XS)])]
    unnamed x20 -> x12, local copies, waits for them, and re-layouts: 4.26 us -> 0.03 us
    pallas_call x4, Pallas kernels: 18.5 us -> 15.2 us  [the longest x1 6.26 us: decoder(): call(decoder_kernel, 'decoder', 5, [((KMAX, D), BF16), ((H, HS, KMAX), BF...]
    all_to_all x4, starting transfers between devices: 30.5 us -> 33.2 us  [swap(): return lax.all_to_all(array, axes, 0, 0, tiled=True)]
  transfers between devices with their start and end apart: 10 -> 16, of which waited for: 4 -> 8; matrix products, arithmetic and copies ran while one was open for 0% -> 0% of each run, Pallas kernels for 12% -> 6%
where the time goes in v3:
time: 137 us; the launch traced here: 135 us
  starting transfers between devices  43.2 us (32%)
  blocking collectives  40.4 us (29%)
  waiting for transfers between devices  27.2 us (20%)
  Pallas kernels  22.9 us (17%)
  between operations  1.47 us (1%)
    all_to_all x4, starting transfers between devices, swap(): return lax.all_to_all(array, axes, 0, 0, tiled=True)  33.2 us
    all_to_all x1, blocking collectives, swap(): return lax.all_to_all(array, axes, 0, 0, tiled=True)  18.8 us
    all_gather x2, blocking collectives, per_device(): weights = lax.all_gather(weights, axis, axis=0)  14.7 us
    ppermute x3, waiting for transfers between devices, per_device(): lax.ppermute(near, 'x', [(i, (i + r) % XS) for i in range(XS)])  11.2 us
    ppermute x1, waiting for transfers between devices, per_device(): other = lax.ppermute(other, 'y_lo', [(0, 1), (1, 0)])  7.96 us
    all_gather x1, blocking collectives, per_device(): weights = lax.all_gather(weights, 'y_lo', axis=0)  6.9 us
    pallas_call x1, Pallas kernels, decoder(): call(decoder_kernel, 'decoder', 5, [((KMAX, D), BF16), ((H, HS, KMAX), BF...  6.26 us
    all_to_all x4, waiting for transfers between devices, swap(): return lax.all_to_all(array, axes, 0, 0, tiled=True)  5.83 us
  transfers between devices with their start and end apart: 16, of which 8 were waited for; matrix products, arithmetic and copies ran while one was open for 0% of the time, Pallas kernels for 6%

profile of v3, /device:TPU:32, one launch (start us, length us, event | category | flops | bytes accessed | tf_op | source)
XLA Modules:
  0.0 135.3 jit_solution(9117795836693218705)
XLA Ops:
  1.4 2.5 %pack.1 = (bf16[16,16,1664]{2,1,0:T(8,128)(2,1)}, bf16[16,128]{1,0:T(8,128)(2,1)S(1)}, bf16[608,128]{1,0:T(8,128)(2,1)S(1)}) custom-call(s32[4]{0:T(128)S(1)} %pad_add_fusion.place_ref, s32[1,1]{1,0:T(1,128)S(6)} %copy.12.count_ref, bf16[1,16,1024]{2,1,0:T(8,128)(2,1)} %frames_hbm.1, bf16[1,16,1024]{2,1,0:T(8,128)(2,1)} %targets_ref.1, ...), custom_call_target="tpu_custom_call" | custom-call | flops 1000000000 | bytes 1024 | tf_op jit(solution)/shard_map/pack/pallas_call | solution.py:121
  3.9 11.2 %all-to-all-start = ((bf16[16,16,1664]{2,1,0:T(8,128)(2,1)}), bf16[16,16,1664]{2,1,0:T(8,128)(2,1)S(1)}, u32[]{:S(2)}, u32[]{:S(2)}) async-start(bf16[16,16,1664]{2,1,0:T(8,128)(2,1)} %get-tuple-element.22), calls=%async_computation | async-start | bytes 1703936 | tf_op jit(solution)/shard_map/all_to_all | solution.py:503
  15.1 6.9 %all-gather = bf16[1216,128]{1,0:T(8,128)(2,1)S(1)} all-gather(bf16[608,128]{1,0:T(8,128)(2,1)S(1)} %get-tuple-element.23), channel_id=2, replica_groups=mesh['x'=4,'y_lo'=2,'core'=2,'z'=8,'y_hi'=2] {'y_lo'}, dimensions={0}, use_global_device_ids=true | all-gather | bytes 466944 | tf_op jit(solution)/shard_map/all_gather | solution.py:531
  22.0 12.5 %all-gather.1 = bf16[8,96,128]{2,1,0:T(8,128)(2,1)S(1)} all-gather(bf16[2,96,128]{2,1,0:T(8,128)(2,1)S(1)} %slice.40), channel_id=3, replica_groups=mesh['x'=4,'y_lo'=2,'core'=2,'z'=8,'y_hi'=2] {'x'}, dimensions={0}, use_global_device_ids=true | all-gather | bytes 245760 | tf_op jit(solution)/shard_map/all_gather | solution.py:535
  34.5 2.2 %all-gather.2 = bf16[8,2,96,128]{3,2,1,0:T(8,128)(2,1)S(1)} all-gather(bf16[4,2,96,128]{3,2,1,0:T(8,128)(2,1)S(1)} %bitcast.26), channel_id=4, replica_groups=mesh['x'=4,'y_lo'=2,'core'=2,'z'=8,'y_hi'=2] {'core'}, dimensions={0}, use_global_device_ids=true | all-gather | bytes 589824 | tf_op jit(solution)/shard_map/all_gather | solution.py:535
  37.7 4.7 %forward.1 = (bf16[16,128,128]{2,1,0:T(8,128)(2,1)}, f32[16,128,128]{2,1,0:T(8,128)}, bf16[256,2048]{1,0:T(8,128)(2,1)}, bf16[16,192,128]{2,1,0:T(8,128)(2,1)}) custom-call(bf16[256,1664]{1,0:T(8,128)(2,1)S(1)} %bitcast.15, bf16[2,4,2,96,128]{4,3,2,1,0:T(8,128)(2,1)S(1)} %bitcast.18, f32[1,1024]{1,0:T(1,128)} %bitcast.27, bf16[1,16,1024]{2,1,0:T(8,128)(2,1)S(1)} %copy-done), custom_call_target="tpu_custom_call" | custom-call | flops 100000000 | bytes 1024 | tf_op jit(solution)/shard_map/forward/pallas_call | solution.py:205
  42.4 8.4 %all-to-all-start.1 = ((bf16[16,128,128]{2,1,0:T(8,128)(2,1)}), bf16[16,128,128]{2,1,0:T(8,128)(2,1)S(1)}, u32[]{:S(2)}, u32[]{:S(2)}) async-start(bf16[16,128,128]{2,1,0:T(8,128)(2,1)} %get-tuple-element.24), calls=%async_computation.1 | async-start | bytes 1048576 | tf_op jit(solution)/shard_map/all_to_all | solution.py:503
  50.8 1.3 collective-permute-start
  52.1 2.7 %collective-permute-start.1 = (bf16[2,8,64,128]{3,2,1,0:T(8,128)(2,1)S(1)}, bf16[2,8,64,128]{3,2,1,0:T(8,128)(2,1)S(1)}, u32[]{:S(2)}, u32[]{:S(2)}) collective-permute-start(bf16[2,8,64,128]{3,2,1,0:T(8,128)(2,1)S(1)} %bitcast.20), channel_id=1, source_target_pairs={{0,128},{64,192},{128,0},{192,64},{1,129},{65,193},{129,1},{193,65... | collective-permute-start | bytes 786440 | tf_op jit(solution)/shard_map/ppermute | solution.py:543
  55.0 5.7 %collective-permute-done.refs_1_ = bf16[2,8,64,128]{3,2,1,0:T(8,128)(2,1)S(1)} collective-permute-done((bf16[2,8,64,128]{3,2,1,0:T(8,128)(2,1)S(1)}, bf16[2,8,64,128]{3,2,1,0:T(8,128)(2,1)S(1)}, u32[]{:S(2)}, u32[]{:S(2)}) %collective-permute-start) | collective-permute-done | bytes 262176 | tf_op jit(solution)/shard_map/ppermute | solution.py:543
  60.7 5.4 %collective-permute-done.1.refs_2_ = bf16[2,8,64,128]{3,2,1,0:T(8,128)(2,1)S(1)} collective-permute-done((bf16[2,8,64,128]{3,2,1,0:T(8,128)(2,1)S(1)}, bf16[2,8,64,128]{3,2,1,0:T(8,128)(2,1)S(1)}, u32[]{:S(2)}, u32[]{:S(2)}) %collective-permute-start.1) | collective-permute-done | bytes 262176 | tf_op jit(solution)/shard_map/ppermute | solution.py:543
  68.1 6.3 %decoder.1 = (bf16[128,1024]{1,0:T(8,128)(2,1)}, bf16[16,64,128]{2,1,0:T(8,128)(2,1)}, bf16[16,64,128]{2,1,0:T(8,128)(2,1)}, bf16[128,1024]{1,0:T(8,128)(2,1)}, bf16[8,192,128]{2,1,0:T(8,128)(2,1)}) custom-call(s32[4]{0:T(128)S(1)} %pad_add_fusion.place_ref, s32[1,1]{1,0:T(1,128)S(6)} %copy.12.count_ref, bf16[16,128,128]{2,1,0:T(8,128)(2,1)S(1)} %all-to-all-done.1.recv_ref, ...), custom_call_target="tpu_custom_call" | custom-call | flops 5000000000 | bytes 1024 | tf_op jit(solution)/shard_map/decoder/pallas_call | solution.py:343
  74.4 9.8 %all-to-all-start.2 = ((bf16[16,64,128]{2,1,0:T(8,128)(2,1)}), bf16[16,64,128]{2,1,0:T(8,128)(2,1)S(1)}, u32[]{:S(2)}, u32[]{:S(2)}) async-start(bf16[16,64,128]{2,1,0:T(8,128)(2,1)} %get-tuple-element.28), calls=%async_computation.2 | async-start | bytes 524288 | tf_op jit(solution)/shard_map/all_to_all | solution.py:503
  84.4 1.8 %prepare.1.normed_hbm = bf16[1024,256]{1,0:T(8,128)(2,1)} custom-call(bf16[256,1664]{1,0:T(8,128)(2,1)S(1)} %bitcast.17, f32[1,1024]{1,0:T(1,128)} %bitcast.28), custom_call_target="tpu_custom_call" | custom-call | flops 2000000000 | bytes 1024 | tf_op jit(solution)/shard_map/prepare/pallas_call | solution.py:237
  86.2 1.5 %out_grad.1 = (bf16[2,16,32,128]{3,2,1,0:T(8,128)(2,1)S(1)}, bf16[2,16,32,128]{3,2,1,0:T(8,128)(2,1)S(1)}, bf16[2,16,32,128]{3,2,1,0:T(8,128)(2,1)S(1)}, bf16[2,16,32,128]{3,2,1,0:T(8,128)(2,1)S(1)}) custom-call(s32[4]{0:T(128)S(1)} %pad_add_fusion.place_ref, bf16[16,64,128]{2,1,0:T(8,128)(2,1)S(1)} %copy-done.2, bf16[128,1024]{1,0:T(8,128)(2,1)S(1)} %copy-done.3, ...), custom_call_target="tpu_custom_call" | custom-call | flops 1000000000 | bytes 1024 | tf_op jit(solution)/shard_map/out_grad/pallas_call | solution.py:391
  87.8 2.3 %collective-permute-start.10 = (bf16[2,16,32,128]{3,2,1,0:T(8,128)(2,1)S(1)}, bf16[2,16,32,128]{3,2,1,0:T(8,128)(2,1)S(1)}, u32[]{:S(2)}, u32[]{:S(2)}) collective-permute-start(bf16[2,16,32,128]{3,2,1,0:T(8,128)(2,1)S(1)} %get-tuple-element.38), channel_id=1, source_target_pairs={{0,192},{64,0},{128,64},{192,128},{1,193},{65,1},{129,65},{193,129... | collective-permute-start | bytes 786440 | tf_op jit(solution)/shard_map/ppermute | solution.py:553
  90.1 1.6 %collective-permute-start.9 = (bf16[2,16,32,128]{3,2,1,0:T(8,128)(2,1)S(1)}, bf16[2,16,32,128]{3,2,1,0:T(8,128)(2,1)S(1)}, u32[]{:S(2)}, u32[]{:S(2)}) collective-permute-start(bf16[2,16,32,128]{3,2,1,0:T(8,128)(2,1)S(1)} %get-tuple-element.37), channel_id=1, source_target_pairs={{0,128},{64,192},{128,0},{192,64},{1,129},{65,193},{129,1},{193,65... | collective-permute-start | bytes 786440 | tf_op jit(solution)/shard_map/ppermute | solution.py:553
  91.6 4.8 %all-to-all-done.2.dctx_ref = bf16[16,64,128]{2,1,0:T(8,128)(2,1)S(1)} async-done(((bf16[16,64,128]{2,1,0:T(8,128)(2,1)}), bf16[16,64,128]{2,1,0:T(8,128)(2,1)S(1)}, u32[]{:S(2)}, u32[]{:S(2)}) %all-to-all-start.2) | async-done | bytes 262176 | tf_op jit(solution)/shard_map/all_to_all | solution.py:503
  96.5 4.2 %backward.1 = bf16[16,96,128]{2,1,0:T(8,128)(2,1)} custom-call(bf16[16,64,128]{2,1,0:T(8,128)(2,1)S(1)} %all-to-all-done.2.dctx_ref, f32[16,128,128]{2,1,0:T(8,128)} %get-tuple-element.29.probs_hbm, bf16[256,2048]{1,0:T(8,128)(2,1)} %get-tuple-element.30.pick_hbm, bf16[16,192,128]{2,1,0:T(8,128)(2,1)} %get-tuple-element.31.qkv_hbm, ...), custom_call_target="tpu_custom_call" | custom-call | flops 5000000000 | bytes 1024 | tf_op jit(solution)/shard_map/backward/pallas_call | solution.py:440
  100.7 3.8 %all-to-all-start.3 = ((bf16[16,96,128]{2,1,0:T(8,128)(2,1)}), bf16[16,96,128]{2,1,0:T(8,128)(2,1)S(1)}, u32[]{:S(2)}, u32[]{:S(2)}) async-start(bf16[16,96,128]{2,1,0:T(8,128)(2,1)} %backward.1), calls=%async_computation.3 | async-start | bytes 786432 | tf_op jit(solution)/shard_map/all_to_all | solution.py:503
  105.5 1.2 collective-permute-start.11
  106.6 8.0 %collective-permute-done.11.other_ref = bf16[16,32,128]{2,1,0:T(8,128)(2,1)S(1)} collective-permute-done((bf16[16,32,128]{2,1,0:T(8,128)(2,1)S(1)}, bf16[16,32,128]{2,1,0:T(8,128)(2,1)S(1)}, u32[]{:S(2)}, u32[]{:S(2)}) %collective-permute-start.11) | collective-permute-done | bytes 131104 | tf_op jit(solution)/shard_map/ppermute | solution.py:556
  115.3 18.8 %all_to_all.25.last_ref = bf16[16,64,128]{2,1,0:T(8,128)(2,1)S(1)} all-to-all(bf16[16,64,128]{2,1,0:T(8,128)(2,1)S(1)} %collect.1), channel_id=1, replica_groups=mesh['x'=4,'y_lo'=2,'core'=2,'z'=8,'y_hi'=2] {'z','y_hi'}, dimensions={0} | all-to-all | bytes 524288 | tf_op jit(solution)/shard_map/all_to_all | solution.py:503
  134.1 1.3 finish.1
  (37 shorter events, 5.2 us)
Async XLA Ops:
  3.9 33.8 %all-to-all-start = ((bf16[16,16,1664]{2,1,0:T(8,128)(2,1)}), bf16[16,16,1664]{2,1,0:T(8,128)(2,1)S(1)}, u32[]{:S(2)}, u32[]{:S(2)}) async-start(bf16[16,16,1664]{2,1,0:T(8,128)(2,1)} %get-tuple-element.22), calls=%async_computation | async-start | bytes 1703936 | tf_op jit(solution)/shard_map/all_to_all | solution.py:503
  34.5 3.2 %copy-start = (bf16[1,16,1024]{2,1,0:T(8,128)(2,1)S(1)}, bf16[1,16,1024]{2,1,0:T(8,128)(2,1)}, u32[]{:S(2)}) copy-start(bf16[1,16,1024]{2,1,0:T(8,128)(2,1)} %targets_ref.1) | copy-start | bytes 98308
  42.4 25.7 %all-to-all-start.1 = ((bf16[16,128,128]{2,1,0:T(8,128)(2,1)}), bf16[16,128,128]{2,1,0:T(8,128)(2,1)S(1)}, u32[]{:S(2)}, u32[]{:S(2)}) async-start(bf16[16,128,128]{2,1,0:T(8,128)(2,1)} %get-tuple-element.24), calls=%async_computation.1 | async-start | bytes 1048576 | tf_op jit(solution)/shard_map/all_to_all | solution.py:503
  50.8 15.9 %copy-start.4 = (bf16[1024]{0:T(1024)(128)(2,1)S(1)}, bf16[1024]{0:T(1024)(128)(2,1)}, u32[]{:S(2)}) copy-start(bf16[1024]{0:T(1024)(128)(2,1)} %param.17) | copy-start | bytes 6148
  50.8 17.3 %copy-start.1 = (f32[7,1024]{1,0:T(8,128)S(1)}, f32[7,1024]{1,0:T(8,128)}, u32[]{:S(2)}) copy-start(f32[7,1024]{1,0:T(8,128)} %taps_ref.1) | copy-start | bytes 86020
  50.8 9.9 %collective-permute-start = (bf16[2,8,64,128]{3,2,1,0:T(8,128)(2,1)S(1)}, bf16[2,8,64,128]{3,2,1,0:T(8,128)(2,1)S(1)}, u32[]{:S(2)}, u32[]{:S(2)}) collective-permute-start(bf16[2,8,64,128]{3,2,1,0:T(8,128)(2,1)S(1)} %bitcast.19), channel_id=1, source_target_pairs={{0,64},{64,128},{128,192},{192,0},{1,65},{65,129},{129,193},{193,1... | collective-permute-start | bytes 786440 | tf_op jit(solution)/shard_map/ppermute | solution.py:543
  52.1 14.1 %collective-permute-start.1 = (bf16[2,8,64,128]{3,2,1,0:T(8,128)(2,1)S(1)}, bf16[2,8,64,128]{3,2,1,0:T(8,128)(2,1)S(1)}, u32[]{:S(2)}, u32[]{:S(2)}) collective-permute-start(bf16[2,8,64,128]{3,2,1,0:T(8,128)(2,1)S(1)} %bitcast.20), channel_id=1, source_target_pairs={{0,128},{64,192},{128,0},{192,64},{1,129},{65,193},{129,1},{193,65... | collective-permute-start | bytes 786440 | tf_op jit(solution)/shard_map/ppermute | solution.py:543
  54.8 11.4 %collective-permute-start.2 = (bf16[2,8,64,128]{3,2,1,0:T(8,128)(2,1)S(1)}, bf16[2,8,64,128]{3,2,1,0:T(8,128)(2,1)S(1)}, u32[]{:S(2)}, u32[]{:S(2)}) collective-permute-start(bf16[2,8,64,128]{3,2,1,0:T(8,128)(2,1)S(1)} %bitcast.21), channel_id=1, source_target_pairs={{0,192},{64,0},{128,64},{192,128},{1,193},{65,1},{129,65},{193,129... | collective-permute-start | bytes 786440 | tf_op jit(solution)/shard_map/ppermute | solution.py:543
  55.0 11.7 %collective-permute-start.3 = (bf16[2,8,64,128]{3,2,1,0:T(8,128)(2,1)S(1)}, bf16[2,8,64,128]{3,2,1,0:T(8,128)(2,1)S(1)}, u32[]{:S(2)}, u32[]{:S(2)}) collective-permute-start(bf16[2,8,64,128]{3,2,1,0:T(8,128)(2,1)S(1)} %bitcast.22), channel_id=1, source_target_pairs={{0,16},{16,0},{1,17},{17,1},{2,18},{18,2},{3,19},{19,3},{4,20},{20... | collective-permute-start | bytes 786440 | tf_op jit(solution)/shard_map/ppermute | solution.py:544
  60.7 6.0 %collective-permute-start.4 = (bf16[2,8,64,128]{3,2,1,0:T(8,128)(2,1)S(1)}, bf16[2,8,64,128]{3,2,1,0:T(8,128)(2,1)S(1)}, u32[]{:S(2)}, u32[]{:S(2)}) collective-permute-start(bf16[2,8,64,128]{3,2,1,0:T(8,128)(2,1)S(1)} %collective-permute-done.refs_1_), channel_id=1, source_target_pairs={{0,16},{16,0},{1,17},{17,1},{2,18},{18,2},{3,19},{19,3},{4,20},{20... | collective-permute-start | bytes 786440 | tf_op jit(solution)/shard_map/ppermute | solution.py:544
  66.2 1.5 %collective-permute-start.5 = (bf16[2,8,64,128]{3,2,1,0:T(8,128)(2,1)S(1)}, bf16[2,8,64,128]{3,2,1,0:T(8,128)(2,1)S(1)}, u32[]{:S(2)}, u32[]{:S(2)}) collective-permute-start(bf16[2,8,64,128]{3,2,1,0:T(8,128)(2,1)S(1)} %collective-permute-done.1.refs_2_), channel_id=1, source_target_pairs={{0,16},{16,0},{1,17},{17,1},{2,18},{18,2},{3,19},{19,3},{4,20},{20... | collective-permute-start | bytes 786440 | tf_op jit(solution)/shard_map/ppermute | solution.py:544
  66.2 1.9 %collective-permute-start.6 = (bf16[2,8,64,128]{3,2,1,0:T(8,128)(2,1)S(1)}, bf16[2,8,64,128]{3,2,1,0:T(8,128)(2,1)S(1)}, u32[]{:S(2)}, u32[]{:S(2)}) collective-permute-start(bf16[2,8,64,128]{3,2,1,0:T(8,128)(2,1)S(1)} %collective-permute-done.2.refs_3_), channel_id=1, source_target_pairs={{0,16},{16,0},{1,17},{17,1},{2,18},{18,2},{3,19},{19,3},{4,20},{20... | collective-permute-start | bytes 786440 | tf_op jit(solution)/shard_map/ppermute | solution.py:544
  74.3 9.8 %copy-start.5 = (bf16[8,192,128]{2,1,0:T(8,128)(2,1)S(1)}, bf16[8,192,128]{2,1,0:T(8,128)(2,1)}, u32[]{:S(2)}) copy-start(bf16[8,192,128]{2,1,0:T(8,128)(2,1)} %get-tuple-element.34) | copy-start | bytes 1179652
  74.4 22.1 %all-to-all-start.2 = ((bf16[16,64,128]{2,1,0:T(8,128)(2,1)}), bf16[16,64,128]{2,1,0:T(8,128)(2,1)S(1)}, u32[]{:S(2)}, u32[]{:S(2)}) async-start(bf16[16,64,128]{2,1,0:T(8,128)(2,1)} %get-tuple-element.28), calls=%async_computation.2 | async-start | bytes 524288 | tf_op jit(solution)/shard_map/all_to_all | solution.py:503
  84.1 2.1 %copy-start.2 = (bf16[16,64,128]{2,1,0:T(8,128)(2,1)S(1)}, bf16[16,64,128]{2,1,0:T(8,128)(2,1)}, u32[]{:S(2)}) copy-start(bf16[16,64,128]{2,1,0:T(8,128)(2,1)} %get-tuple-element.32.ctx_ref) | copy-start | bytes 786436
  84.1 2.1 %copy-start.3 = (bf16[128,1024]{1,0:T(8,128)(2,1)S(1)}, bf16[128,1024]{1,0:T(8,128)(2,1)}, u32[]{:S(2)}) copy-start(bf16[128,1024]{1,0:T(8,128)(2,1)} %get-tuple-element.33.denc_ref) | copy-start | bytes 786436
  84.2 2.1 %collective-permute-start.7 = (bf16[8,192,128]{2,1,0:T(8,128)(2,1)S(1)}, bf16[8,192,128]{2,1,0:T(8,128)(2,1)S(1)}, u32[]{:S(2)}, u32[]{:S(2)}) collective-permute-start(bf16[8,192,128]{2,1,0:T(8,128)(2,1)S(1)} %copy-done.5), channel_id=1, source_target_pairs={{0,16},{16,0},{1,17},{17,1},{2,18},{18,2},{3,19},{19,3},{4,20},{20... | collective-permute-start | bytes 1179656 | tf_op jit(solution)/shard_map/ppermute | solution.py:550
  87.8 16.7 %collective-permute-start.10 = (bf16[2,16,32,128]{3,2,1,0:T(8,128)(2,1)S(1)}, bf16[2,16,32,128]{3,2,1,0:T(8,128)(2,1)S(1)}, u32[]{:S(2)}, u32[]{:S(2)}) collective-permute-start(bf16[2,16,32,128]{3,2,1,0:T(8,128)(2,1)S(1)} %get-tuple-element.38), channel_id=1, source_target_pairs={{0,192},{64,0},{128,64},{192,128},{1,193},{65,1},{129,65},{193,129... | collective-permute-start | bytes 786440 | tf_op jit(solution)/shard_map/ppermute | solution.py:553
  90.1 15.3 %collective-permute-start.8 = (bf16[2,16,32,128]{3,2,1,0:T(8,128)(2,1)S(1)}, bf16[2,16,32,128]{3,2,1,0:T(8,128)(2,1)S(1)}, u32[]{:S(2)}, u32[]{:S(2)}) collective-permute-start(bf16[2,16,32,128]{3,2,1,0:T(8,128)(2,1)S(1)} %get-tuple-element.36), channel_id=1, source_target_pairs={{0,64},{64,128},{128,192},{192,0},{1,65},{65,129},{129,193},{193,1... | collective-permute-start | bytes 786440 | tf_op jit(solution)/shard_map/ppermute | solution.py:553
  90.1 15.3 %collective-permute-start.9 = (bf16[2,16,32,128]{3,2,1,0:T(8,128)(2,1)S(1)}, bf16[2,16,32,128]{3,2,1,0:T(8,128)(2,1)S(1)}, u32[]{:S(2)}, u32[]{:S(2)}) collective-permute-start(bf16[2,16,32,128]{3,2,1,0:T(8,128)(2,1)S(1)} %get-tuple-element.37), channel_id=1, source_target_pairs={{0,128},{64,192},{128,0},{192,64},{1,129},{65,193},{129,1},{193,65... | collective-permute-start | bytes 786440 | tf_op jit(solution)/shard_map/ppermute | solution.py:553
  100.7 13.9 %all-to-all-start.3 = ((bf16[16,96,128]{2,1,0:T(8,128)(2,1)}), bf16[16,96,128]{2,1,0:T(8,128)(2,1)S(1)}, u32[]{:S(2)}, u32[]{:S(2)}) async-start(bf16[16,96,128]{2,1,0:T(8,128)(2,1)} %backward.1), calls=%async_computation.3 | async-start | bytes 786432 | tf_op jit(solution)/shard_map/all_to_all | solution.py:503
  105.5 9.1 %collective-permute-start.11 = (bf16[16,32,128]{2,1,0:T(8,128)(2,1)S(1)}, bf16[16,32,128]{2,1,0:T(8,128)(2,1)S(1)}, u32[]{:S(2)}, u32[]{:S(2)}) collective-permute-start(bf16[16,32,128]{2,1,0:T(8,128)(2,1)S(1)} %get-tuple-element.41), channel_id=1, source_target_pairs={{0,32},{32,0},{1,33},{33,1},{2,34},{34,2},{3,35},{35,3},{4,36},{36... | collective-permute-start | bytes 393224 | tf_op jit(solution)/shard_map/ppermute | solution.py:556

commit v4 on v3

--- a/solution.py
+++ b/solution.py
@@ -25,7 +25,7 @@
 PAD = 8
 LANES = 256
 BLOCK = 128
-EARLY = D // 2
+EARLY = D // 4
 LATE = (D - EARLY) // BLOCK * ROWS
 QKV = HS + HALF
 EXTRA = 16
@@ -35,12 +35,34 @@
 XS, YS = 4, 2
 CLIP = ("x", "y_lo", "core")
 COPY = ("z", "y_hi")
+RING = ("y_hi", "z")
+ZS, ZY = 8, 2
 F32 = jnp.float32
 BF16 = jnp.bfloat16
 
 VMEM = pl.BlockSpec(memory_space=pltpu.VMEM)
-SMEM = pl.BlockSpec(memory_space=pltpu.SMEM)
 HBM = pl.BlockSpec(memory_space=pltpu.HBM)
+
+
+def slot(copy):
+    return copy % ZY * ZS + copy // ZY
+
+
+def copy_of(place):
+    return place % ZS * ZY + place // ZS
+
+
+def in_order(blocks):
+    return jnp.concatenate([blocks(slot(copy)) for copy in range(COPIES)], axis=0)
+
+
+def frame_ids(width):
+    row = lax.broadcasted_iota(jnp.int32, (L, width), 0)
+    return (copy_of(row // ROWS) * ROWS + row % ROWS).astype(F32)
+
+
+def head_here():
+    return lax.axis_index("z") * ZY + lax.axis_index("y_hi")
 
 
 def mm(left, right):
@@ -74,13 +96,15 @@
 
 
 def pack_kernel(
-    place_ref, count_ref, frames_hbm, targets_hbm, index_hbm, w_ref, wo_hbm,
-    sent_ref, index_out, weights_ref, w_buf, wo_buf, frames_ref, targets_ref, index_ref, sems,
+    slots_hbm, frames_hbm, targets_hbm, index_hbm, w_ref, wo_hbm,
+    sent_ref, index_out, weights_ref, w_buf, wo_buf, frames_ref, targets_ref, index_ref, slots_ref, sems,
 ):
-    head = place_ref[0]
+    head = head_here()
     copies = []
     load_index = pltpu.make_async_copy(index_hbm.at[0], index_ref, sems.at[3])
     load_index.start()
+    load_slots = pltpu.make_async_copy(slots_hbm.at[0], slots_ref, sems.at[7])
+    load_slots.start()
     load_frames = pltpu.make_async_copy(frames_hbm.at[0], frames_ref, sems.at[4])
     load_frames.start()
     load_targets = pltpu.make_async_copy(targets_hbm.at[0, :, :EARLY], targets_ref, sems.at[6])
@@ -95,8 +119,11 @@
         copies[part].start()
     lanes = lax.broadcasted_iota(jnp.int32, (ROWS, KMAX), 1)
     load_index.wait()
+    load_slots.wait()
+    kept = jnp.where(slots_ref[...] < KMAX, 1.0, 0.0)
+    count = jnp.sum(kept, axis=1, keepdims=True)
     index = jnp.broadcast_to(index_ref[...], (ROWS, KMAX))
-    index = jnp.where(lanes < count_ref[0, 0], index, L).astype(F32).astype(BF16)
+    index = jnp.where(lanes.astype(F32) < count, index, L).astype(F32).astype(BF16)
     index_out[...] = index
     load_frames.wait()
     load_targets.wait()
@@ -117,13 +144,13 @@
         weights_ref[QKV + a * HS : QKV + (a + 1) * HS, :] = wo_buf[:, a * BLOCK : (a + 1) * BLOCK]
 
 
-def pack(place, count, frames, targets, index, w_qkv, w_out):
+def pack(slots, frames, targets, index, w_qkv, w_out):
     return call(
         pack_kernel,
         "pack",
         1,
         [((COPIES, ROWS, D + KMAX + EARLY), BF16), ((ROWS, KMAX), BF16), ((QKV + HS * D // BLOCK, BLOCK), BF16)],
-        [SMEM, SMEM] + [HBM] * 5,
+        [HBM] * 6,
         [VMEM, VMEM, VMEM],
         [
             pltpu.VMEM((3, HS, BLOCK), BF16),
@@ -131,9 +158,10 @@
             pltpu.VMEM((ROWS, D), BF16),
             pltpu.VMEM((ROWS, EARLY), BF16),
             pltpu.VMEM((1, KMAX), jnp.int32),
-            pltpu.SemaphoreType.DMA((7,)),
+            pltpu.VMEM((1, L), jnp.int32),
+            pltpu.SemaphoreType.DMA((8,)),
         ],
-    )(place, count, in_hbm(frames), in_hbm(targets), in_hbm(index), in_hbm(w_qkv), in_hbm(w_out))
+    )(in_hbm(slots), in_hbm(frames), in_hbm(targets), in_hbm(index), in_hbm(w_qkv), in_hbm(w_out))
 
 
 def normalize(got_ref, gain_hbm, gain_ref, sem):
@@ -155,8 +183,9 @@
             lanes = slice(EARLY + a * BLOCK, EARLY + (a + 1) * BLOCK)
             out_ref[m, HS + a * ROWS : HS + (a + 1) * ROWS, :] = targets_ref[0, :, lanes]
     normed = normalize(got_ref, gain_hbm, gain_ref, sems.at[3 * COPIES // GROUP])
+    x = lax.axis_index("x")
     for c in range(CLIPS):
-        block = w_ref[c % 2, c // (2 * YS), c // 2 % YS]
+        block = w_ref[c % 2, lax.rem(x + XS - c // (2 * YS), XS), c // 2 % YS]
         wqk_ref[c * HS : (c + 1) * HS, :] = block[:HS]
         wv_ref[c * HS : c * HS + HALF, :] = block[HS:, :HS]
         wv_ref[c * HS + HALF : (c + 1) * HS, :] = block[HS:, HS:]
@@ -164,7 +193,7 @@
     v = mm(normed, wv_ref[...]).astype(BF16).astype(F32)
     qk_t = qk.T
     qkv_t = jnp.concatenate([qk_t[:HS] * SCORE_SCALE, qk_t[HS:], v.T], axis=0).astype(BF16)
-    rows = lax.broadcasted_iota(jnp.int32, (L, KMAX), 0).astype(F32)
+    rows = frame_ids(KMAX)
     first = lax.broadcasted_iota(jnp.int32, (EXTRA, KMAX), 0) == 0
     one_row = jnp.where(first, 1.0, 0.0).astype(BF16)
     saves = []
@@ -246,30 +275,32 @@
 
 
 def decoder_kernel(
-    place_ref, count_ref, recv_ref, got_ref, index_ref, embed_ref, taps_ref, *refs
+    recv_ref, got_ref, index_ref, embed_ref, taps_ref, *refs
 ):
     w_refs = refs[: 2 * XS]
     encoded_ref, dctx_ref, ctx_out, denc_out, share_out = refs[2 * XS : 2 * XS + 5]
     ctx_ref, denc_ref, share_ref, field_ref, error_ref, dfilled_ref, sems = refs[2 * XS + 5 :]
     chunks = D // LANES
-    core, x = place_ref[1], place_ref[2]
+    core, x = lax.axis_index("core"), lax.axis_index("x")
     parts = []
     for s in range(XS):
         chip = YS * lax.rem(x + XS - s, XS)
-        clips = [2 * (chip + t) + side for side in (core, 1 - core) for t in range(YS)]
+        slots = [side * ZS + chip + t for side in (core, 1 - core) for t in range(YS)]
         weights = [
             jnp.concatenate(
                 [w_refs[s][:, a].reshape(YS * HS, BLOCK), w_refs[XS + s][:, a].reshape(YS * HS, BLOCK)], axis=0
             )
             for a in range(D // BLOCK)
         ]
-        parts.append((clips, weights))
-    live = lax.broadcasted_iota(jnp.int32, (KMAX, 1), 0) < count_ref[0, 0]
+        parts.append((slots, weights))
     rows = lax.broadcasted_iota(jnp.int32, (L, KMAX), 0).astype(F32)
     hit = jnp.where(rows == index_ref[...].astype(F32)[:1], 1.0, 0.0)
     masked = 1.0 - jnp.sum(hit, axis=1, keepdims=True)
     place = hit.astype(BF16)
-    pick = hit.T.astype(BF16)
+    hit = hit.T
+    live = jnp.sum(hit, axis=1, keepdims=True) > 0.5
+    pick = hit.astype(BF16)
+    gather = jnp.where(frame_ids(KMAX) == index_ref[...].astype(F32)[:1], 1.0, 0.0).T.astype(BF16)
     ctx_ref[...] = recv_ref[:, :HS, :]
     saves = [
         pltpu.make_async_copy(here, there, sems.at[at])
@@ -279,10 +310,10 @@
     ]
     saves[0].start()
     ctx = [
-        jnp.concatenate([ctx_ref[clip] for clip in clips], axis=0).T for clips, weights in parts
+        jnp.concatenate([ctx_ref[at] for at in slots], axis=0).T for slots, weights in parts
     ]
     for i in range(CLIPS // 2):
-        share_ref[i, :HS, :] = ctx_ref[2 * i + 1 - core]
+        share_ref[i, :HS, :] = ctx_ref[(1 - core) * ZS + i]
     reach = KW // 2
     blocks = D // BLOCK
     for ref in (field_ref, error_ref):
@@ -290,10 +321,10 @@
         ref[PAD + L :] = jnp.zeros((PAD, D), F32)
     inside = slice(PAD, PAD + L)
     columns = [slice(c * LANES, (c + 1) * LANES) for c in range(chunks)]
-    inputs = [mm(pick, got_ref[:, lanes]) for lanes in columns]
+    inputs = [mm(gather, got_ref[:, lanes]) for lanes in columns]
     per = LANES // BLOCK
     mixed = inputs
-    for left, (clips, weights) in zip(ctx, parts):
+    for left, (slots, weights) in zip(ctx, parts):
         wide = [
             jnp.concatenate(weights[c * per : (c + 1) * per], axis=1) for c in range(chunks)
         ]
@@ -311,10 +342,10 @@
             predicted = predicted + taps_ref[t : t + 1, lanes] * field_ref[begin : begin + L, lanes]
         if (a + 1) * BLOCK <= EARLY:
             begin = D + KMAX + a * BLOCK
-            wanted = got_ref[:, begin : begin + BLOCK]
+            wanted = in_order(lambda p: got_ref[p * ROWS : (p + 1) * ROWS, begin : begin + BLOCK])
         else:
             begin = HS + (a * BLOCK - EARLY) // BLOCK * ROWS
-            wanted = recv_ref[:, begin : begin + ROWS, :].reshape(L, BLOCK)
+            wanted = in_order(lambda p: recv_ref[p, begin : begin + ROWS, :])
         error_ref[inside, lanes] = masked * (predicted - wanted.astype(F32)) * LOSS_SCALE
     for a in range(blocks):
         lanes = slice(a * BLOCK, (a + 1) * BLOCK)
@@ -331,15 +362,15 @@
     saves[1].start()
     saves[2].start()
     denc = denc_ref[...]
-    for clips, weights in parts:
+    for slots, weights in parts:
         dctx = mm_nt(jnp.concatenate(weights, axis=1), denc).astype(BF16)
-        for r, clip in enumerate(clips):
-            dctx_ref[clip] = dctx[r * HS : (r + 1) * HS]
+        for r, at in enumerate(slots):
+            dctx_ref[at] = dctx[r * HS : (r + 1) * HS]
     for save in saves:
         save.wait()
 
 
-def decoder(place, count, recv, got, w_out, index, embed, taps):
+def decoder(recv, got, w_out, index, embed, taps):
     return call(
         decoder_kernel,
         "decoder",
@@ -351,7 +382,7 @@
             ((KMAX, D), BF16),
             ((CLIPS // 2, HS + KMAX, KMAX), BF16),
         ],
-        [SMEM, SMEM] + [VMEM] * (5 + 2 * XS),
+        [VMEM] * (5 + 2 * XS),
         [VMEM] * 2 + [HBM] * 3,
         [
             pltpu.VMEM((H, HS, KMAX), BF16),
@@ -362,12 +393,12 @@
             pltpu.VMEM((L, D), BF16),
             pltpu.SemaphoreType.DMA((3,)),
         ],
-    )(place, count, recv, got, index, embed, taps, *w_out)
-
-
-def out_grad_kernel(place_ref, ctx_ref, denc_ref, share_ref, *refs):
+    )(recv, got, index, embed, taps, *w_out)
+
+
+def out_grad_kernel(ctx_ref, denc_ref, share_ref, *refs):
     outs, both_ref = refs[:XS], refs[XS]
-    core, x, y = place_ref[1], place_ref[2], place_ref[3]
+    core, x, y = lax.axis_index("core"), lax.axis_index("x"), lax.axis_index("y_lo")
     for a in range(D // BLOCK):
         lanes = slice(a * BLOCK, (a + 1) * BLOCK)
         both_ref[:KMAX, lanes] = denc_ref[:, lanes]
@@ -375,7 +406,7 @@
     for r in range(XS):
         for s in range(YS):
             chip = YS * lax.rem(x + r, XS) + lax.rem(y + s, YS)
-            left = jnp.concatenate([ctx_ref[2 * chip + core], share_ref[chip, :HS, :]], axis=1)
+            left = jnp.concatenate([ctx_ref[core * ZS + chip], share_ref[chip, :HS, :]], axis=1)
             block = mm(left, both_ref[...])
             upper, lower = block[:HALF], block[HALF:]
             for a in range(D // BLOCK):
@@ -383,20 +414,20 @@
                 first, second = upper[:, lanes], lower[:, lanes]
                 even = jnp.concatenate([first[:, :HS], second[:, :HS]], axis=1)
                 odd = jnp.concatenate([first[:, HS:], second[:, HS:]], axis=1)
-                outs[r][s, 2 * a] = even.astype(BF16)
-                outs[r][s, 2 * a + 1] = odd.astype(BF16)
-
-
-def out_grad(place, ctx, denc, share):
+                outs[r][s, slot(2 * a)] = even.astype(BF16)
+                outs[r][s, slot(2 * a + 1)] = odd.astype(BF16)
+
+
+def out_grad(ctx, denc, share):
     return call(
         out_grad_kernel,
         "out_grad",
         1,
         [((YS, COPIES, HALF, BLOCK), BF16)] * XS,
-        [SMEM] + [VMEM] * 3,
+        [VMEM] * 3,
         [VMEM] * XS,
         [pltpu.VMEM((2 * KMAX, D), BF16)],
-    )(place, ctx, denc, share)
+    )(ctx, denc, share)
 
 
 def backward_kernel(
@@ -455,8 +486,8 @@
     )(dctx, in_hbm(probs), in_hbm(pick), in_hbm(qkv), in_hbm(normed))[0]
 
 
-def collect_kernel(place_ref, terms_ref, mine_ref, other_ref, out_ref):
-    head = place_ref[0]
+def collect_kernel(terms_ref, mine_ref, other_ref, out_ref):
+    head = head_here()
     out_ref[:, :HALF, :] = (mine_ref[...].astype(F32) + other_ref[...].astype(F32)).astype(BF16)
     out_ref[:, HALF:, :] = jnp.zeros((COPIES, HALF, BLOCK), BF16)
     term = jnp.sum(terms_ref[...].astype(F32), axis=0)
@@ -464,39 +495,58 @@
     query = jnp.concatenate([upper[:, :HS], lower[:, :HS]], axis=1)
     key = jnp.concatenate([upper[:, HS:], lower[:, HS:]], axis=1)
     for part, piece in enumerate((query, key, term[HS:])):
-        out_ref[(part * H + head) // 3, HALF:, :] = piece.astype(BF16)
-
-
-def collect(place, terms, mine, other):
+        out_ref[slot((part * H + head) // 3), HALF:, :] = piece.astype(BF16)
+
+
+def collect(terms, mine, other):
     return call(
         collect_kernel,
         "collect",
         1,
         [((COPIES, HS, BLOCK), BF16)],
-        [SMEM] + [VMEM] * 3,
+        [VMEM] * 3,
         [VMEM],
-    )(place, terms, mine, other)[0]
-
-
-def finish_kernel(place_ref, last_ref, qkv_ref, out_ref):
+    )(terms, mine, other)[0]
+
+
+def emit_kernel(source_hbm, out_ref, buf, sem):
+    load = pltpu.make_async_copy(source_hbm, buf, sem)
+    load.start()
+    load.wait()
+    out_ref[...] = buf[...]
+
+
+def emit(encoded):
+    return call(
+        emit_kernel,
+        "emit",
+        5,
+        [((KMAX, D), BF16)],
+        [HBM],
+        [VMEM],
+        [pltpu.VMEM((KMAX, D), BF16), pltpu.SemaphoreType.DMA(())],
+    )(in_hbm(encoded))[0]
+
+
+def finish_kernel(last_ref, qkv_ref, out_ref):
     total = jnp.sum(last_ref[:, :HALF, :].astype(F32), axis=0)
     out_ref[:HALF, :] = total[:, :HS]
     out_ref[HALF:, :] = total[:, HS:]
     for i in range(3):
-        block = last_ref[lax.rem(3 * place_ref[0] + i, COPIES), HALF:, :].astype(F32)
+        block = last_ref[slot(lax.rem(3 * head_here() + i, COPIES)), HALF:, :].astype(F32)
         qkv_ref[:HALF, i * HS : (i + 1) * HS] = block[:, :HS]
         qkv_ref[HALF:, i * HS : (i + 1) * HS] = block[:, HS:]
 
 
-def finish(place, last):
+def finish(last):
     return call(
         finish_kernel,
         "finish",
         1,
         [((HS, 3 * HS), F32), ((HS, HS), F32)],
-        [SMEM, VMEM],
+        [VMEM],
         [VMEM] * 2,
-    )(place, last)
+    )(last)
 
 
 def swap(array, axes):
@@ -522,33 +572,32 @@
     mask_embed,
     dec_kernel,
 ):
-    place = jnp.stack(
-        [lax.axis_index(COPY), lax.axis_index("core"), lax.axis_index("x"), lax.axis_index("y_lo")]
-    )
     gain = norm_gain[None, :]
-    sent, index, weights = pack(place, kept_count, frames, targets, kept_index, w_qkv, w_out)
-    got = swap(sent, COPY).reshape(L, D + KMAX + EARLY)
+    sent, index, weights = pack(fill_slot, frames, targets, kept_index, w_qkv, w_out)
+    got = swap(sent, RING).reshape(L, D + KMAX + EARLY)
     weights = lax.all_gather(weights, "y_lo", axis=0)
     near = weights[:, QKV:].reshape(YS, D // BLOCK, HS, BLOCK)
     weights = weights[:, :QKV]
-    for axis in ("x", "core"):
-        weights = lax.all_gather(weights, axis, axis=0)
+    around = [weights] + [
+        lax.ppermute(weights, "x", [(i, (i + r) % XS) for i in range(XS)]) for r in range(1, XS)
+    ]
+    weights = lax.all_gather(jnp.stack(around), "core", axis=0)
 
     sent, probs, pick, qkv = forward(got, weights, gain, targets)
     normed = prepare(got, gain)
-    recv = swap(sent, COPY)
+    recv = swap(sent, RING)
     near, sent = lax.optimization_barrier((near, sent))
     w_out = [near]
     for r in range(1, XS):
         w_out.append(lax.ppermute(near, "x", [(i, (i + r) % XS) for i in range(XS)]))
     w_out += [lax.ppermute(part, "core", [(0, 1), (1, 0)]) for part in w_out]
     encoded, dctx, ctx, denc, share = decoder(
-        place, kept_count, recv, got, w_out, index, mask_embed[None, :], dec_kernel
+        recv, got, w_out, index, mask_embed[None, :], dec_kernel
     )
-    dctx = swap(dctx, COPY)
+    dctx = swap(dctx, RING)
 
     share = lax.ppermute(share, "core", [(0, 1), (1, 0)])
-    parts = list(out_grad(place, ctx, denc, share))
+    parts = list(out_grad(ctx, denc, share))
     for r in range(1, XS):
         parts[r] = lax.ppermute(parts[r], "x", [(i, (i + r) % XS) for i in range(XS)])
     mine = total(*[part[0] for part in parts])
@@ -556,8 +605,8 @@
     other = lax.ppermute(other, "y_lo", [(0, 1), (1, 0)])
 
     terms = swap(backward(dctx, probs, pick, qkv, normed), CLIP)
-    grad_qkv, grad_out = finish(place, swap(collect(place, terms, mine, other), COPY))
-    return (encoded[None, None], grad_qkv, grad_out)
+    grad_qkv, grad_out = finish(swap(collect(terms, mine, other), RING))
+    return (emit(encoded)[None, None], grad_qkv, grad_out)
 
 
 def solution(mesh):

time: 137 us -> 131 us (0.956)
  blocking collectives: 40.4 us -> 10.9 us
  waiting for transfers between devices: 27.2 us -> 42.1 us
  starting transfers between devices: 43.2 us -> 52.6 us
    all_to_all x1 -> x0, blocking collectives: 18.8 us -> none  [swap(): return lax.all_to_all(array, axes, 0, 0, tiled=True)]
    all_to_all x4 -> x5, waiting for transfers between devices: 5.83 us -> 18.8 us  [swap(): return lax.all_to_all(array, axes, 0, 0, tiled=True)]
    all_gather x2 -> x1, blocking collectives: 14.7 us -> 2.09 us  [per_device(): weights = lax.all_gather(jnp.stack(around), 'core', axis=0)]
    ppermute x0 -> x3, starting transfers between devices: none -> 5.73 us  [per_device(): lax.ppermute(weights, 'x', [(i, (i + r) % XS) for i in range(XS)])]
    all_to_all x4 -> x5, starting transfers between devices: 33.2 us -> 36.5 us  [swap(): return lax.all_to_all(array, axes, 0, 0, tiled=True)]
    ppermute x0 -> x3, waiting for transfers between devices: none -> 2.65 us  [per_device(): lax.ppermute(weights, 'x', [(i, (i + r) % XS) for i in range(XS)])]
    all_gather x1, blocking collectives: 6.9 us -> 8.82 us  [per_device(): weights = lax.all_gather(weights, 'y_lo', axis=0)]
    pallas_call x1 -> x2, Pallas kernels: 0.65 us -> 2.49 us  [the longest x1 1.68 us: emit(): call(emit_kernel, 'emit', 5, [((KMAX, D), BF16)], [HBM], [VMEM], [pltpu.V...]
  transfers between devices with their start and end apart: 16 -> 20, of which waited for: 8 -> 11; matrix products, arithmetic and copies ran while one was open for 0% -> 0% of each run, Pallas kernels for 6% -> 7%
where the time goes in v4:
time: 131 us; the launch traced here: 130 us
  starting transfers between devices  52.6 us (40%)
  waiting for transfers between devices  42.1 us (32%)
  Pallas kernels  22.7 us (17%)
  blocking collectives  10.9 us (8%)
    all_to_all x5, starting transfers between devices, swap(): return lax.all_to_all(array, axes, 0, 0, tiled=True)  36.5 us
    all_to_all x5, waiting for transfers between devices, swap(): return lax.all_to_all(array, axes, 0, 0, tiled=True)  18.8 us
    ppermute x3, waiting for transfers between devices, per_device(): lax.ppermute(near, 'x', [(i, (i + r) % XS) for i in range(XS)])  11.3 us
    all_gather x1, blocking collectives, per_device(): weights = lax.all_gather(weights, 'y_lo', axis=0)  8.82 us
    ppermute x1, waiting for transfers between devices, per_device(): other = lax.ppermute(other, 'y_lo', [(0, 1), (1, 0)])  7.96 us
    ppermute x3, starting transfers between devices, per_device(): lax.ppermute(weights, 'x', [(i, (i + r) % XS) for i in range(XS)])  5.73 us
    pallas_call x1, Pallas kernels, decoder(): call(decoder_kernel, 'decoder', 5, [((KMAX, D), BF16), ((H, HS, KMAX), BF...  5.73 us
    pallas_call x1, Pallas kernels, forward(): call(forward_kernel, 'forward', 0.1, [((COPIES, HS + LATE, KMAX), BF16),...  4.75 us
  transfers between devices with their start and end apart: 20, of which 11 were waited for; matrix products, arithmetic and copies ran while one was open for 0% of the time, Pallas kernels for 7%

profile of v4, /device:TPU:32, one launch (start us, length us, event | category | flops | bytes accessed | tf_op | source)
XLA Modules:
  0.0 130.0 jit_solution(4249331864870273741)
XLA Ops:
  0.6 2.0 %pack.1 = (bf16[16,16,1408]{2,1,0:T(8,128)(2,1)}, bf16[16,128]{1,0:T(8,128)(2,1)S(1)}, bf16[608,128]{1,0:T(8,128)(2,1)S(1)}) custom-call(s32[1,1,256]{2,1,0:T(1,128)} %slots_hbm.1, bf16[1,16,1024]{2,1,0:T(8,128)(2,1)} %frames_hbm.1, bf16[1,16,1024]{2,1,0:T(8,128)(2,1)} %targets_ref.1, s32[1,1,128]{2,1,0:T(1,128)} %index_hbm.1, bf16[64,3072]{1,0:T(8,128)(2,1)} %w_ref.1, ...), custom_call_target="tpu_custom_call" | custom-call | flops 1000000000 | bytes 1024 | tf_op jit(solution)/shard_map/pack/pallas_call | solution.py:148
  2.6 11.2 %all-to-all-start = ((bf16[16,16,1408]{2,1,0:T(8,128)(2,1)}), bf16[16,16,1408]{2,1,0:T(8,128)(2,1)S(1)}, u32[]{:S(2)}, u32[]{:S(2)}) async-start(bf16[16,16,1408]{2,1,0:T(8,128)(2,1)} %get-tuple-element.22), calls=%async_computation | async-start | bytes 1441792 | tf_op jit(solution)/shard_map/all_to_all | solution.py:553
  13.8 8.8 %all-gather = bf16[1216,128]{1,0:T(8,128)(2,1)S(1)} all-gather(bf16[608,128]{1,0:T(8,128)(2,1)S(1)} %get-tuple-element.23), channel_id=2, replica_groups=mesh['x'=4,'y_lo'=2,'core'=2,'z'=8,'y_hi'=2] {'y_lo'}, dimensions={0}, use_global_device_ids=true | all-gather | bytes 466944 | tf_op jit(solution)/shard_map/all_gather | solution.py:578
  22.7 1.6 %collective-permute-start = (bf16[2,96,128]{2,1,0:T(8,128)(2,1)S(1)}, bf16[2,96,128]{2,1,0:T(8,128)(2,1)S(1)}, u32[]{:S(2)}, u32[]{:S(2)}) collective-permute-start(bf16[2,96,128]{2,1,0:T(8,128)(2,1)S(1)} %get-tuple-element.44), channel_id=1, source_target_pairs={{0,64},{64,128},{128,192},{192,0},{1,65},{65,129},{129,193},{193,1... | collective-permute-start | bytes 147464 | tf_op jit(solution)/shard_map/ppermute | solution.py:582
  24.3 2.7 %collective-permute-start.1 = (bf16[2,96,128]{2,1,0:T(8,128)(2,1)S(1)}, bf16[2,96,128]{2,1,0:T(8,128)(2,1)S(1)}, u32[]{:S(2)}, u32[]{:S(2)}) collective-permute-start(bf16[2,96,128]{2,1,0:T(8,128)(2,1)S(1)} %get-tuple-element.44), channel_id=1, source_target_pairs={{0,128},{64,192},{128,0},{192,64},{1,129},{65,193},{129,1},{193,65... | collective-permute-start | bytes 147464 | tf_op jit(solution)/shard_map/ppermute | solution.py:582
  31.1 2.1 %all-gather.1 = bf16[8,2,96,128]{3,2,1,0:T(8,128)(2,1)S(1)} all-gather(bf16[4,2,96,128]{3,2,1,0:T(8,128)(2,1)S(1)} %pad_maximum_fusion), channel_id=3, replica_groups=mesh['x'=4,'y_lo'=2,'core'=2,'z'=8,'y_hi'=2] {'core'}, dimensions={0}, use_global_device_ids=true | all-gather | bytes 589824 | tf_op jit(solution)/shard_map/all_gather | solution.py:584
  34.7 4.8 %forward.1 = (bf16[16,160,128]{2,1,0:T(8,128)(2,1)}, f32[16,128,128]{2,1,0:T(8,128)}, bf16[256,2048]{1,0:T(8,128)(2,1)}, bf16[16,192,128]{2,1,0:T(8,128)(2,1)}) custom-call(bf16[256,1408]{1,0:T(8,128)(2,1)S(1)} %bitcast.15, bf16[2,4,2,96,128]{4,3,2,1,0:T(8,128)(2,1)S(1)} %bitcast.18, f32[1,1024]{1,0:T(1,128)} %bitcast.29, bf16[1,16,1024]{2,1,0:T(8,128)(2,1)S(1)} %copy-done), custom_call_target="tpu_custom_call" | custom-call | flops 100000000 | bytes 1024 | tf_op jit(solution)/shard_map/forward/pallas_call | solution.py:234
  39.5 7.8 %all-to-all-start.1 = ((bf16[16,160,128]{2,1,0:T(8,128)(2,1)}), bf16[16,160,128]{2,1,0:T(8,128)(2,1)S(1)}, u32[]{:S(2)}, u32[]{:S(2)}) async-start(bf16[16,160,128]{2,1,0:T(8,128)(2,1)} %get-tuple-element.24), calls=%async_computation.1 | async-start | bytes 1310720 | tf_op jit(solution)/shard_map/all_to_all | solution.py:553
  47.8 3.7 %collective-permute-start.4 = (bf16[2,8,64,128]{3,2,1,0:T(8,128)(2,1)S(1)}, bf16[2,8,64,128]{3,2,1,0:T(8,128)(2,1)S(1)}, u32[]{:S(2)}, u32[]{:S(2)}) collective-permute-start(bf16[2,8,64,128]{3,2,1,0:T(8,128)(2,1)S(1)} %bitcast.20), channel_id=1, source_target_pairs={{0,128},{64,192},{128,0},{192,64},{1,129},{65,193},{129,1},{193,65... | collective-permute-start | bytes 786440 | tf_op jit(solution)/shard_map/ppermute | solution.py:592
  51.5 5.4 %collective-permute-done.3.refs_1_ = bf16[2,8,64,128]{3,2,1,0:T(8,128)(2,1)S(1)} collective-permute-done((bf16[2,8,64,128]{3,2,1,0:T(8,128)(2,1)S(1)}, bf16[2,8,64,128]{3,2,1,0:T(8,128)(2,1)S(1)}, u32[]{:S(2)}, u32[]{:S(2)}) %collective-permute-start.3) | collective-permute-done | bytes 262176 | tf_op jit(solution)/shard_map/ppermute | solution.py:592
  57.0 5.9 %collective-permute-done.4.refs_2_ = bf16[2,8,64,128]{3,2,1,0:T(8,128)(2,1)S(1)} collective-permute-done((bf16[2,8,64,128]{3,2,1,0:T(8,128)(2,1)S(1)}, bf16[2,8,64,128]{3,2,1,0:T(8,128)(2,1)S(1)}, u32[]{:S(2)}, u32[]{:S(2)}) %collective-permute-start.4) | collective-permute-done | bytes 262176 | tf_op jit(solution)/shard_map/ppermute | solution.py:592
  64.8 2.2 %all-to-all-done.1.recv_ref = bf16[16,160,128]{2,1,0:T(8,128)(2,1)S(1)} async-done(((bf16[16,160,128]{2,1,0:T(8,128)(2,1)}), bf16[16,160,128]{2,1,0:T(8,128)(2,1)S(1)}, u32[]{:S(2)}, u32[]{:S(2)}) %all-to-all-start.1) | async-done | bytes 655392 | tf_op jit(solution)/shard_map/all_to_all | solution.py:553
  67.0 5.7 %decoder.1 = (bf16[128,1024]{1,0:T(8,128)(2,1)S(1)}, bf16[16,64,128]{2,1,0:T(8,128)(2,1)}, bf16[16,64,128]{2,1,0:T(8,128)(2,1)}, bf16[128,1024]{1,0:T(8,128)(2,1)}, bf16[8,192,128]{2,1,0:T(8,128)(2,1)}) custom-call(bf16[16,160,128]{2,1,0:T(8,128)(2,1)S(1)} %all-to-all-done.1.recv_ref, bf16[256,1408]{1,0:T(8,128)(2,1)S(1)} %bitcast.16, ...), custom_call_target="tpu_custom_call" | custom-call | flops 5000000000 | bytes 1024 | tf_op jit(solution)/shard_map/decoder/pallas_call | solution.py:374
  73.4 7.6 %all-to-all-start.2 = ((bf16[16,64,128]{2,1,0:T(8,128)(2,1)}), bf16[16,64,128]{2,1,0:T(8,128)(2,1)S(1)}, u32[]{:S(2)}, u32[]{:S(2)}) async-start(bf16[16,64,128]{2,1,0:T(8,128)(2,1)} %get-tuple-element.28), calls=%async_computation.2 | async-start | bytes 524288 | tf_op jit(solution)/shard_map/all_to_all | solution.py:553
  81.1 1.8 %prepare.1.normed_hbm = bf16[1024,256]{1,0:T(8,128)(2,1)} custom-call(bf16[256,1408]{1,0:T(8,128)(2,1)S(1)} %bitcast.17, f32[1,1024]{1,0:T(1,128)} %bitcast.30), custom_call_target="tpu_custom_call" | custom-call | flops 2000000000 | bytes 1024 | tf_op jit(solution)/shard_map/prepare/pallas_call | solution.py:266
  84.2 3.2 %collective-permute-start.12 = (bf16[2,16,32,128]{3,2,1,0:T(8,128)(2,1)S(1)}, bf16[2,16,32,128]{3,2,1,0:T(8,128)(2,1)S(1)}, u32[]{:S(2)}, u32[]{:S(2)}) collective-permute-start(bf16[2,16,32,128]{3,2,1,0:T(8,128)(2,1)S(1)} %get-tuple-element.37), channel_id=1, source_target_pairs={{0,128},{64,192},{128,0},{192,64},{1,129},{65,193},{129,1},{193,65... | collective-permute-start | bytes 786440 | tf_op jit(solution)/shard_map/ppermute | solution.py:602
  87.5 5.4 %all-to-all-done.2.dctx_ref = bf16[16,64,128]{2,1,0:T(8,128)(2,1)S(1)} async-done(((bf16[16,64,128]{2,1,0:T(8,128)(2,1)}), bf16[16,64,128]{2,1,0:T(8,128)(2,1)S(1)}, u32[]{:S(2)}, u32[]{:S(2)}) %all-to-all-start.2) | async-done | bytes 262176 | tf_op jit(solution)/shard_map/all_to_all | solution.py:553
  92.8 4.2 %backward.1 = bf16[16,96,128]{2,1,0:T(8,128)(2,1)} custom-call(bf16[16,64,128]{2,1,0:T(8,128)(2,1)S(1)} %all-to-all-done.2.dctx_ref, f32[16,128,128]{2,1,0:T(8,128)} %get-tuple-element.29.probs_hbm, bf16[256,2048]{1,0:T(8,128)(2,1)} %get-tuple-element.30.pick_hbm, bf16[16,192,128]{2,1,0:T(8,128)(2,1)} %get-tuple-element.31.qkv_hbm, ...), custom_call_target="tpu_custom_call" | custom-call | flops 5000000000 | bytes 1024 | tf_op jit(solution)/shard_map/backward/pallas_call | solution.py:471
  97.1 3.6 %all-to-all-start.3 = ((bf16[16,96,128]{2,1,0:T(8,128)(2,1)}), bf16[16,96,128]{2,1,0:T(8,128)(2,1)S(1)}, u32[]{:S(2)}, u32[]{:S(2)}) async-start(bf16[16,96,128]{2,1,0:T(8,128)(2,1)} %backward.1), calls=%async_computation.3 | async-start | bytes 786432 | tf_op jit(solution)/shard_map/all_to_all | solution.py:553
  100.9 1.9 %collective-permute-start.14 = (bf16[16,32,128]{2,1,0:T(8,128)(2,1)S(1)}, bf16[16,32,128]{2,1,0:T(8,128)(2,1)S(1)}, u32[]{:S(2)}, u32[]{:S(2)}) collective-permute-start(bf16[16,32,128]{2,1,0:T(8,128)(2,1)S(1)} %get-tuple-element.41), channel_id=1, source_target_pairs={{0,32},{32,0},{1,33},{33,1},{2,34},{34,2},{3,35},{35,3},{4,36},{36... | collective-permute-start | bytes 393224 | tf_op jit(solution)/shard_map/ppermute | solution.py:605
  102.7 8.0 %collective-permute-done.14.other_ref = bf16[16,32,128]{2,1,0:T(8,128)(2,1)S(1)} collective-permute-done((bf16[16,32,128]{2,1,0:T(8,128)(2,1)S(1)}, bf16[16,32,128]{2,1,0:T(8,128)(2,1)S(1)}, u32[]{:S(2)}, u32[]{:S(2)}) %collective-permute-start.14) | collective-permute-done | bytes 131104 | tf_op jit(solution)/shard_map/ppermute | solution.py:605
  111.5 6.3 %all-to-all-start.4 = ((bf16[16,64,128]{2,1,0:T(8,128)(2,1)}), bf16[16,64,128]{2,1,0:T(8,128)(2,1)S(1)}, u32[]{:S(2)}, u32[]{:S(2)}) async-start(bf16[16,64,128]{2,1,0:T(8,128)(2,1)} %collect.1), calls=%async_computation.4 | async-start | bytes 524288 | tf_op jit(solution)/shard_map/all_to_all | solution.py:553
  117.9 1.7 %emit.1 = bf16[128,1024]{1,0:T(8,128)(2,1)} custom-call(bf16[128,1024]{1,0:T(8,128)(2,1)} %copy-done.4), custom_call_target="tpu_custom_call" | custom-call | flops 5000000000 | bytes 1024 | tf_op jit(solution)/shard_map/emit/pallas_call | solution.py:520
  119.5 9.7 %all-to-all-done.4.last_ref = bf16[16,64,128]{2,1,0:T(8,128)(2,1)S(1)} async-done(((bf16[16,64,128]{2,1,0:T(8,128)(2,1)}), bf16[16,64,128]{2,1,0:T(8,128)(2,1)S(1)}, u32[]{:S(2)}, u32[]{:S(2)}) %all-to-all-start.4) | async-done | bytes 262176 | tf_op jit(solution)/shard_map/all_to_all | solution.py:553
  (46 shorter events, 11.9 us)
Async XLA Ops:
  2.6 32.1 %all-to-all-start = ((bf16[16,16,1408]{2,1,0:T(8,128)(2,1)}), bf16[16,16,1408]{2,1,0:T(8,128)(2,1)S(1)}, u32[]{:S(2)}, u32[]{:S(2)}) async-start(bf16[16,16,1408]{2,1,0:T(8,128)(2,1)} %get-tuple-element.22), calls=%async_computation | async-start | bytes 1441792 | tf_op jit(solution)/shard_map/all_to_all | solution.py:553
  22.7 5.7 %collective-permute-start = (bf16[2,96,128]{2,1,0:T(8,128)(2,1)S(1)}, bf16[2,96,128]{2,1,0:T(8,128)(2,1)S(1)}, u32[]{:S(2)}, u32[]{:S(2)}) collective-permute-start(bf16[2,96,128]{2,1,0:T(8,128)(2,1)S(1)} %get-tuple-element.44), channel_id=1, source_target_pairs={{0,64},{64,128},{128,192},{192,0},{1,65},{65,129},{129,193},{193,1... | collective-permute-start | bytes 147464 | tf_op jit(solution)/shard_map/ppermute | solution.py:582
  24.3 5.6 %collective-permute-start.1 = (bf16[2,96,128]{2,1,0:T(8,128)(2,1)S(1)}, bf16[2,96,128]{2,1,0:T(8,128)(2,1)S(1)}, u32[]{:S(2)}, u32[]{:S(2)}) collective-permute-start(bf16[2,96,128]{2,1,0:T(8,128)(2,1)S(1)} %get-tuple-element.44), channel_id=1, source_target_pairs={{0,128},{64,192},{128,0},{192,64},{1,129},{65,193},{129,1},{193,65... | collective-permute-start | bytes 147464 | tf_op jit(solution)/shard_map/ppermute | solution.py:582
  27.0 4.1 %collective-permute-start.2 = (bf16[2,96,128]{2,1,0:T(8,128)(2,1)S(1)}, bf16[2,96,128]{2,1,0:T(8,128)(2,1)S(1)}, u32[]{:S(2)}, u32[]{:S(2)}) collective-permute-start(bf16[2,96,128]{2,1,0:T(8,128)(2,1)S(1)} %get-tuple-element.44), channel_id=1, source_target_pairs={{0,192},{64,0},{128,64},{192,128},{1,193},{65,1},{129,65},{193,129... | collective-permute-start | bytes 147464 | tf_op jit(solution)/shard_map/ppermute | solution.py:582
  31.1 3.6 %copy-start = (bf16[1,16,1024]{2,1,0:T(8,128)(2,1)S(1)}, bf16[1,16,1024]{2,1,0:T(8,128)(2,1)}, u32[]{:S(2)}) copy-start(bf16[1,16,1024]{2,1,0:T(8,128)(2,1)} %targets_ref.1) | copy-start | bytes 98308
  39.5 27.5 %all-to-all-start.1 = ((bf16[16,160,128]{2,1,0:T(8,128)(2,1)}), bf16[16,160,128]{2,1,0:T(8,128)(2,1)S(1)}, u32[]{:S(2)}, u32[]{:S(2)}) async-start(bf16[16,160,128]{2,1,0:T(8,128)(2,1)} %get-tuple-element.24), calls=%async_computation.1 | async-start | bytes 1310720 | tf_op jit(solution)/shard_map/all_to_all | solution.py:553
  47.2 16.1 %copy-start.5 = (bf16[1024]{0:T(1024)(128)(2,1)S(1)}, bf16[1024]{0:T(1024)(128)(2,1)}, u32[]{:S(2)}) copy-start(bf16[1024]{0:T(1024)(128)(2,1)} %param.17) | copy-start | bytes 6148
  47.3 19.7 %copy-start.1 = (f32[7,1024]{1,0:T(8,128)S(1)}, f32[7,1024]{1,0:T(8,128)}, u32[]{:S(2)}) copy-start(f32[7,1024]{1,0:T(8,128)} %taps_ref.1) | copy-start | bytes 86020
  47.3 9.7 %collective-permute-start.3 = (bf16[2,8,64,128]{3,2,1,0:T(8,128)(2,1)S(1)}, bf16[2,8,64,128]{3,2,1,0:T(8,128)(2,1)S(1)}, u32[]{:S(2)}, u32[]{:S(2)}) collective-permute-start(bf16[2,8,64,128]{3,2,1,0:T(8,128)(2,1)S(1)} %bitcast.19), channel_id=1, source_target_pairs={{0,64},{64,128},{128,192},{192,0},{1,65},{65,129},{129,193},{193,1... | collective-permute-start | bytes 786440 | tf_op jit(solution)/shard_map/ppermute | solution.py:592
  47.8 15.1 %collective-permute-start.4 = (bf16[2,8,64,128]{3,2,1,0:T(8,128)(2,1)S(1)}, bf16[2,8,64,128]{3,2,1,0:T(8,128)(2,1)S(1)}, u32[]{:S(2)}, u32[]{:S(2)}) collective-permute-start(bf16[2,8,64,128]{3,2,1,0:T(8,128)(2,1)S(1)} %bitcast.20), channel_id=1, source_target_pairs={{0,128},{64,192},{128,0},{192,64},{1,129},{65,193},{129,1},{193,65... | collective-permute-start | bytes 786440 | tf_op jit(solution)/shard_map/ppermute | solution.py:592
  51.5 11.4 %collective-permute-start.5 = (bf16[2,8,64,128]{3,2,1,0:T(8,128)(2,1)S(1)}, bf16[2,8,64,128]{3,2,1,0:T(8,128)(2,1)S(1)}, u32[]{:S(2)}, u32[]{:S(2)}) collective-permute-start(bf16[2,8,64,128]{3,2,1,0:T(8,128)(2,1)S(1)} %bitcast.21), channel_id=1, source_target_pairs={{0,192},{64,0},{128,64},{192,128},{1,193},{65,1},{129,65},{193,129... | collective-permute-start | bytes 786440 | tf_op jit(solution)/shard_map/ppermute | solution.py:592
  51.5 11.9 %collective-permute-start.6 = (bf16[2,8,64,128]{3,2,1,0:T(8,128)(2,1)S(1)}, bf16[2,8,64,128]{3,2,1,0:T(8,128)(2,1)S(1)}, u32[]{:S(2)}, u32[]{:S(2)}) collective-permute-start(bf16[2,8,64,128]{3,2,1,0:T(8,128)(2,1)S(1)} %bitcast.22), channel_id=1, source_target_pairs={{0,16},{16,0},{1,17},{17,1},{2,18},{18,2},{3,19},{19,3},{4,20},{20... | collective-permute-start | bytes 786440 | tf_op jit(solution)/shard_map/ppermute | solution.py:593
  57.0 6.4 %collective-permute-start.7 = (bf16[2,8,64,128]{3,2,1,0:T(8,128)(2,1)S(1)}, bf16[2,8,64,128]{3,2,1,0:T(8,128)(2,1)S(1)}, u32[]{:S(2)}, u32[]{:S(2)}) collective-permute-start(bf16[2,8,64,128]{3,2,1,0:T(8,128)(2,1)S(1)} %collective-permute-done.3.refs_1_), channel_id=1, source_target_pairs={{0,16},{16,0},{1,17},{17,1},{2,18},{18,2},{3,19},{19,3},{4,20},{20... | collective-permute-start | bytes 786440 | tf_op jit(solution)/shard_map/ppermute | solution.py:593
  62.9 1.5 %collective-permute-start.8 = (bf16[2,8,64,128]{3,2,1,0:T(8,128)(2,1)S(1)}, bf16[2,8,64,128]{3,2,1,0:T(8,128)(2,1)S(1)}, u32[]{:S(2)}, u32[]{:S(2)}) collective-permute-start(bf16[2,8,64,128]{3,2,1,0:T(8,128)(2,1)S(1)} %collective-permute-done.4.refs_2_), channel_id=1, source_target_pairs={{0,16},{16,0},{1,17},{17,1},{2,18},{18,2},{3,19},{19,3},{4,20},{20... | collective-permute-start | bytes 786440 | tf_op jit(solution)/shard_map/ppermute | solution.py:593
  62.9 1.9 %collective-permute-start.9 = (bf16[2,8,64,128]{3,2,1,0:T(8,128)(2,1)S(1)}, bf16[2,8,64,128]{3,2,1,0:T(8,128)(2,1)S(1)}, u32[]{:S(2)}, u32[]{:S(2)}) collective-permute-start(bf16[2,8,64,128]{3,2,1,0:T(8,128)(2,1)S(1)} %collective-permute-done.5.refs_3_), channel_id=1, source_target_pairs={{0,16},{16,0},{1,17},{17,1},{2,18},{18,2},{3,19},{19,3},{4,20},{20... | collective-permute-start | bytes 786440 | tf_op jit(solution)/shard_map/ppermute | solution.py:593
  73.4 7.6 %copy-start.6 = (bf16[8,192,128]{2,1,0:T(8,128)(2,1)S(1)}, bf16[8,192,128]{2,1,0:T(8,128)(2,1)}, u32[]{:S(2)}) copy-start(bf16[8,192,128]{2,1,0:T(8,128)(2,1)} %get-tuple-element.34) | copy-start | bytes 1179652
  73.4 19.5 %all-to-all-start.2 = ((bf16[16,64,128]{2,1,0:T(8,128)(2,1)}), bf16[16,64,128]{2,1,0:T(8,128)(2,1)S(1)}, u32[]{:S(2)}, u32[]{:S(2)}) async-start(bf16[16,64,128]{2,1,0:T(8,128)(2,1)} %get-tuple-element.28), calls=%async_computation.2 | async-start | bytes 524288 | tf_op jit(solution)/shard_map/all_to_all | solution.py:553
  81.0 1.9 %collective-permute-start.10 = (bf16[8,192,128]{2,1,0:T(8,128)(2,1)S(1)}, bf16[8,192,128]{2,1,0:T(8,128)(2,1)S(1)}, u32[]{:S(2)}, u32[]{:S(2)}) collective-permute-start(bf16[8,192,128]{2,1,0:T(8,128)(2,1)S(1)} %copy-done.6), channel_id=1, source_target_pairs={{0,16},{16,0},{1,17},{17,1},{2,18},{18,2},{3,19},{19,3},{4,20},{20... | collective-permute-start | bytes 1179656 | tf_op jit(solution)/shard_map/ppermute | solution.py:599
  83.9 16.8 %collective-permute-start.11 = (bf16[2,16,32,128]{3,2,1,0:T(8,128)(2,1)S(1)}, bf16[2,16,32,128]{3,2,1,0:T(8,128)(2,1)S(1)}, u32[]{:S(2)}, u32[]{:S(2)}) collective-permute-start(bf16[2,16,32,128]{3,2,1,0:T(8,128)(2,1)S(1)} %get-tuple-element.36), channel_id=1, source_target_pairs={{0,64},{64,128},{128,192},{192,0},{1,65},{65,129},{129,193},{193,1... | collective-permute-start | bytes 786440 | tf_op jit(solution)/shard_map/ppermute | solution.py:602
  84.2 16.5 %collective-permute-start.12 = (bf16[2,16,32,128]{3,2,1,0:T(8,128)(2,1)S(1)}, bf16[2,16,32,128]{3,2,1,0:T(8,128)(2,1)S(1)}, u32[]{:S(2)}, u32[]{:S(2)}) collective-permute-start(bf16[2,16,32,128]{3,2,1,0:T(8,128)(2,1)S(1)} %get-tuple-element.37), channel_id=1, source_target_pairs={{0,128},{64,192},{128,0},{192,64},{1,129},{65,193},{129,1},{193,65... | collective-permute-start | bytes 786440 | tf_op jit(solution)/shard_map/ppermute | solution.py:602
  87.4 13.3 %collective-permute-start.13 = (bf16[2,16,32,128]{3,2,1,0:T(8,128)(2,1)S(1)}, bf16[2,16,32,128]{3,2,1,0:T(8,128)(2,1)S(1)}, u32[]{:S(2)}, u32[]{:S(2)}) collective-permute-start(bf16[2,16,32,128]{3,2,1,0:T(8,128)(2,1)S(1)} %get-tuple-element.38), channel_id=1, source_target_pairs={{0,192},{64,0},{128,64},{192,128},{1,193},{65,1},{129,65},{193,129... | collective-permute-start | bytes 786440 | tf_op jit(solution)/shard_map/ppermute | solution.py:602
  97.1 13.6 %all-to-all-start.3 = ((bf16[16,96,128]{2,1,0:T(8,128)(2,1)}), bf16[16,96,128]{2,1,0:T(8,128)(2,1)S(1)}, u32[]{:S(2)}, u32[]{:S(2)}) async-start(bf16[16,96,128]{2,1,0:T(8,128)(2,1)} %backward.1), calls=%async_computation.3 | async-start | bytes 786432 | tf_op jit(solution)/shard_map/all_to_all | solution.py:553
  100.9 9.9 %collective-permute-start.14 = (bf16[16,32,128]{2,1,0:T(8,128)(2,1)S(1)}, bf16[16,32,128]{2,1,0:T(8,128)(2,1)S(1)}, u32[]{:S(2)}, u32[]{:S(2)}) collective-permute-start(bf16[16,32,128]{2,1,0:T(8,128)(2,1)S(1)} %get-tuple-element.41), channel_id=1, source_target_pairs={{0,32},{32,0},{1,33},{33,1},{2,34},{34,2},{3,35},{35,3},{4,36},{36... | collective-permute-start | bytes 393224 | tf_op jit(solution)/shard_map/ppermute | solution.py:605
  111.5 17.8 %all-to-all-start.4 = ((bf16[16,64,128]{2,1,0:T(8,128)(2,1)}), bf16[16,64,128]{2,1,0:T(8,128)(2,1)S(1)}, u32[]{:S(2)}, u32[]{:S(2)}) async-start(bf16[16,64,128]{2,1,0:T(8,128)(2,1)} %collect.1), calls=%async_computation.4 | async-start | bytes 524288 | tf_op jit(solution)/shard_map/all_to_all | solution.py:553
  (3 other events, 4.5 us)

commit v5 on v4

--- a/solution.py
+++ b/solution.py
@@ -197,6 +197,11 @@
     first = lax.broadcasted_iota(jnp.int32, (EXTRA, KMAX), 0) == 0
     one_row = jnp.where(first, 1.0, 0.0).astype(BF16)
     saves = []
+
+    def save(here, there):
+        saves.append(pltpu.make_async_copy(here, there, sems.at[len(saves)]))
+        saves[-1].start()
+
     for begin in range(0, COPIES, GROUP):
         group = range(begin, begin + GROUP)
         index = [got_ref[m * ROWS : (m + 1) * ROWS, D : D + KMAX].astype(F32)[:1] for m in group]
@@ -206,6 +211,10 @@
         qkv = [mm(qkv_t, p).astype(BF16) for p in pick]
         for m, a in zip(group, qkv):
             qkv_ref[m] = a
+        part = pl.ds(begin, GROUP)
+        lanes = pl.ds(begin * KMAX, GROUP * KMAX)
+        save(pick_ref.at[:, lanes], pick_out.at[:, lanes])
+        save(qkv_ref.at[part], qkv_out.at[part])
         bias = [jnp.where(first & (i > L - 0.5), MASKED_SCORE, 0.0).astype(BF16) for i in index]
         queries = [jnp.concatenate([a[:HS], one_row], axis=0) for a in qkv]
         keys = [jnp.concatenate([a[HS : 2 * HS], e], axis=0).T for a, e in zip(qkv, bias)]
@@ -217,17 +226,9 @@
         ctx = [mm(a[2 * HS :], p.astype(BF16)) for a, p in zip(qkv, probs)]
         for m, a in zip(group, ctx):
             out_ref[m, :HS, :] = a.astype(BF16)
-        part = pl.ds(begin, GROUP)
-        lanes = pl.ds(begin * KMAX, GROUP * KMAX)
-        for here, there in (
-            (probs_ref.at[part], probs_out.at[part]),
-            (qkv_ref.at[part], qkv_out.at[part]),
-            (pick_ref.at[:, lanes], pick_out.at[:, lanes]),
-        ):
-            saves.append(pltpu.make_async_copy(here, there, sems.at[len(saves)]))
-            saves[-1].start()
-    for save in saves:
-        save.wait()
+        save(probs_ref.at[part], probs_out.at[part])
+    for copy in saves:
+        copy.wait()
 
 
 def forward(got, weights, gain, targets):
@@ -278,8 +279,8 @@
     recv_ref, got_ref, index_ref, embed_ref, taps_ref, *refs
 ):
     w_refs = refs[: 2 * XS]
-    encoded_ref, dctx_ref, ctx_out, denc_out, share_out = refs[2 * XS : 2 * XS + 5]
-    ctx_ref, denc_ref, share_ref, field_ref, error_ref, dfilled_ref, sems = refs[2 * XS + 5 :]
+    encoded_out, dctx_out, ctx_out, denc_out, share_out = refs[2 * XS : 2 * XS + 5]
+    encoded_ref, dctx_ref, ctx_ref, denc_ref, share_ref, field_ref, error_ref, dfilled_ref, sems = refs[2 * XS + 5 :]
     chunks = D // LANES
     core, x = lax.axis_index("core"), lax.axis_index("x")
     parts = []
@@ -305,7 +306,7 @@
     saves = [
         pltpu.make_async_copy(here, there, sems.at[at])
         for at, (here, there) in enumerate(
-            ((ctx_ref, ctx_out), (denc_ref, denc_out), (share_ref, share_out))
+            ((ctx_ref, ctx_out), (denc_ref, denc_out), (share_ref, share_out), (encoded_ref, encoded_out))
         )
     ]
     saves[0].start()
@@ -332,6 +333,7 @@
     encoded = [jnp.where(live, m, 0.0).astype(BF16) for m in mixed]
     for lanes, e in zip(columns, encoded):
         encoded_ref[:, lanes] = e
+    saves[3].start()
     for lanes, e in zip(columns, encoded):
         field_ref[inside, lanes] = mm(place, e) + masked * embed_ref[:, lanes].astype(F32)
     for a in range(blocks):
@@ -366,6 +368,8 @@
         dctx = mm_nt(jnp.concatenate(weights, axis=1), denc).astype(BF16)
         for r, at in enumerate(slots):
             dctx_ref[at] = dctx[r * HS : (r + 1) * HS]
+            saves.append(pltpu.make_async_copy(dctx_ref.at[at], dctx_out.at[at], sems.at[len(saves)]))
+            saves[-1].start()
     for save in saves:
         save.wait()
 
@@ -383,15 +387,17 @@
             ((CLIPS // 2, HS + KMAX, KMAX), BF16),
         ],
         [VMEM] * (5 + 2 * XS),
-        [VMEM] * 2 + [HBM] * 3,
+        [HBM] * 5,
         [
+            pltpu.VMEM((KMAX, D), BF16),
+            pltpu.VMEM((H, HS, KMAX), BF16),
             pltpu.VMEM((H, HS, KMAX), BF16),
             pltpu.VMEM((KMAX, D), BF16),
             pltpu.VMEM((CLIPS // 2, HS + KMAX, KMAX), BF16),
             pltpu.VMEM((L + 2 * PAD, D), F32),
             pltpu.VMEM((L + 2 * PAD, D), F32),
             pltpu.VMEM((L, D), BF16),
-            pltpu.SemaphoreType.DMA((3,)),
+            pltpu.SemaphoreType.DMA((4 + H,)),
         ],
     )(recv, got, index, embed, taps, *w_out)
 
@@ -431,17 +437,12 @@
 
 
 def backward_kernel(
-    dctx_ref, probs_hbm, pick_hbm, qkv_hbm, normed_hbm, out_ref,
-    probs_ref, pick_ref, qkv_ref, normed_ref, dqkv_ref, sems,
+    dctx_ref, probs_ref, pick_hbm, qkv_ref, normed_hbm, out_ref, pick_ref, normed_ref, dqkv_ref, sems
 ):
     loads = []
-    for at, (there, here) in enumerate(
-        ((qkv_hbm, qkv_ref), (probs_hbm, probs_ref), (pick_hbm, pick_ref), (normed_hbm, normed_ref))
-    ):
+    for at, (there, here) in enumerate(((pick_hbm, pick_ref), (normed_hbm, normed_ref))):
         loads.append(pltpu.make_async_copy(there, here, sems.at[at]))
         loads[at].start()
-    loads[0].wait()
-    loads[1].wait()
     for begin in range(0, COPIES, GROUP):
         group = range(begin, begin + GROUP)
         dctx = [dctx_ref[m] for m in group]
@@ -456,8 +457,8 @@
         for m, q, k, v in zip(group, dquery, dkey, dvalue):
             dqkv = jnp.concatenate([q, k, v], axis=1)
             dqkv_ref[m * KMAX : (m + 1) * KMAX, :] = dqkv.astype(BF16)
-    loads[2].wait()
-    loads[3].wait()
+    loads[0].wait()
+    loads[1].wait()
     total = mm(pick_ref[...], dqkv_ref[...]).astype(BF16)
     grad = mm(normed_ref[...], total).astype(BF16)
     for c in range(CLIPS):
@@ -473,17 +474,15 @@
         "backward",
         5,
         [((CLIPS, HS + HALF, BLOCK), BF16)],
-        [VMEM] + [HBM] * 4,
+        [VMEM, VMEM, HBM, VMEM, HBM],
         [VMEM],
         [
-            pltpu.VMEM((COPIES, KMAX, KMAX), F32),
             pltpu.VMEM((L, QALL), BF16),
-            pltpu.VMEM((COPIES, 3 * HS, KMAX), BF16),
             pltpu.VMEM((D, L), BF16),
             pltpu.VMEM((QALL, 3 * HS), BF16),
-            pltpu.SemaphoreType.DMA((4,)),
+            pltpu.SemaphoreType.DMA((2,)),
         ],
-    )(dctx, in_hbm(probs), in_hbm(pick), in_hbm(qkv), in_hbm(normed))[0]
+    )(dctx, probs, in_hbm(pick), qkv, in_hbm(normed))[0]
 
 
 def collect_kernel(terms_ref, mine_ref, other_ref, out_ref):

time: 131 us -> 129 us (0.985)
  waiting for transfers between devices: 42.1 us -> 40.6 us
  transfers between devices with their start and end apart: 20 -> 20, of which waited for: 11 -> 12; matrix products, arithmetic and copies ran while one was open for 0% -> 1% of each run, Pallas kernels for 7% -> 7%
where the time goes in v5:
time: 129 us
  starting transfers between devices  52.9 us (41%)
  waiting for transfers between devices  40.6 us (31%)
  Pallas kernels  22 us (17%)
  blocking collectives  10.9 us (8%)
  other arithmetic  1.37 us (1%)
    all_to_all x5, starting transfers between devices, swap(): return lax.all_to_all(array, axes, 0, 0, tiled=True)  37.1 us
    all_to_all x5, waiting for transfers between devices, swap(): return lax.all_to_all(array, axes, 0, 0, tiled=True)  18 us
    ppermute x3, waiting for transfers between devices, per_device(): lax.ppermute(near, 'x', [(i, (i + r) % XS) for i in range(XS)])  11.3 us
    all_gather x1, blocking collectives, per_device(): weights = lax.all_gather(weights, 'y_lo', axis=0)  8.82 us
    ppermute x1, waiting for transfers between devices, per_device(): other = lax.ppermute(other, 'y_lo', [(0, 1), (1, 0)])  7.04 us
    ppermute x3, starting transfers between devices, per_device(): lax.ppermute(weights, 'x', [(i, (i + r) % XS) for i in range(XS)])  5.73 us
    pallas_call x1, Pallas kernels, decoder(): call(decoder_kernel, 'decoder', 5, [((KMAX, D), BF16), ((H, HS, KMAX), BF...  5.14 us
    pallas_call x1, Pallas kernels, forward(): call(forward_kernel, 'forward', 0.1, [((COPIES, HS + LATE, KMAX), BF16),...  4.66 us
  transfers between devices with their start and end apart: 20, of which 12 were waited for; matrix products, arithmetic and copies ran while one was open for 1% of the time, Pallas kernels for 7%

profile of v5, /device:TPU:32, one launch (start us, length us, event | category | flops | bytes accessed | tf_op | source)
XLA Modules:
  0.0 128.7 jit_solution(16536346846200233063)
XLA Ops:
  0.6 2.0 %pack.1 = (bf16[16,16,1408]{2,1,0:T(8,128)(2,1)}, bf16[16,128]{1,0:T(8,128)(2,1)S(1)}, bf16[608,128]{1,0:T(8,128)(2,1)S(1)}) custom-call(s32[1,1,256]{2,1,0:T(1,128)} %slots_hbm.1, bf16[1,16,1024]{2,1,0:T(8,128)(2,1)} %frames_hbm.1, bf16[1,16,1024]{2,1,0:T(8,128)(2,1)} %targets_ref.1, s32[1,1,128]{2,1,0:T(1,128)} %index_hbm.1, bf16[64,3072]{1,0:T(8,128)(2,1)} %w_ref.1, ...), custom_call_target="tpu_custom_call" | custom-call | flops 1000000000 | bytes 1024 | tf_op jit(solution)/shard_map/pack/pallas_call | solution.py:148
  2.6 11.2 %all-to-all-start = ((bf16[16,16,1408]{2,1,0:T(8,128)(2,1)}), bf16[16,16,1408]{2,1,0:T(8,128)(2,1)S(1)}, u32[]{:S(2)}, u32[]{:S(2)}) async-start(bf16[16,16,1408]{2,1,0:T(8,128)(2,1)} %get-tuple-element.22), calls=%async_computation | async-start | bytes 1441792 | tf_op jit(solution)/shard_map/all_to_all | solution.py:552
  13.8 8.8 %all-gather = bf16[1216,128]{1,0:T(8,128)(2,1)S(1)} all-gather(bf16[608,128]{1,0:T(8,128)(2,1)S(1)} %get-tuple-element.23), channel_id=2, replica_groups=mesh['x'=4,'y_lo'=2,'core'=2,'z'=8,'y_hi'=2] {'y_lo'}, dimensions={0}, use_global_device_ids=true | all-gather | bytes 466944 | tf_op jit(solution)/shard_map/all_gather | solution.py:577
  22.7 1.6 %collective-permute-start = (bf16[2,96,128]{2,1,0:T(8,128)(2,1)S(1)}, bf16[2,96,128]{2,1,0:T(8,128)(2,1)S(1)}, u32[]{:S(2)}, u32[]{:S(2)}) collective-permute-start(bf16[2,96,128]{2,1,0:T(8,128)(2,1)S(1)} %get-tuple-element.44), channel_id=1, source_target_pairs={{0,64},{64,128},{128,192},{192,0},{1,65},{65,129},{129,193},{193,1... | collective-permute-start | bytes 147464 | tf_op jit(solution)/shard_map/ppermute | solution.py:581
  24.2 2.7 %collective-permute-start.1 = (bf16[2,96,128]{2,1,0:T(8,128)(2,1)S(1)}, bf16[2,96,128]{2,1,0:T(8,128)(2,1)S(1)}, u32[]{:S(2)}, u32[]{:S(2)}) collective-permute-start(bf16[2,96,128]{2,1,0:T(8,128)(2,1)S(1)} %get-tuple-element.44), channel_id=1, source_target_pairs={{0,128},{64,192},{128,0},{192,64},{1,129},{65,193},{129,1},{193,65... | collective-permute-start | bytes 147464 | tf_op jit(solution)/shard_map/ppermute | solution.py:581
  31.1 2.1 %all-gather.1 = bf16[8,2,96,128]{3,2,1,0:T(8,128)(2,1)S(1)} all-gather(bf16[4,2,96,128]{3,2,1,0:T(8,128)(2,1)S(1)} %pad_maximum_fusion), channel_id=3, replica_groups=mesh['x'=4,'y_lo'=2,'core'=2,'z'=8,'y_hi'=2] {'core'}, dimensions={0}, use_global_device_ids=true | all-gather | bytes 589824 | tf_op jit(solution)/shard_map/all_gather | solution.py:583
  34.7 4.7 %forward.1 = (bf16[16,160,128]{2,1,0:T(8,128)(2,1)}, f32[16,128,128]{2,1,0:T(8,128)}, bf16[256,2048]{1,0:T(8,128)(2,1)}, bf16[16,192,128]{2,1,0:T(8,128)(2,1)}) custom-call(bf16[256,1408]{1,0:T(8,128)(2,1)S(1)} %bitcast.15, bf16[2,4,2,96,128]{4,3,2,1,0:T(8,128)(2,1)S(1)} %bitcast.18, f32[1,1024]{1,0:T(1,128)} %bitcast.29, bf16[1,16,1024]{2,1,0:T(8,128)(2,1)S(1)} %copy-done), custom_call_target="tpu_custom_call" | custom-call | flops 100000000 | bytes 1024 | tf_op jit(solution)/shard_map/forward/pallas_call | solution.py:235
  39.4 7.8 %all-to-all-start.1 = ((bf16[16,160,128]{2,1,0:T(8,128)(2,1)}), bf16[16,160,128]{2,1,0:T(8,128)(2,1)S(1)}, u32[]{:S(2)}, u32[]{:S(2)}) async-start(bf16[16,160,128]{2,1,0:T(8,128)(2,1)} %get-tuple-element.24), calls=%async_computation.1 | async-start | bytes 1310720 | tf_op jit(solution)/shard_map/all_to_all | solution.py:552
  47.7 3.7 %collective-permute-start.4 = (bf16[2,8,64,128]{3,2,1,0:T(8,128)(2,1)S(1)}, bf16[2,8,64,128]{3,2,1,0:T(8,128)(2,1)S(1)}, u32[]{:S(2)}, u32[]{:S(2)}) collective-permute-start(bf16[2,8,64,128]{3,2,1,0:T(8,128)(2,1)S(1)} %bitcast.20), channel_id=1, source_target_pairs={{0,128},{64,192},{128,0},{192,64},{1,129},{65,193},{129,1},{193,65... | collective-permute-start | bytes 786440 | tf_op jit(solution)/shard_map/ppermute | solution.py:591
  51.4 5.4 %collective-permute-done.3.refs_1_ = bf16[2,8,64,128]{3,2,1,0:T(8,128)(2,1)S(1)} collective-permute-done((bf16[2,8,64,128]{3,2,1,0:T(8,128)(2,1)S(1)}, bf16[2,8,64,128]{3,2,1,0:T(8,128)(2,1)S(1)}, u32[]{:S(2)}, u32[]{:S(2)}) %collective-permute-start.3) | collective-permute-done | bytes 262176 | tf_op jit(solution)/shard_map/ppermute | solution.py:591
  56.8 5.9 %collective-permute-done.4.refs_2_ = bf16[2,8,64,128]{3,2,1,0:T(8,128)(2,1)S(1)} collective-permute-done((bf16[2,8,64,128]{3,2,1,0:T(8,128)(2,1)S(1)}, bf16[2,8,64,128]{3,2,1,0:T(8,128)(2,1)S(1)}, u32[]{:S(2)}, u32[]{:S(2)}) %collective-permute-start.4) | collective-permute-done | bytes 262176 | tf_op jit(solution)/shard_map/ppermute | solution.py:591
  64.7 2.2 %all-to-all-done.1.recv_ref = bf16[16,160,128]{2,1,0:T(8,128)(2,1)S(1)} async-done(((bf16[16,160,128]{2,1,0:T(8,128)(2,1)}), bf16[16,160,128]{2,1,0:T(8,128)(2,1)S(1)}, u32[]{:S(2)}, u32[]{:S(2)}) %all-to-all-start.1) | async-done | bytes 655392 | tf_op jit(solution)/shard_map/all_to_all | solution.py:552
  66.9 5.1 %decoder.1 = (bf16[128,1024]{1,0:T(8,128)(2,1)}, bf16[16,64,128]{2,1,0:T(8,128)(2,1)}, bf16[16,64,128]{2,1,0:T(8,128)(2,1)}, bf16[128,1024]{1,0:T(8,128)(2,1)}, bf16[8,192,128]{2,1,0:T(8,128)(2,1)}) custom-call(bf16[16,160,128]{2,1,0:T(8,128)(2,1)S(1)} %all-to-all-done.1.recv_ref, bf16[256,1408]{1,0:T(8,128)(2,1)S(1)} %bitcast.16, ...), custom_call_target="tpu_custom_call" | custom-call | flops 5000000000 | bytes 1024 | tf_op jit(solution)/shard_map/decoder/pallas_call | solution.py:378
  72.0 7.6 %all-to-all-start.2 = ((bf16[16,64,128]{2,1,0:T(8,128)(2,1)}), bf16[16,64,128]{2,1,0:T(8,128)(2,1)S(1)}, u32[]{:S(2)}, u32[]{:S(2)}) async-start(bf16[16,64,128]{2,1,0:T(8,128)(2,1)} %get-tuple-element.28), calls=%async_computation.2 | async-start | bytes 524288 | tf_op jit(solution)/shard_map/all_to_all | solution.py:552
  79.7 1.8 %prepare.1.normed_hbm = bf16[1024,256]{1,0:T(8,128)(2,1)} custom-call(bf16[256,1408]{1,0:T(8,128)(2,1)S(1)} %bitcast.17, f32[1,1024]{1,0:T(1,128)} %bitcast.30), custom_call_target="tpu_custom_call" | custom-call | flops 2000000000 | bytes 1024 | tf_op jit(solution)/shard_map/prepare/pallas_call | solution.py:267
  83.2 3.2 %collective-permute-start.12 = (bf16[2,16,32,128]{3,2,1,0:T(8,128)(2,1)S(1)}, bf16[2,16,32,128]{3,2,1,0:T(8,128)(2,1)}, u32[]{:S(2)}, u32[]{:S(2)}) collective-permute-start(bf16[2,16,32,128]{3,2,1,0:T(8,128)(2,1)S(1)} %get-tuple-element.37), channel_id=1, source_target_pairs={{0,128},{64,192},{128,0},{192,64},{1,129},{65,193},{129,1},{193,65... | collective-permute-start | bytes 786440 | tf_op jit(solution)/shard_map/ppermute | solution.py:601
  86.4 5.1 %all-to-all-done.2.dctx_ref = bf16[16,64,128]{2,1,0:T(8,128)(2,1)S(1)} async-done(((bf16[16,64,128]{2,1,0:T(8,128)(2,1)}), bf16[16,64,128]{2,1,0:T(8,128)(2,1)S(1)}, u32[]{:S(2)}, u32[]{:S(2)}) %all-to-all-start.2) | async-done | bytes 262176 | tf_op jit(solution)/shard_map/all_to_all | solution.py:552
  91.5 3.9 %backward.1 = bf16[16,96,128]{2,1,0:T(8,128)(2,1)} custom-call(bf16[16,64,128]{2,1,0:T(8,128)(2,1)S(1)} %all-to-all-done.2.dctx_ref, f32[16,128,128]{2,1,0:T(8,128)S(1)} %copy-done.1, bf16[256,2048]{1,0:T(8,128)(2,1)} %get-tuple-element.30.pick_hbm, bf16[16,192,128]{2,1,0:T(8,128)(2,1)S(1)} %copy-done.2, bf16[1024,256]{1,0:T(8,128)(2,1)} %prepare.1.normed_hbm), custom_call_target="tpu_custom_call" | custom-call | flops 5000000000 | bytes 1024 | tf_op jit(solution)/shard_map/backward/pallas_call | solution.py:472
  95.4 3.6 %all-to-all-start.3 = ((bf16[16,96,128]{2,1,0:T(8,128)(2,1)}), bf16[16,96,128]{2,1,0:T(8,128)(2,1)S(1)}, u32[]{:S(2)}, u32[]{:S(2)}) async-start(bf16[16,96,128]{2,1,0:T(8,128)(2,1)} %backward.1), calls=%async_computation.3 | async-start | bytes 786432 | tf_op jit(solution)/shard_map/all_to_all | solution.py:552
  100.5 1.7 %collective-permute-start.14 = (bf16[16,32,128]{2,1,0:T(8,128)(2,1)S(1)}, bf16[16,32,128]{2,1,0:T(8,128)(2,1)S(1)}, u32[]{:S(2)}, u32[]{:S(2)}) collective-permute-start(bf16[16,32,128]{2,1,0:T(8,128)(2,1)S(1)} %get-tuple-element.41), channel_id=1, source_target_pairs={{0,32},{32,0},{1,33},{33,1},{2,34},{34,2},{3,35},{35,3},{4,36},{36... | collective-permute-start | bytes 393224 | tf_op jit(solution)/shard_map/ppermute | solution.py:604
  102.2 7.0 %collective-permute-done.14.other_ref = bf16[16,32,128]{2,1,0:T(8,128)(2,1)S(1)} collective-permute-done((bf16[16,32,128]{2,1,0:T(8,128)(2,1)S(1)}, bf16[16,32,128]{2,1,0:T(8,128)(2,1)S(1)}, u32[]{:S(2)}, u32[]{:S(2)}) %collective-permute-start.14) | collective-permute-done | bytes 131104 | tf_op jit(solution)/shard_map/ppermute | solution.py:604
  110.1 6.9 %all-to-all-start.4 = ((bf16[16,64,128]{2,1,0:T(8,128)(2,1)}), bf16[16,64,128]{2,1,0:T(8,128)(2,1)S(1)}, u32[]{:S(2)}, u32[]{:S(2)}) async-start(bf16[16,64,128]{2,1,0:T(8,128)(2,1)} %collect.1), calls=%async_computation.4 | async-start | bytes 524288 | tf_op jit(solution)/shard_map/all_to_all | solution.py:552
  117.0 1.7 %emit.1 = bf16[128,1024]{1,0:T(8,128)(2,1)} custom-call(bf16[128,1024]{1,0:T(8,128)(2,1)} %get-tuple-element.27.source_hbm), custom_call_target="tpu_custom_call" | custom-call | flops 5000000000 | bytes 1024 | tf_op jit(solution)/shard_map/emit/pallas_call | solution.py:519
  118.7 9.3 %all-to-all-done.4.last_ref = bf16[16,64,128]{2,1,0:T(8,128)(2,1)S(1)} async-done(((bf16[16,64,128]{2,1,0:T(8,128)(2,1)}), bf16[16,64,128]{2,1,0:T(8,128)(2,1)S(1)}, u32[]{:S(2)}, u32[]{:S(2)}) %all-to-all-start.4) | async-done | bytes 262176 | tf_op jit(solution)/shard_map/all_to_all | solution.py:552
  (48 shorter events, 12.9 us)
Async XLA Ops:
  2.6 32.1 %all-to-all-start = ((bf16[16,16,1408]{2,1,0:T(8,128)(2,1)}), bf16[16,16,1408]{2,1,0:T(8,128)(2,1)S(1)}, u32[]{:S(2)}, u32[]{:S(2)}) async-start(bf16[16,16,1408]{2,1,0:T(8,128)(2,1)} %get-tuple-element.22), calls=%async_computation | async-start | bytes 1441792 | tf_op jit(solution)/shard_map/all_to_all | solution.py:552
  22.7 5.7 %collective-permute-start = (bf16[2,96,128]{2,1,0:T(8,128)(2,1)S(1)}, bf16[2,96,128]{2,1,0:T(8,128)(2,1)S(1)}, u32[]{:S(2)}, u32[]{:S(2)}) collective-permute-start(bf16[2,96,128]{2,1,0:T(8,128)(2,1)S(1)} %get-tuple-element.44), channel_id=1, source_target_pairs={{0,64},{64,128},{128,192},{192,0},{1,65},{65,129},{129,193},{193,1... | collective-permute-start | bytes 147464 | tf_op jit(solution)/shard_map/ppermute | solution.py:581
  24.2 5.6 %collective-permute-start.1 = (bf16[2,96,128]{2,1,0:T(8,128)(2,1)S(1)}, bf16[2,96,128]{2,1,0:T(8,128)(2,1)S(1)}, u32[]{:S(2)}, u32[]{:S(2)}) collective-permute-start(bf16[2,96,128]{2,1,0:T(8,128)(2,1)S(1)} %get-tuple-element.44), channel_id=1, source_target_pairs={{0,128},{64,192},{128,0},{192,64},{1,129},{65,193},{129,1},{193,65... | collective-permute-start | bytes 147464 | tf_op jit(solution)/shard_map/ppermute | solution.py:581
  27.0 4.1 %collective-permute-start.2 = (bf16[2,96,128]{2,1,0:T(8,128)(2,1)S(1)}, bf16[2,96,128]{2,1,0:T(8,128)(2,1)S(1)}, u32[]{:S(2)}, u32[]{:S(2)}) collective-permute-start(bf16[2,96,128]{2,1,0:T(8,128)(2,1)S(1)} %get-tuple-element.44), channel_id=1, source_target_pairs={{0,192},{64,0},{128,64},{192,128},{1,193},{65,1},{129,65},{193,129... | collective-permute-start | bytes 147464 | tf_op jit(solution)/shard_map/ppermute | solution.py:581
  39.4 27.5 %all-to-all-start.1 = ((bf16[16,160,128]{2,1,0:T(8,128)(2,1)}), bf16[16,160,128]{2,1,0:T(8,128)(2,1)S(1)}, u32[]{:S(2)}, u32[]{:S(2)}) async-start(bf16[16,160,128]{2,1,0:T(8,128)(2,1)} %get-tuple-element.24), calls=%async_computation.1 | async-start | bytes 1310720 | tf_op jit(solution)/shard_map/all_to_all | solution.py:552
  47.2 16.1 %copy-start.6 = (bf16[1024]{0:T(1024)(128)(2,1)S(1)}, bf16[1024]{0:T(1024)(128)(2,1)}, u32[]{:S(2)}) copy-start(bf16[1024]{0:T(1024)(128)(2,1)} %param.17) | copy-start | bytes 6148
  47.2 19.7 %copy-start.3 = (f32[7,1024]{1,0:T(8,128)S(1)}, f32[7,1024]{1,0:T(8,128)}, u32[]{:S(2)}) copy-start(f32[7,1024]{1,0:T(8,128)} %taps_ref.1) | copy-start | bytes 86020
  47.2 9.6 %collective-permute-start.3 = (bf16[2,8,64,128]{3,2,1,0:T(8,128)(2,1)S(1)}, bf16[2,8,64,128]{3,2,1,0:T(8,128)(2,1)S(1)}, u32[]{:S(2)}, u32[]{:S(2)}) collective-permute-start(bf16[2,8,64,128]{3,2,1,0:T(8,128)(2,1)S(1)} %bitcast.19), channel_id=1, source_target_pairs={{0,64},{64,128},{128,192},{192,0},{1,65},{65,129},{129,193},{193,1... | collective-permute-start | bytes 786440 | tf_op jit(solution)/shard_map/ppermute | solution.py:591
  47.7 15.1 %collective-permute-start.4 = (bf16[2,8,64,128]{3,2,1,0:T(8,128)(2,1)S(1)}, bf16[2,8,64,128]{3,2,1,0:T(8,128)(2,1)S(1)}, u32[]{:S(2)}, u32[]{:S(2)}) collective-permute-start(bf16[2,8,64,128]{3,2,1,0:T(8,128)(2,1)S(1)} %bitcast.20), channel_id=1, source_target_pairs={{0,128},{64,192},{128,0},{192,64},{1,129},{65,193},{129,1},{193,65... | collective-permute-start | bytes 786440 | tf_op jit(solution)/shard_map/ppermute | solution.py:591
  51.4 11.4 %collective-permute-start.5 = (bf16[2,8,64,128]{3,2,1,0:T(8,128)(2,1)S(1)}, bf16[2,8,64,128]{3,2,1,0:T(8,128)(2,1)S(1)}, u32[]{:S(2)}, u32[]{:S(2)}) collective-permute-start(bf16[2,8,64,128]{3,2,1,0:T(8,128)(2,1)S(1)} %bitcast.21), channel_id=1, source_target_pairs={{0,192},{64,0},{128,64},{192,128},{1,193},{65,1},{129,65},{193,129... | collective-permute-start | bytes 786440 | tf_op jit(solution)/shard_map/ppermute | solution.py:591
  51.4 11.9 %collective-permute-start.6 = (bf16[2,8,64,128]{3,2,1,0:T(8,128)(2,1)S(1)}, bf16[2,8,64,128]{3,2,1,0:T(8,128)(2,1)S(1)}, u32[]{:S(2)}, u32[]{:S(2)}) collective-permute-start(bf16[2,8,64,128]{3,2,1,0:T(8,128)(2,1)S(1)} %bitcast.22), channel_id=1, source_target_pairs={{0,16},{16,0},{1,17},{17,1},{2,18},{18,2},{3,19},{19,3},{4,20},{20... | collective-permute-start | bytes 786440 | tf_op jit(solution)/shard_map/ppermute | solution.py:592
  56.8 6.5 %collective-permute-start.7 = (bf16[2,8,64,128]{3,2,1,0:T(8,128)(2,1)S(1)}, bf16[2,8,64,128]{3,2,1,0:T(8,128)(2,1)S(1)}, u32[]{:S(2)}, u32[]{:S(2)}) collective-permute-start(bf16[2,8,64,128]{3,2,1,0:T(8,128)(2,1)S(1)} %collective-permute-done.3.refs_1_), channel_id=1, source_target_pairs={{0,16},{16,0},{1,17},{17,1},{2,18},{18,2},{3,19},{19,3},{4,20},{20... | collective-permute-start | bytes 786440 | tf_op jit(solution)/shard_map/ppermute | solution.py:592
  62.8 1.5 %collective-permute-start.8 = (bf16[2,8,64,128]{3,2,1,0:T(8,128)(2,1)S(1)}, bf16[2,8,64,128]{3,2,1,0:T(8,128)(2,1)S(1)}, u32[]{:S(2)}, u32[]{:S(2)}) collective-permute-start(bf16[2,8,64,128]{3,2,1,0:T(8,128)(2,1)S(1)} %collective-permute-done.4.refs_2_), channel_id=1, source_target_pairs={{0,16},{16,0},{1,17},{17,1},{2,18},{18,2},{3,19},{19,3},{4,20},{20... | collective-permute-start | bytes 786440 | tf_op jit(solution)/shard_map/ppermute | solution.py:592
  62.8 1.9 %collective-permute-start.9 = (bf16[2,8,64,128]{3,2,1,0:T(8,128)(2,1)S(1)}, bf16[2,8,64,128]{3,2,1,0:T(8,128)(2,1)S(1)}, u32[]{:S(2)}, u32[]{:S(2)}) collective-permute-start(bf16[2,8,64,128]{3,2,1,0:T(8,128)(2,1)S(1)} %collective-permute-done.5.refs_3_), channel_id=1, source_target_pairs={{0,16},{16,0},{1,17},{17,1},{2,18},{18,2},{3,19},{19,3},{4,20},{20... | collective-permute-start | bytes 786440 | tf_op jit(solution)/shard_map/ppermute | solution.py:592
  72.0 19.5 %all-to-all-start.2 = ((bf16[16,64,128]{2,1,0:T(8,128)(2,1)}), bf16[16,64,128]{2,1,0:T(8,128)(2,1)S(1)}, u32[]{:S(2)}, u32[]{:S(2)}) async-start(bf16[16,64,128]{2,1,0:T(8,128)(2,1)} %get-tuple-element.28), calls=%async_computation.2 | async-start | bytes 524288 | tf_op jit(solution)/shard_map/all_to_all | solution.py:552
  79.6 1.9 %collective-permute-start.10 = (bf16[8,192,128]{2,1,0:T(8,128)(2,1)S(1)}, bf16[8,192,128]{2,1,0:T(8,128)(2,1)S(1)}, u32[]{:S(2)}, u32[]{:S(2)}) collective-permute-start(bf16[8,192,128]{2,1,0:T(8,128)(2,1)S(1)} %copy-done.7), channel_id=1, source_target_pairs={{0,16},{16,0},{1,17},{17,1},{2,18},{18,2},{3,19},{19,3},{4,20},{20... | collective-permute-start | bytes 1179656 | tf_op jit(solution)/shard_map/ppermute | solution.py:598
  81.5 10.0 %copy-start.1 = (f32[16,128,128]{2,1,0:T(8,128)S(1)}, f32[16,128,128]{2,1,0:T(8,128)}, u32[]{:S(2)}) copy-start(f32[16,128,128]{2,1,0:T(8,128)} %get-tuple-element.29.probs_ref) | copy-start | bytes 3145732
  81.5 10.0 %copy-start.2 = (bf16[16,192,128]{2,1,0:T(8,128)(2,1)S(1)}, bf16[16,192,128]{2,1,0:T(8,128)(2,1)}, u32[]{:S(2)}) copy-start(bf16[16,192,128]{2,1,0:T(8,128)(2,1)} %get-tuple-element.31.qkv_ref) | copy-start | bytes 2359300
  82.9 16.1 %collective-permute-start.11 = (bf16[2,16,32,128]{3,2,1,0:T(8,128)(2,1)}, bf16[2,16,32,128]{3,2,1,0:T(8,128)(2,1)}, u32[]{:S(2)}, u32[]{:S(2)}) collective-permute-start(bf16[2,16,32,128]{3,2,1,0:T(8,128)(2,1)} %get-tuple-element.36), channel_id=1, source_target_pairs={{0,64},{64,128},{128,192},{192,0},{1,65},{65,129},{129,193},{193,1... | collective-permute-start | bytes 786440 | tf_op jit(solution)/shard_map/ppermute | solution.py:601
  83.2 15.8 %collective-permute-start.12 = (bf16[2,16,32,128]{3,2,1,0:T(8,128)(2,1)S(1)}, bf16[2,16,32,128]{3,2,1,0:T(8,128)(2,1)}, u32[]{:S(2)}, u32[]{:S(2)}) collective-permute-start(bf16[2,16,32,128]{3,2,1,0:T(8,128)(2,1)S(1)} %get-tuple-element.37), channel_id=1, source_target_pairs={{0,128},{64,192},{128,0},{192,64},{1,129},{65,193},{129,1},{193,65... | collective-permute-start | bytes 786440 | tf_op jit(solution)/shard_map/ppermute | solution.py:601
  86.4 12.8 %collective-permute-start.13 = (bf16[2,16,32,128]{3,2,1,0:T(8,128)(2,1)S(1)}, bf16[2,16,32,128]{3,2,1,0:T(8,128)(2,1)}, u32[]{:S(2)}, u32[]{:S(2)}) collective-permute-start(bf16[2,16,32,128]{3,2,1,0:T(8,128)(2,1)S(1)} %get-tuple-element.38), channel_id=1, source_target_pairs={{0,192},{64,0},{128,64},{192,128},{1,193},{65,1},{129,65},{193,129... | collective-permute-start | bytes 786440 | tf_op jit(solution)/shard_map/ppermute | solution.py:601
  95.4 13.9 %all-to-all-start.3 = ((bf16[16,96,128]{2,1,0:T(8,128)(2,1)}), bf16[16,96,128]{2,1,0:T(8,128)(2,1)S(1)}, u32[]{:S(2)}, u32[]{:S(2)}) async-start(bf16[16,96,128]{2,1,0:T(8,128)(2,1)} %backward.1), calls=%async_computation.3 | async-start | bytes 786432 | tf_op jit(solution)/shard_map/all_to_all | solution.py:552
  100.5 8.8 %collective-permute-start.14 = (bf16[16,32,128]{2,1,0:T(8,128)(2,1)S(1)}, bf16[16,32,128]{2,1,0:T(8,128)(2,1)S(1)}, u32[]{:S(2)}, u32[]{:S(2)}) collective-permute-start(bf16[16,32,128]{2,1,0:T(8,128)(2,1)S(1)} %get-tuple-element.41), channel_id=1, source_target_pairs={{0,32},{32,0},{1,33},{33,1},{2,34},{34,2},{3,35},{35,3},{4,36},{36... | collective-permute-start | bytes 393224 | tf_op jit(solution)/shard_map/ppermute | solution.py:604
  110.1 17.8 %all-to-all-start.4 = ((bf16[16,64,128]{2,1,0:T(8,128)(2,1)}), bf16[16,64,128]{2,1,0:T(8,128)(2,1)S(1)}, u32[]{:S(2)}, u32[]{:S(2)}) async-start(bf16[16,64,128]{2,1,0:T(8,128)(2,1)} %collect.1), calls=%async_computation.4 | async-start | bytes 524288 | tf_op jit(solution)/shard_map/all_to_all | solution.py:552
  (4 other events, 15.0 us)

commit v6 on v5

--- a/solution.py
+++ b/solution.py
@@ -96,8 +96,8 @@
 
 
 def pack_kernel(
-    slots_hbm, frames_hbm, targets_hbm, index_hbm, w_ref, wo_hbm,
-    sent_ref, index_out, weights_ref, w_buf, wo_buf, frames_ref, targets_ref, index_ref, slots_ref, sems,
+    slots_hbm, frames_hbm, targets_hbm, index_hbm, w_ref,
+    sent_ref, index_out, weights_ref, w_buf, frames_ref, targets_ref, index_ref, slots_ref, sems,
 ):
     head = head_here()
     copies = []
@@ -109,8 +109,6 @@
     load_frames.start()
     load_targets = pltpu.make_async_copy(targets_hbm.at[0, :, :EARLY], targets_ref, sems.at[6])
     load_targets.start()
-    load_out = pltpu.make_async_copy(wo_hbm, wo_buf, sems.at[5])
-    load_out.start()
     for part in range(3):
         begin = pl.multiple_of(part * D + (head // 2) * BLOCK, BLOCK)
         copies.append(
@@ -139,29 +137,25 @@
     ]
     weights_ref[:HS, :] = jnp.concatenate([q, k], axis=1).astype(BF16)
     weights_ref[HS:QKV, :] = jnp.concatenate([v[:HALF], v[HALF:]], axis=1).astype(BF16)
-    load_out.wait()
-    for a in range(D // BLOCK):
-        weights_ref[QKV + a * HS : QKV + (a + 1) * HS, :] = wo_buf[:, a * BLOCK : (a + 1) * BLOCK]
-
-
-def pack(slots, frames, targets, index, w_qkv, w_out):
+
+
+def pack(slots, frames, targets, index, w_qkv):
     return call(
         pack_kernel,
         "pack",
         1,
-        [((COPIES, ROWS, D + KMAX + EARLY), BF16), ((ROWS, KMAX), BF16), ((QKV + HS * D // BLOCK, BLOCK), BF16)],
-        [HBM] * 6,
+        [((COPIES, ROWS, D + KMAX + EARLY), BF16), ((ROWS, KMAX), BF16), ((QKV, BLOCK), BF16)],
+        [HBM] * 5,
         [VMEM, VMEM, VMEM],
         [
             pltpu.VMEM((3, HS, BLOCK), BF16),
-            pltpu.VMEM((HS, D), BF16),
             pltpu.VMEM((ROWS, D), BF16),
             pltpu.VMEM((ROWS, EARLY), BF16),
             pltpu.VMEM((1, KMAX), jnp.int32),
             pltpu.VMEM((1, L), jnp.int32),
             pltpu.SemaphoreType.DMA((8,)),
         ],
-    )(in_hbm(slots), in_hbm(frames), in_hbm(targets), in_hbm(index), in_hbm(w_qkv), in_hbm(w_out))
+    )(in_hbm(slots), in_hbm(frames), in_hbm(targets), in_hbm(index), in_hbm(w_qkv))
 
 
 def normalize(got_ref, gain_hbm, gain_ref, sem):
@@ -282,17 +276,16 @@
     encoded_out, dctx_out, ctx_out, denc_out, share_out = refs[2 * XS : 2 * XS + 5]
     encoded_ref, dctx_ref, ctx_ref, denc_ref, share_ref, field_ref, error_ref, dfilled_ref, sems = refs[2 * XS + 5 :]
     chunks = D // LANES
-    core, x = lax.axis_index("core"), lax.axis_index("x")
+    core, x, y = lax.axis_index("core"), lax.axis_index("x"), lax.axis_index("y_lo")
     parts = []
     for s in range(XS):
         chip = YS * lax.rem(x + XS - s, XS)
-        slots = [side * ZS + chip + t for side in (core, 1 - core) for t in range(YS)]
-        weights = [
-            jnp.concatenate(
-                [w_refs[s][:, a].reshape(YS * HS, BLOCK), w_refs[XS + s][:, a].reshape(YS * HS, BLOCK)], axis=0
-            )
-            for a in range(D // BLOCK)
+        slots = [
+            side * ZS + chip + lax.rem(y + YS - t, YS) for side in (core, 1 - core) for t in range(YS)
         ]
+        weights = jnp.concatenate(
+            [w_refs[s][...].reshape(YS * HS, D), w_refs[XS + s][...].reshape(YS * HS, D)], axis=0
+        )
         parts.append((slots, weights))
     rows = lax.broadcasted_iota(jnp.int32, (L, KMAX), 0).astype(F32)
     hit = jnp.where(rows == index_ref[...].astype(F32)[:1], 1.0, 0.0)
@@ -326,10 +319,7 @@
     per = LANES // BLOCK
     mixed = inputs
     for left, (slots, weights) in zip(ctx, parts):
-        wide = [
-            jnp.concatenate(weights[c * per : (c + 1) * per], axis=1) for c in range(chunks)
-        ]
-        mixed = [m + mm(left, w) for m, w in zip(mixed, wide)]
+        mixed = [m + mm(left, weights[:, lanes]) for m, lanes in zip(mixed, columns)]
     encoded = [jnp.where(live, m, 0.0).astype(BF16) for m in mixed]
     for lanes, e in zip(columns, encoded):
         encoded_ref[:, lanes] = e
@@ -365,7 +355,7 @@
     saves[2].start()
     denc = denc_ref[...]
     for slots, weights in parts:
-        dctx = mm_nt(jnp.concatenate(weights, axis=1), denc).astype(BF16)
+        dctx = mm_nt(weights, denc).astype(BF16)
         for r, at in enumerate(slots):
             dctx_ref[at] = dctx[r * HS : (r + 1) * HS]
             saves.append(pltpu.make_async_copy(dctx_ref.at[at], dctx_out.at[at], sems.at[len(saves)]))
@@ -572,20 +562,21 @@
     dec_kernel,
 ):
     gain = norm_gain[None, :]
-    sent, index, weights = pack(fill_slot, frames, targets, kept_index, w_qkv, w_out)
+    sent, index, weights = pack(fill_slot, frames, targets, kept_index, w_qkv)
     got = swap(sent, RING).reshape(L, D + KMAX + EARLY)
-    weights = lax.all_gather(weights, "y_lo", axis=0)
-    near = weights[:, QKV:].reshape(YS, D // BLOCK, HS, BLOCK)
-    weights = weights[:, :QKV]
-    around = [weights] + [
-        lax.ppermute(weights, "x", [(i, (i + r) % XS) for i in range(XS)]) for r in range(1, XS)
+    pair = lax.all_gather(weights, "y_lo", axis=0)
+    around = [pair] + [
+        lax.ppermute(pair, "x", [(i, (i + r) % XS) for i in range(XS)]) for r in range(1, XS)
     ]
     weights = lax.all_gather(jnp.stack(around), "core", axis=0)
+    beyond, pair = lax.optimization_barrier((w_out, pair))
+    beyond = lax.ppermute(beyond, "y_lo", [(0, 1), (1, 0)])
+    weights, beyond = lax.optimization_barrier((weights, beyond))
 
     sent, probs, pick, qkv = forward(got, weights, gain, targets)
     normed = prepare(got, gain)
     recv = swap(sent, RING)
-    near, sent = lax.optimization_barrier((near, sent))
+    near, sent = lax.optimization_barrier((jnp.stack([w_out, beyond]), sent))
     w_out = [near]
     for r in range(1, XS):
         w_out.append(lax.ppermute(near, "x", [(i, (i + r) % XS) for i in range(XS)]))
@@ -599,8 +590,9 @@
     parts = list(out_grad(ctx, denc, share))
     for r in range(1, XS):
         parts[r] = lax.ppermute(parts[r], "x", [(i, (i + r) % XS) for i in range(XS)])
+    other = total(*[part[1] for part in parts])
+    other, parts = lax.optimization_barrier((other, parts))
     mine = total(*[part[0] for part in parts])
-    other = total(*[part[1] for part in parts])
     other = lax.ppermute(other, "y_lo", [(0, 1), (1, 0)])
 
     terms = swap(backward(dctx, probs, pick, qkv, normed), CLIP)

time: 129 us -> 129 us (level)
  blocking collectives: 10.9 us -> 6.58 us
  starting transfers between devices: 52.9 us -> 54.4 us
  waiting for transfers between devices: 40.6 us -> 42 us
    all_gather x1, blocking collectives: 8.82 us -> 4.49 us  [per_device(): pair = lax.all_gather(weights, 'y_lo', axis=0)]
    all_to_all x5, waiting for transfers between devices: 18 us -> 19.9 us  [swap(): return lax.all_to_all(array, axes, 0, 0, tiled=True)]
    ppermute x3 -> x4, starting transfers between devices: 5.73 us -> 6.69 us  [the longest x3 5.65 us: per_device(): lax.ppermute(pair, 'x', [(i, (i + r) % XS) for i in range(XS)])]
    ppermute x3 -> x4, waiting for transfers between devices: 2.65 us -> 3.21 us  [the longest x3 1.62 us: per_device(): lax.ppermute(pair, 'x', [(i, (i + r) % XS) for i in range(XS)])]
  transfers between devices with their start and end apart: 20 -> 21, of which waited for: 12 -> 13; matrix products, arithmetic and copies ran while one was open for 1% -> 2% of each run, Pallas kernels for 7% -> 7%
where the time goes in v6:
time: 129 us; the launch traced here: 128 us
  starting transfers between devices  54.4 us (42%)
  waiting for transfers between devices  42 us (33%)
  Pallas kernels  21.9 us (17%)
  blocking collectives  6.58 us (5%)
  other arithmetic  2.26 us (2%)
    all_to_all x5, starting transfers between devices, swap(): return lax.all_to_all(array, axes, 0, 0, tiled=True)  37.3 us
    all_to_all x5, waiting for transfers between devices, swap(): return lax.all_to_all(array, axes, 0, 0, tiled=True)  19.9 us
    ppermute x3, waiting for transfers between devices, per_device(): lax.ppermute(near, 'x', [(i, (i + r) % XS) for i in range(XS)])  11.4 us
    ppermute x1, waiting for transfers between devices, per_device(): other = lax.ppermute(other, 'y_lo', [(0, 1), (1, 0)])  5.94 us
    ppermute x3, starting transfers between devices, per_device(): lax.ppermute(pair, 'x', [(i, (i + r) % XS) for i in range(XS)])  5.65 us
    pallas_call x1, Pallas kernels, decoder(): call(decoder_kernel, 'decoder', 5, [((KMAX, D), BF16), ((H, HS, KMAX), BF...  5.16 us
    ppermute x3, starting transfers between devices, per_device(): lax.ppermute(near, 'x', [(i, (i + r) % XS) for i in range(XS)])  4.74 us
    pallas_call x1, Pallas kernels, forward(): call(forward_kernel, 'forward', 0.1, [((COPIES, HS + LATE, KMAX), BF16),...  4.67 us
  transfers between devices with their start and end apart: 21, of which 13 were waited for; matrix products, arithmetic and copies ran while one was open for 2% of the time, Pallas kernels for 7%

profile of v6, /device:TPU:32, one launch (start us, length us, event | category | flops | bytes accessed | tf_op | source)
XLA Modules:
  0.0 128.0 jit_solution(2065058160025660296)
XLA Ops:
  0.6 1.8 %pack.1 = (bf16[16,16,1408]{2,1,0:T(8,128)(2,1)}, bf16[16,128]{1,0:T(8,128)(2,1)S(1)}, bf16[96,128]{1,0:T(8,128)(2,1)S(1)}) custom-call(s32[1,1,256]{2,1,0:T(1,128)} %slots_hbm.1, bf16[1,16,1024]{2,1,0:T(8,128)(2,1)} %frames_hbm.1, bf16[1,16,1024]{2,1,0:T(8,128)(2,1)} %targets_ref.1, s32[1,1,128]{2,1,0:T(1,128)} %index_hbm.1, bf16[64,3072]{1,0:T(8,128)(2,1)} %w_ref.1), custom_call_target="tpu_custom_call" | custom-call | flops 1000000000 | bytes 1024 | tf_op jit(solution)/shard_map/pack/pallas_call | solution.py:143
  2.4 11.4 %all-to-all-start = ((bf16[16,16,1408]{2,1,0:T(8,128)(2,1)}), bf16[16,16,1408]{2,1,0:T(8,128)(2,1)S(1)}, u32[]{:S(2)}, u32[]{:S(2)}) async-start(bf16[16,16,1408]{2,1,0:T(8,128)(2,1)} %get-tuple-element.30), calls=%async_computation | async-start | bytes 1441792 | tf_op jit(solution)/shard_map/all_to_all | solution.py:542
  13.8 4.5 %all-gather = bf16[192,128]{1,0:T(8,128)(2,1)S(1)} all-gather(bf16[96,128]{1,0:T(8,128)(2,1)S(1)} %get-tuple-element.31), channel_id=2, replica_groups=mesh['x'=4,'y_lo'=2,'core'=2,'z'=8,'y_hi'=2] {'y_lo'}, dimensions={0}, use_global_device_ids=true | all-gather | bytes 73728 | tf_op jit(solution)/shard_map/all_gather | solution.py:567
  19.8 2.7 %collective-permute-start.1 = (bf16[2,96,128]{2,1,0:T(8,128)(2,1)S(1)}, bf16[2,96,128]{2,1,0:T(8,128)(2,1)S(1)}, u32[]{:S(2)}, u32[]{:S(2)}) collective-permute-start(bf16[2,96,128]{2,1,0:T(8,128)(2,1)S(1)} %bitcast.20), channel_id=1, source_target_pairs={{0,128},{64,192},{128,0},{192,64},{1,129},{65,193},{129,1},{193,65... | collective-permute-start | bytes 147464 | tf_op jit(solution)/shard_map/ppermute | solution.py:569
  26.6 2.1 %all-gather.1 = bf16[8,2,96,128]{3,2,1,0:T(8,128)(2,1)S(1)} all-gather(bf16[4,2,96,128]{3,2,1,0:T(8,128)(2,1)S(1)} %pad_maximum_fusion.1), channel_id=3, replica_groups=mesh['x'=4,'y_lo'=2,'core'=2,'z'=8,'y_hi'=2] {'core'}, dimensions={0}, use_global_device_ids=true | all-gather | bytes 589824 | tf_op jit(solution)/shard_map/all_gather | solution.py:571
  30.3 4.3 %all-to-all-done = bf16[16,16,1408]{2,1,0:T(8,128)(2,1)S(1)} async-done(((bf16[16,16,1408]{2,1,0:T(8,128)(2,1)}), bf16[16,16,1408]{2,1,0:T(8,128)(2,1)S(1)}, u32[]{:S(2)}, u32[]{:S(2)}) %all-to-all-start) | async-done | bytes 720928 | tf_op jit(solution)/shard_map/all_to_all | solution.py:542
  34.7 4.7 %forward.1 = (bf16[16,160,128]{2,1,0:T(8,128)(2,1)}, f32[16,128,128]{2,1,0:T(8,128)}, bf16[256,2048]{1,0:T(8,128)(2,1)}, bf16[16,192,128]{2,1,0:T(8,128)(2,1)}) custom-call(bf16[256,1408]{1,0:T(8,128)(2,1)S(1)} %bitcast.15, bf16[2,4,2,96,128]{4,3,2,1,0:T(8,128)(2,1)S(1)} %bitcast.18, f32[1,1024]{1,0:T(1,128)} %bitcast.28, bf16[1,16,1024]{2,1,0:T(8,128)(2,1)S(1)} %copy-done), custom_call_target="tpu_custom_call" | custom-call | flops 100000000 | bytes 1024 | tf_op jit(solution)/shard_map/forward/pallas_call | solution.py:229
  39.3 5.5 %all-to-all-start.1 = ((bf16[16,160,128]{2,1,0:T(8,128)(2,1)}), bf16[16,160,128]{2,1,0:T(8,128)(2,1)S(1)}, u32[]{:S(2)}, u32[]{:S(2)}) async-start(bf16[16,160,128]{2,1,0:T(8,128)(2,1)} %get-tuple-element.34), calls=%async_computation.1 | async-start | bytes 1310720 | tf_op jit(solution)/shard_map/all_to_all | solution.py:542
  44.9 2.4 %collective-permute-start.6 = (bf16[2,64,1024]{2,1,0:T(8,128)(2,1)S(1)}, bf16[2,64,1024]{2,1,0:T(8,128)(2,1)S(1)}, u32[]{:S(2)}, u32[]{:S(2)}) collective-permute-start(bf16[2,64,1024]{2,1,0:T(8,128)(2,1)S(1)} %pad_maximum_fusion.refs_0_), channel_id=1, source_target_pairs={{0,192},{64,0},{128,64},{192,128},{1,193},{65,1},{129,65},{193,129... | collective-permute-start | bytes 786440 | tf_op jit(solution)/shard_map/ppermute | solution.py:582
  47.4 2.3 %collective-permute-start.5 = (bf16[2,64,1024]{2,1,0:T(8,128)(2,1)S(1)}, bf16[2,64,1024]{2,1,0:T(8,128)(2,1)S(1)}, u32[]{:S(2)}, u32[]{:S(2)}) collective-permute-start(bf16[2,64,1024]{2,1,0:T(8,128)(2,1)S(1)} %pad_maximum_fusion.refs_0_), channel_id=1, source_target_pairs={{0,128},{64,192},{128,0},{192,64},{1,129},{65,193},{129,1},{193,65... | collective-permute-start | bytes 786440 | tf_op jit(solution)/shard_map/ppermute | solution.py:582
  49.7 8.1 %collective-permute-done.6.refs_3_ = bf16[2,64,1024]{2,1,0:T(8,128)(2,1)S(1)} collective-permute-done((bf16[2,64,1024]{2,1,0:T(8,128)(2,1)S(1)}, bf16[2,64,1024]{2,1,0:T(8,128)(2,1)S(1)}, u32[]{:S(2)}, u32[]{:S(2)}) %collective-permute-start.6) | collective-permute-done | bytes 262176 | tf_op jit(solution)/shard_map/ppermute | solution.py:582
  57.7 3.4 %collective-permute-done.4.refs_1_ = bf16[2,64,1024]{2,1,0:T(8,128)(2,1)S(1)} collective-permute-done((bf16[2,64,1024]{2,1,0:T(8,128)(2,1)S(1)}, bf16[2,64,1024]{2,1,0:T(8,128)(2,1)S(1)}, u32[]{:S(2)}, u32[]{:S(2)}) %collective-permute-start.4) | collective-permute-done | bytes 262176 | tf_op jit(solution)/shard_map/ppermute | solution.py:582
  63.5 5.2 %decoder.1 = (bf16[128,1024]{1,0:T(8,128)(2,1)}, bf16[16,64,128]{2,1,0:T(8,128)(2,1)}, bf16[16,64,128]{2,1,0:T(8,128)(2,1)}, bf16[128,1024]{1,0:T(8,128)(2,1)}, bf16[8,192,128]{2,1,0:T(8,128)(2,1)}) custom-call(bf16[16,160,128]{2,1,0:T(8,128)(2,1)S(1)} %all-to-all-done.1.recv_ref, bf16[256,1408]{1,0:T(8,128)(2,1)S(1)} %bitcast.16, ...), custom_call_target="tpu_custom_call" | custom-call | flops 5000000000 | bytes 1024 | tf_op jit(solution)/shard_map/decoder/pallas_call | solution.py:368
  68.7 9.3 %all-to-all-start.2 = ((bf16[16,64,128]{2,1,0:T(8,128)(2,1)}), bf16[16,64,128]{2,1,0:T(8,128)(2,1)S(1)}, u32[]{:S(2)}, u32[]{:S(2)}) async-start(bf16[16,64,128]{2,1,0:T(8,128)(2,1)} %get-tuple-element.39), calls=%async_computation.2 | async-start | bytes 524288 | tf_op jit(solution)/shard_map/all_to_all | solution.py:542
  78.1 1.8 %prepare.1.normed_hbm = bf16[1024,256]{1,0:T(8,128)(2,1)} custom-call(bf16[256,1408]{1,0:T(8,128)(2,1)S(1)} %bitcast.17, f32[1,1024]{1,0:T(1,128)} %bitcast.29), custom_call_target="tpu_custom_call" | custom-call | flops 2000000000 | bytes 1024 | tf_op jit(solution)/shard_map/prepare/pallas_call | solution.py:261
  81.3 2.1 %collective-permute-start.13 = (bf16[2,16,32,128]{3,2,1,0:T(8,128)(2,1)S(1)}, bf16[2,16,32,128]{3,2,1,0:T(8,128)(2,1)}, u32[]{:S(2)}, u32[]{:S(2)}) collective-permute-start(bf16[2,16,32,128]{3,2,1,0:T(8,128)(2,1)S(1)} %get-tuple-element.48), channel_id=1, source_target_pairs={{0,128},{64,192},{128,0},{192,64},{1,129},{65,193},{129,1},{193,65... | collective-permute-start | bytes 786440 | tf_op jit(solution)/shard_map/ppermute | solution.py:592
  84.5 5.3 %all-to-all-done.2.dctx_ref = bf16[16,64,128]{2,1,0:T(8,128)(2,1)S(1)} async-done(((bf16[16,64,128]{2,1,0:T(8,128)(2,1)}), bf16[16,64,128]{2,1,0:T(8,128)(2,1)S(1)}, u32[]{:S(2)}, u32[]{:S(2)}) %all-to-all-start.2) | async-done | bytes 262176 | tf_op jit(solution)/shard_map/all_to_all | solution.py:542
  89.8 3.9 %backward.1 = bf16[16,96,128]{2,1,0:T(8,128)(2,1)} custom-call(bf16[16,64,128]{2,1,0:T(8,128)(2,1)S(1)} %all-to-all-done.2.dctx_ref, f32[16,128,128]{2,1,0:T(8,128)S(1)} %copy-done.1, bf16[256,2048]{1,0:T(8,128)(2,1)} %get-tuple-element.41.pick_hbm, bf16[16,192,128]{2,1,0:T(8,128)(2,1)S(1)} %copy-done.2, bf16[1024,256]{1,0:T(8,128)(2,1)} %prepare.1.normed_hbm), custom_call_target="tpu_custom_call" | custom-call | flops 5000000000 | bytes 1024 | tf_op jit(solution)/shard_map/backward/pallas_call | solution.py:462
  93.8 3.6 %all-to-all-start.3 = ((bf16[16,96,128]{2,1,0:T(8,128)(2,1)}), bf16[16,96,128]{2,1,0:T(8,128)(2,1)S(1)}, u32[]{:S(2)}, u32[]{:S(2)}) async-start(bf16[16,96,128]{2,1,0:T(8,128)(2,1)} %backward.1), calls=%async_computation.3 | async-start | bytes 786432 | tf_op jit(solution)/shard_map/all_to_all | solution.py:542
  98.6 1.8 %collective-permute-start.15 = (bf16[16,32,128]{2,1,0:T(8,128)(2,1)S(1)}, bf16[16,32,128]{2,1,0:T(8,128)(2,1)S(1)}, u32[]{:S(2)}, u32[]{:S(2)}) collective-permute-start(bf16[16,32,128]{2,1,0:T(8,128)(2,1)S(1)} %fusion), channel_id=1, source_target_pairs={{0,32},{32,0},{1,33},{33,1},{2,34},{34,2},{3,35},{35,3},{4,36},{36... | collective-permute-start | bytes 393224 | tf_op jit(solution)/shard_map/ppermute | solution.py:596
  101.5 5.9 %collective-permute-done.15.other_ref = bf16[16,32,128]{2,1,0:T(8,128)(2,1)S(1)} collective-permute-done((bf16[16,32,128]{2,1,0:T(8,128)(2,1)S(1)}, bf16[16,32,128]{2,1,0:T(8,128)(2,1)S(1)}, u32[]{:S(2)}, u32[]{:S(2)}) %collective-permute-start.15) | collective-permute-done | bytes 131104 | tf_op jit(solution)/shard_map/ppermute | solution.py:596
  108.2 7.6 %all-to-all-start.4 = ((bf16[16,64,128]{2,1,0:T(8,128)(2,1)}), bf16[16,64,128]{2,1,0:T(8,128)(2,1)S(1)}, u32[]{:S(2)}, u32[]{:S(2)}) async-start(bf16[16,64,128]{2,1,0:T(8,128)(2,1)} %collect.1), calls=%async_computation.4 | async-start | bytes 524288 | tf_op jit(solution)/shard_map/all_to_all | solution.py:542
  115.8 1.7 %emit.1 = bf16[128,1024]{1,0:T(8,128)(2,1)} custom-call(bf16[128,1024]{1,0:T(8,128)(2,1)} %get-tuple-element.38.source_hbm), custom_call_target="tpu_custom_call" | custom-call | flops 5000000000 | bytes 1024 | tf_op jit(solution)/shard_map/emit/pallas_call | solution.py:509
  117.5 9.8 %all-to-all-done.4.last_ref = bf16[16,64,128]{2,1,0:T(8,128)(2,1)S(1)} async-done(((bf16[16,64,128]{2,1,0:T(8,128)(2,1)}), bf16[16,64,128]{2,1,0:T(8,128)(2,1)S(1)}, u32[]{:S(2)}, u32[]{:S(2)}) %all-to-all-start.4) | async-done | bytes 262176 | tf_op jit(solution)/shard_map/all_to_all | solution.py:542
  (52 shorter events, 16.2 us)
Async XLA Ops:
  2.4 21.5 %copy-start.6 = (bf16[64,1024]{1,0:T(8,128)(2,1)S(1)}, bf16[64,1024]{1,0:T(8,128)(2,1)}, u32[]{:S(2)}) copy-start(bf16[64,1024]{1,0:T(8,128)(2,1)} %param.16) | copy-start | bytes 393220
  2.4 32.2 %all-to-all-start = ((bf16[16,16,1408]{2,1,0:T(8,128)(2,1)}), bf16[16,16,1408]{2,1,0:T(8,128)(2,1)S(1)}, u32[]{:S(2)}, u32[]{:S(2)}) async-start(bf16[16,16,1408]{2,1,0:T(8,128)(2,1)} %get-tuple-element.30), calls=%async_computation | async-start | bytes 1441792 | tf_op jit(solution)/shard_map/all_to_all | solution.py:542
  18.3 6.7 %collective-permute-start = (bf16[2,96,128]{2,1,0:T(8,128)(2,1)S(1)}, bf16[2,96,128]{2,1,0:T(8,128)(2,1)S(1)}, u32[]{:S(2)}, u32[]{:S(2)}) collective-permute-start(bf16[2,96,128]{2,1,0:T(8,128)(2,1)S(1)} %bitcast.19), channel_id=1, source_target_pairs={{0,64},{64,128},{128,192},{192,0},{1,65},{65,129},{129,193},{193,1... | collective-permute-start | bytes 147464 | tf_op jit(solution)/shard_map/ppermute | solution.py:569
  19.8 5.6 %collective-permute-start.1 = (bf16[2,96,128]{2,1,0:T(8,128)(2,1)S(1)}, bf16[2,96,128]{2,1,0:T(8,128)(2,1)S(1)}, u32[]{:S(2)}, u32[]{:S(2)}) collective-permute-start(bf16[2,96,128]{2,1,0:T(8,128)(2,1)S(1)} %bitcast.20), channel_id=1, source_target_pairs={{0,128},{64,192},{128,0},{192,64},{1,129},{65,193},{129,1},{193,65... | collective-permute-start | bytes 147464 | tf_op jit(solution)/shard_map/ppermute | solution.py:569
  22.5 4.1 %collective-permute-start.2 = (bf16[2,96,128]{2,1,0:T(8,128)(2,1)S(1)}, bf16[2,96,128]{2,1,0:T(8,128)(2,1)S(1)}, u32[]{:S(2)}, u32[]{:S(2)}) collective-permute-start(bf16[2,96,128]{2,1,0:T(8,128)(2,1)S(1)} %bitcast.21), channel_id=1, source_target_pairs={{0,192},{64,0},{128,64},{192,128},{1,193},{65,1},{129,65},{193,129... | collective-permute-start | bytes 147464 | tf_op jit(solution)/shard_map/ppermute | solution.py:569
  24.0 6.4 %collective-permute-start.3 = (bf16[64,1024]{1,0:T(8,128)(2,1)S(1)}, bf16[64,1024]{1,0:T(8,128)(2,1)S(1)}, u32[]{:S(2)}, u32[]{:S(2)}) collective-permute-start(bf16[64,1024]{1,0:T(8,128)(2,1)S(1)} %copy-done.6), channel_id=1, source_target_pairs={{0,32},{32,0},{1,33},{33,1},{2,34},{34,2},{3,35},{35,3},{4,36},{36... | collective-permute-start | bytes 393224 | tf_op jit(solution)/shard_map/ppermute | solution.py:573
  39.3 24.1 %all-to-all-start.1 = ((bf16[16,160,128]{2,1,0:T(8,128)(2,1)}), bf16[16,160,128]{2,1,0:T(8,128)(2,1)S(1)}, u32[]{:S(2)}, u32[]{:S(2)}) async-start(bf16[16,160,128]{2,1,0:T(8,128)(2,1)} %get-tuple-element.34), calls=%async_computation.1 | async-start | bytes 1310720 | tf_op jit(solution)/shard_map/all_to_all | solution.py:542
  44.9 16.7 %copy-start.7 = (bf16[1024]{0:T(1024)(128)(2,1)S(1)}, bf16[1024]{0:T(1024)(128)(2,1)}, u32[]{:S(2)}) copy-start(bf16[1024]{0:T(1024)(128)(2,1)} %param.17) | copy-start | bytes 6148
  44.9 18.6 %copy-start.3 = (f32[7,1024]{1,0:T(8,128)S(1)}, f32[7,1024]{1,0:T(8,128)}, u32[]{:S(2)}) copy-start(f32[7,1024]{1,0:T(8,128)} %taps_ref.1) | copy-start | bytes 86020
  44.9 12.8 %collective-permute-start.6 = (bf16[2,64,1024]{2,1,0:T(8,128)(2,1)S(1)}, bf16[2,64,1024]{2,1,0:T(8,128)(2,1)S(1)}, u32[]{:S(2)}, u32[]{:S(2)}) collective-permute-start(bf16[2,64,1024]{2,1,0:T(8,128)(2,1)S(1)} %pad_maximum_fusion.refs_0_), channel_id=1, source_target_pairs={{0,192},{64,0},{128,64},{192,128},{1,193},{65,1},{129,65},{193,129... | collective-permute-start | bytes 786440 | tf_op jit(solution)/shard_map/ppermute | solution.py:582
  47.4 13.7 %collective-permute-start.4 = (bf16[2,64,1024]{2,1,0:T(8,128)(2,1)S(1)}, bf16[2,64,1024]{2,1,0:T(8,128)(2,1)S(1)}, u32[]{:S(2)}, u32[]{:S(2)}) collective-permute-start(bf16[2,64,1024]{2,1,0:T(8,128)(2,1)S(1)} %pad_maximum_fusion.refs_0_), channel_id=1, source_target_pairs={{0,64},{64,128},{128,192},{192,0},{1,65},{65,129},{129,193},{193,1... | collective-permute-start | bytes 786440 | tf_op jit(solution)/shard_map/ppermute | solution.py:582
  47.4 13.7 %collective-permute-start.5 = (bf16[2,64,1024]{2,1,0:T(8,128)(2,1)S(1)}, bf16[2,64,1024]{2,1,0:T(8,128)(2,1)S(1)}, u32[]{:S(2)}, u32[]{:S(2)}) collective-permute-start(bf16[2,64,1024]{2,1,0:T(8,128)(2,1)S(1)} %pad_maximum_fusion.refs_0_), channel_id=1, source_target_pairs={{0,128},{64,192},{128,0},{192,64},{1,129},{65,193},{129,1},{193,65... | collective-permute-start | bytes 786440 | tf_op jit(solution)/shard_map/ppermute | solution.py:582
  49.7 12.0 %collective-permute-start.7 = (bf16[2,64,1024]{2,1,0:T(8,128)(2,1)S(1)}, bf16[2,64,1024]{2,1,0:T(8,128)(2,1)S(1)}, u32[]{:S(2)}, u32[]{:S(2)}) collective-permute-start(bf16[2,64,1024]{2,1,0:T(8,128)(2,1)S(1)} %pad_maximum_fusion.refs_0_), channel_id=1, source_target_pairs={{0,16},{16,0},{1,17},{17,1},{2,18},{18,2},{3,19},{19,3},{4,20},{20... | collective-permute-start | bytes 786440 | tf_op jit(solution)/shard_map/ppermute | solution.py:583
  57.7 3.9 %collective-permute-start.10 = (bf16[2,64,1024]{2,1,0:T(8,128)(2,1)S(1)}, bf16[2,64,1024]{2,1,0:T(8,128)(2,1)S(1)}, u32[]{:S(2)}, u32[]{:S(2)}) collective-permute-start(bf16[2,64,1024]{2,1,0:T(8,128)(2,1)S(1)} %collective-permute-done.6.refs_3_), channel_id=1, source_target_pairs={{0,16},{16,0},{1,17},{17,1},{2,18},{18,2},{3,19},{19,3},{4,20},{20... | collective-permute-start | bytes 786440 | tf_op jit(solution)/shard_map/ppermute | solution.py:583
  61.1 1.5 %collective-permute-start.8 = (bf16[2,64,1024]{2,1,0:T(8,128)(2,1)S(1)}, bf16[2,64,1024]{2,1,0:T(8,128)(2,1)S(1)}, u32[]{:S(2)}, u32[]{:S(2)}) collective-permute-start(bf16[2,64,1024]{2,1,0:T(8,128)(2,1)S(1)} %collective-permute-done.4.refs_1_), channel_id=1, source_target_pairs={{0,16},{16,0},{1,17},{17,1},{2,18},{18,2},{3,19},{19,3},{4,20},{20... | collective-permute-start | bytes 786440 | tf_op jit(solution)/shard_map/ppermute | solution.py:583
  61.1 1.9 %collective-permute-start.9 = (bf16[2,64,1024]{2,1,0:T(8,128)(2,1)S(1)}, bf16[2,64,1024]{2,1,0:T(8,128)(2,1)S(1)}, u32[]{:S(2)}, u32[]{:S(2)}) collective-permute-start(bf16[2,64,1024]{2,1,0:T(8,128)(2,1)S(1)} %collective-permute-done.5.refs_2_), channel_id=1, source_target_pairs={{0,16},{16,0},{1,17},{17,1},{2,18},{18,2},{3,19},{19,3},{4,20},{20... | collective-permute-start | bytes 786440 | tf_op jit(solution)/shard_map/ppermute | solution.py:583
  68.7 21.2 %all-to-all-start.2 = ((bf16[16,64,128]{2,1,0:T(8,128)(2,1)}), bf16[16,64,128]{2,1,0:T(8,128)(2,1)S(1)}, u32[]{:S(2)}, u32[]{:S(2)}) async-start(bf16[16,64,128]{2,1,0:T(8,128)(2,1)} %get-tuple-element.39), calls=%async_computation.2 | async-start | bytes 524288 | tf_op jit(solution)/shard_map/all_to_all | solution.py:542
  78.0 1.9 %collective-permute-start.11 = (bf16[8,192,128]{2,1,0:T(8,128)(2,1)S(1)}, bf16[8,192,128]{2,1,0:T(8,128)(2,1)S(1)}, u32[]{:S(2)}, u32[]{:S(2)}) collective-permute-start(bf16[8,192,128]{2,1,0:T(8,128)(2,1)S(1)} %copy-done.8), channel_id=1, source_target_pairs={{0,16},{16,0},{1,17},{17,1},{2,18},{18,2},{3,19},{19,3},{4,20},{20... | collective-permute-start | bytes 1179656 | tf_op jit(solution)/shard_map/ppermute | solution.py:589
  81.3 16.1 %collective-permute-start.12 = (bf16[2,16,32,128]{3,2,1,0:T(8,128)(2,1)}, bf16[2,16,32,128]{3,2,1,0:T(8,128)(2,1)}, u32[]{:S(2)}, u32[]{:S(2)}) collective-permute-start(bf16[2,16,32,128]{3,2,1,0:T(8,128)(2,1)} %get-tuple-element.47), channel_id=1, source_target_pairs={{0,64},{64,128},{128,192},{192,0},{1,65},{65,129},{129,193},{193,1... | collective-permute-start | bytes 786440 | tf_op jit(solution)/shard_map/ppermute | solution.py:592
  81.3 16.1 %collective-permute-start.13 = (bf16[2,16,32,128]{3,2,1,0:T(8,128)(2,1)S(1)}, bf16[2,16,32,128]{3,2,1,0:T(8,128)(2,1)}, u32[]{:S(2)}, u32[]{:S(2)}) collective-permute-start(bf16[2,16,32,128]{3,2,1,0:T(8,128)(2,1)S(1)} %get-tuple-element.48), channel_id=1, source_target_pairs={{0,128},{64,192},{128,0},{192,64},{1,129},{65,193},{129,1},{193,65... | collective-permute-start | bytes 786440 | tf_op jit(solution)/shard_map/ppermute | solution.py:592
  83.4 14.1 %collective-permute-start.14 = (bf16[2,16,32,128]{3,2,1,0:T(8,128)(2,1)S(1)}, bf16[2,16,32,128]{3,2,1,0:T(8,128)(2,1)}, u32[]{:S(2)}, u32[]{:S(2)}) collective-permute-start(bf16[2,16,32,128]{3,2,1,0:T(8,128)(2,1)S(1)} %get-tuple-element.49), channel_id=1, source_target_pairs={{0,192},{64,0},{128,64},{192,128},{1,193},{65,1},{129,65},{193,129... | collective-permute-start | bytes 786440 | tf_op jit(solution)/shard_map/ppermute | solution.py:592
  93.8 13.6 %all-to-all-start.3 = ((bf16[16,96,128]{2,1,0:T(8,128)(2,1)}), bf16[16,96,128]{2,1,0:T(8,128)(2,1)S(1)}, u32[]{:S(2)}, u32[]{:S(2)}) async-start(bf16[16,96,128]{2,1,0:T(8,128)(2,1)} %backward.1), calls=%async_computation.3 | async-start | bytes 786432 | tf_op jit(solution)/shard_map/all_to_all | solution.py:542
  98.6 8.8 %collective-permute-start.15 = (bf16[16,32,128]{2,1,0:T(8,128)(2,1)S(1)}, bf16[16,32,128]{2,1,0:T(8,128)(2,1)S(1)}, u32[]{:S(2)}, u32[]{:S(2)}) collective-permute-start(bf16[16,32,128]{2,1,0:T(8,128)(2,1)S(1)} %fusion), channel_id=1, source_target_pairs={{0,32},{32,0},{1,33},{33,1},{2,34},{34,2},{3,35},{35,3},{4,36},{36... | collective-permute-start | bytes 393224 | tf_op jit(solution)/shard_map/ppermute | solution.py:596
  108.2 19.0 %all-to-all-start.4 = ((bf16[16,64,128]{2,1,0:T(8,128)(2,1)}), bf16[16,64,128]{2,1,0:T(8,128)(2,1)S(1)}, u32[]{:S(2)}, u32[]{:S(2)}) async-start(bf16[16,64,128]{2,1,0:T(8,128)(2,1)} %collect.1), calls=%async_computation.4 | async-start | bytes 524288 | tf_op jit(solution)/shard_map/all_to_all | solution.py:542
  (6 other events, 41.0 us)

commit v7 on v6

--- a/solution.py
+++ b/solution.py
@@ -25,7 +25,7 @@
 PAD = 8
 LANES = 256
 BLOCK = 128
-EARLY = D // 4
+EARLY = D // 8
 LATE = (D - EARLY) // BLOCK * ROWS
 QKV = HS + HALF
 EXTRA = 16

time: 129 us -> 128 us (level)
  transfers between devices with their start and end apart: 21 -> 21, of which waited for: 13 -> 12; matrix products, arithmetic and copies ran while one was open for 2% -> 2% of each run, Pallas kernels for 7% -> 7%
where the time goes in v7:
time: 128 us; the launch traced here: 127 us
  starting transfers between devices  53.6 us (42%)
  waiting for transfers between devices  42.2 us (33%)
  Pallas kernels  21.5 us (17%)
  blocking collectives  6.58 us (5%)
  other arithmetic  2.26 us (2%)
    all_to_all x5, starting transfers between devices, swap(): return lax.all_to_all(array, axes, 0, 0, tiled=True)  36.7 us
    all_to_all x5, waiting for transfers between devices, swap(): return lax.all_to_all(array, axes, 0, 0, tiled=True)  20 us
    ppermute x3, waiting for transfers between devices, per_device(): lax.ppermute(near, 'x', [(i, (i + r) % XS) for i in range(XS)])  12.1 us
    ppermute x1, waiting for transfers between devices, per_device(): other = lax.ppermute(other, 'y_lo', [(0, 1), (1, 0)])  5.94 us
    ppermute x3, starting transfers between devices, per_device(): lax.ppermute(pair, 'x', [(i, (i + r) % XS) for i in range(XS)])  5.65 us
    pallas_call x1, Pallas kernels, decoder(): call(decoder_kernel, 'decoder', 5, [((KMAX, D), BF16), ((H, HS, KMAX), BF...  5.15 us
    pallas_call x1, Pallas kernels, forward(): call(forward_kernel, 'forward', 0.1, [((COPIES, HS + LATE, KMAX), BF16),...  4.7 us
    all_gather x1, blocking collectives, per_device(): pair = lax.all_gather(weights, 'y_lo', axis=0)  4.49 us
  transfers between devices with their start and end apart: 21, of which 12 were waited for; matrix products, arithmetic and copies ran while one was open for 2% of the time, Pallas kernels for 7%

profile of v7, /device:TPU:32, one launch (start us, length us, event | category | flops | bytes accessed | tf_op | source)
XLA Modules:
  0.0 127.1 jit_solution(4079750304098124205)
XLA Ops:
  0.6 1.8 %pack.1 = (bf16[16,16,1280]{2,1,0:T(8,128)(2,1)}, bf16[16,128]{1,0:T(8,128)(2,1)S(1)}, bf16[96,128]{1,0:T(8,128)(2,1)S(1)}) custom-call(s32[1,1,256]{2,1,0:T(1,128)} %slots_hbm.1, bf16[1,16,1024]{2,1,0:T(8,128)(2,1)} %frames_hbm.1, bf16[1,16,1024]{2,1,0:T(8,128)(2,1)} %targets_ref.1, s32[1,1,128]{2,1,0:T(1,128)} %index_hbm.1, bf16[64,3072]{1,0:T(8,128)(2,1)} %w_ref.1), custom_call_target="tpu_custom_call" | custom-call | flops 1000000000 | bytes 1024 | tf_op jit(solution)/shard_map/pack/pallas_call | solution.py:143
  2.4 11.4 %all-to-all-start = ((bf16[16,16,1280]{2,1,0:T(8,128)(2,1)}), bf16[16,16,1280]{2,1,0:T(8,128)(2,1)S(1)}, u32[]{:S(2)}, u32[]{:S(2)}) async-start(bf16[16,16,1280]{2,1,0:T(8,128)(2,1)} %get-tuple-element.30), calls=%async_computation | async-start | bytes 1310720 | tf_op jit(solution)/shard_map/all_to_all | solution.py:542
  13.8 4.5 %all-gather = bf16[192,128]{1,0:T(8,128)(2,1)S(1)} all-gather(bf16[96,128]{1,0:T(8,128)(2,1)S(1)} %get-tuple-element.31), channel_id=2, replica_groups=mesh['x'=4,'y_lo'=2,'core'=2,'z'=8,'y_hi'=2] {'y_lo'}, dimensions={0}, use_global_device_ids=true | all-gather | bytes 73728 | tf_op jit(solution)/shard_map/all_gather | solution.py:567
  19.8 2.7 %collective-permute-start.1 = (bf16[2,96,128]{2,1,0:T(8,128)(2,1)S(1)}, bf16[2,96,128]{2,1,0:T(8,128)(2,1)S(1)}, u32[]{:S(2)}, u32[]{:S(2)}) collective-permute-start(bf16[2,96,128]{2,1,0:T(8,128)(2,1)S(1)} %bitcast.20), channel_id=1, source_target_pairs={{0,128},{64,192},{128,0},{192,64},{1,129},{65,193},{129,1},{193,65... | collective-permute-start | bytes 147464 | tf_op jit(solution)/shard_map/ppermute | solution.py:569
  26.6 2.1 %all-gather.1 = bf16[8,2,96,128]{3,2,1,0:T(8,128)(2,1)S(1)} all-gather(bf16[4,2,96,128]{3,2,1,0:T(8,128)(2,1)S(1)} %pad_maximum_fusion.1), channel_id=3, replica_groups=mesh['x'=4,'y_lo'=2,'core'=2,'z'=8,'y_hi'=2] {'core'}, dimensions={0}, use_global_device_ids=true | all-gather | bytes 589824 | tf_op jit(solution)/shard_map/all_gather | solution.py:571
  29.8 2.8 %all-to-all-done = bf16[16,16,1280]{2,1,0:T(8,128)(2,1)S(1)} async-done(((bf16[16,16,1280]{2,1,0:T(8,128)(2,1)}), bf16[16,16,1280]{2,1,0:T(8,128)(2,1)S(1)}, u32[]{:S(2)}, u32[]{:S(2)}) %all-to-all-start) | async-done | bytes 655392 | tf_op jit(solution)/shard_map/all_to_all | solution.py:542
  32.6 4.7 %forward.1 = (bf16[16,176,128]{2,1,0:T(8,128)(2,1)}, f32[16,128,128]{2,1,0:T(8,128)}, bf16[256,2048]{1,0:T(8,128)(2,1)}, bf16[16,192,128]{2,1,0:T(8,128)(2,1)}) custom-call(bf16[256,1280]{1,0:T(8,128)(2,1)S(1)} %bitcast.15, bf16[2,4,2,96,128]{4,3,2,1,0:T(8,128)(2,1)S(1)} %bitcast.18, f32[1,1024]{1,0:T(1,128)} %bitcast.28, bf16[1,16,1024]{2,1,0:T(8,128)(2,1)S(1)} %copy-done), custom_call_target="tpu_custom_call" | custom-call | flops 100000000 | bytes 1024 | tf_op jit(solution)/shard_map/forward/pallas_call | solution.py:229
  37.3 6.5 %all-to-all-start.1 = ((bf16[16,176,128]{2,1,0:T(8,128)(2,1)}), bf16[16,176,128]{2,1,0:T(8,128)(2,1)S(1)}, u32[]{:S(2)}, u32[]{:S(2)}) async-start(bf16[16,176,128]{2,1,0:T(8,128)(2,1)} %get-tuple-element.34), calls=%async_computation.1 | async-start | bytes 1441792 | tf_op jit(solution)/shard_map/all_to_all | solution.py:542
  43.8 2.2 %collective-permute-start.6 = (bf16[2,64,1024]{2,1,0:T(8,128)(2,1)S(1)}, bf16[2,64,1024]{2,1,0:T(8,128)(2,1)S(1)}, u32[]{:S(2)}, u32[]{:S(2)}) collective-permute-start(bf16[2,64,1024]{2,1,0:T(8,128)(2,1)S(1)} %pad_maximum_fusion.refs_0_), channel_id=1, source_target_pairs={{0,192},{64,0},{128,64},{192,128},{1,193},{65,1},{129,65},{193,129... | collective-permute-start | bytes 786440 | tf_op jit(solution)/shard_map/ppermute | solution.py:582
  46.0 2.3 %collective-permute-start.5 = (bf16[2,64,1024]{2,1,0:T(8,128)(2,1)S(1)}, bf16[2,64,1024]{2,1,0:T(8,128)(2,1)S(1)}, u32[]{:S(2)}, u32[]{:S(2)}) collective-permute-start(bf16[2,64,1024]{2,1,0:T(8,128)(2,1)S(1)} %pad_maximum_fusion.refs_0_), channel_id=1, source_target_pairs={{0,128},{64,192},{128,0},{192,64},{1,129},{65,193},{129,1},{193,65... | collective-permute-start | bytes 786440 | tf_op jit(solution)/shard_map/ppermute | solution.py:582
  48.3 8.7 %collective-permute-done.6.refs_3_ = bf16[2,64,1024]{2,1,0:T(8,128)(2,1)S(1)} collective-permute-done((bf16[2,64,1024]{2,1,0:T(8,128)(2,1)S(1)}, bf16[2,64,1024]{2,1,0:T(8,128)(2,1)S(1)}, u32[]{:S(2)}, u32[]{:S(2)}) %collective-permute-start.6) | collective-permute-done | bytes 262176 | tf_op jit(solution)/shard_map/ppermute | solution.py:582
  57.0 3.4 %collective-permute-done.4.refs_1_ = bf16[2,64,1024]{2,1,0:T(8,128)(2,1)S(1)} collective-permute-done((bf16[2,64,1024]{2,1,0:T(8,128)(2,1)S(1)}, bf16[2,64,1024]{2,1,0:T(8,128)(2,1)S(1)}, u32[]{:S(2)}, u32[]{:S(2)}) %collective-permute-start.4) | collective-permute-done | bytes 262176 | tf_op jit(solution)/shard_map/ppermute | solution.py:582
  62.2 1.9 %all-to-all-done.1.recv_ref = bf16[16,176,128]{2,1,0:T(8,128)(2,1)S(1)} async-done(((bf16[16,176,128]{2,1,0:T(8,128)(2,1)}), bf16[16,176,128]{2,1,0:T(8,128)(2,1)S(1)}, u32[]{:S(2)}, u32[]{:S(2)}) %all-to-all-start.1) | async-done | bytes 720928 | tf_op jit(solution)/shard_map/all_to_all | solution.py:542
  64.1 5.2 %decoder.1 = (bf16[128,1024]{1,0:T(8,128)(2,1)}, bf16[16,64,128]{2,1,0:T(8,128)(2,1)}, bf16[16,64,128]{2,1,0:T(8,128)(2,1)}, bf16[128,1024]{1,0:T(8,128)(2,1)}, bf16[8,192,128]{2,1,0:T(8,128)(2,1)}) custom-call(bf16[16,176,128]{2,1,0:T(8,128)(2,1)S(1)} %all-to-all-done.1.recv_ref, bf16[256,1280]{1,0:T(8,128)(2,1)S(1)} %bitcast.16, ...), custom_call_target="tpu_custom_call" | custom-call | flops 5000000000 | bytes 1024 | tf_op jit(solution)/shard_map/decoder/pallas_call | solution.py:368
  69.3 7.9 %all-to-all-start.2 = ((bf16[16,64,128]{2,1,0:T(8,128)(2,1)}), bf16[16,64,128]{2,1,0:T(8,128)(2,1)S(1)}, u32[]{:S(2)}, u32[]{:S(2)}) async-start(bf16[16,64,128]{2,1,0:T(8,128)(2,1)} %get-tuple-element.39), calls=%async_computation.2 | async-start | bytes 524288 | tf_op jit(solution)/shard_map/all_to_all | solution.py:542
  77.3 1.8 %prepare.1.normed_hbm = bf16[1024,256]{1,0:T(8,128)(2,1)} custom-call(bf16[256,1280]{1,0:T(8,128)(2,1)S(1)} %bitcast.17, f32[1,1024]{1,0:T(1,128)} %bitcast.29), custom_call_target="tpu_custom_call" | custom-call | flops 2000000000 | bytes 1024 | tf_op jit(solution)/shard_map/prepare/pallas_call | solution.py:261
  80.2 2.1 %collective-permute-start.13 = (bf16[2,16,32,128]{3,2,1,0:T(8,128)(2,1)S(1)}, bf16[2,16,32,128]{3,2,1,0:T(8,128)(2,1)}, u32[]{:S(2)}, u32[]{:S(2)}) collective-permute-start(bf16[2,16,32,128]{3,2,1,0:T(8,128)(2,1)S(1)} %get-tuple-element.48), channel_id=1, source_target_pairs={{0,128},{64,192},{128,0},{192,64},{1,129},{65,193},{129,1},{193,65... | collective-permute-start | bytes 786440 | tf_op jit(solution)/shard_map/ppermute | solution.py:592
  83.5 5.6 %all-to-all-done.2.dctx_ref = bf16[16,64,128]{2,1,0:T(8,128)(2,1)S(1)} async-done(((bf16[16,64,128]{2,1,0:T(8,128)(2,1)}), bf16[16,64,128]{2,1,0:T(8,128)(2,1)S(1)}, u32[]{:S(2)}, u32[]{:S(2)}) %all-to-all-start.2) | async-done | bytes 262176 | tf_op jit(solution)/shard_map/all_to_all | solution.py:542
  89.1 3.9 %backward.1 = bf16[16,96,128]{2,1,0:T(8,128)(2,1)} custom-call(bf16[16,64,128]{2,1,0:T(8,128)(2,1)S(1)} %all-to-all-done.2.dctx_ref, f32[16,128,128]{2,1,0:T(8,128)S(1)} %copy-done.1, bf16[256,2048]{1,0:T(8,128)(2,1)} %get-tuple-element.41.pick_hbm, bf16[16,192,128]{2,1,0:T(8,128)(2,1)S(1)} %copy-done.2, bf16[1024,256]{1,0:T(8,128)(2,1)} %prepare.1.normed_hbm), custom_call_target="tpu_custom_call" | custom-call | flops 5000000000 | bytes 1024 | tf_op jit(solution)/shard_map/backward/pallas_call | solution.py:462
  93.0 3.6 %all-to-all-start.3 = ((bf16[16,96,128]{2,1,0:T(8,128)(2,1)}), bf16[16,96,128]{2,1,0:T(8,128)(2,1)S(1)}, u32[]{:S(2)}, u32[]{:S(2)}) async-start(bf16[16,96,128]{2,1,0:T(8,128)(2,1)} %backward.1), calls=%async_computation.3 | async-start | bytes 786432 | tf_op jit(solution)/shard_map/all_to_all | solution.py:542
  97.7 1.9 %collective-permute-start.15 = (bf16[16,32,128]{2,1,0:T(8,128)(2,1)S(1)}, bf16[16,32,128]{2,1,0:T(8,128)(2,1)S(1)}, u32[]{:S(2)}, u32[]{:S(2)}) collective-permute-start(bf16[16,32,128]{2,1,0:T(8,128)(2,1)S(1)} %fusion), channel_id=1, source_target_pairs={{0,32},{32,0},{1,33},{33,1},{2,34},{34,2},{3,35},{35,3},{4,36},{36... | collective-permute-start | bytes 393224 | tf_op jit(solution)/shard_map/ppermute | solution.py:596
  100.7 5.9 %collective-permute-done.15.other_ref = bf16[16,32,128]{2,1,0:T(8,128)(2,1)S(1)} collective-permute-done((bf16[16,32,128]{2,1,0:T(8,128)(2,1)S(1)}, bf16[16,32,128]{2,1,0:T(8,128)(2,1)S(1)}, u32[]{:S(2)}, u32[]{:S(2)}) %collective-permute-start.15) | collective-permute-done | bytes 131104 | tf_op jit(solution)/shard_map/ppermute | solution.py:596
  107.5 7.4 %all-to-all-start.4 = ((bf16[16,64,128]{2,1,0:T(8,128)(2,1)}), bf16[16,64,128]{2,1,0:T(8,128)(2,1)S(1)}, u32[]{:S(2)}, u32[]{:S(2)}) async-start(bf16[16,64,128]{2,1,0:T(8,128)(2,1)} %collect.1), calls=%async_computation.4 | async-start | bytes 524288 | tf_op jit(solution)/shard_map/all_to_all | solution.py:542
  116.6 9.8 %all-to-all-done.4.last_ref = bf16[16,64,128]{2,1,0:T(8,128)(2,1)S(1)} async-done(((bf16[16,64,128]{2,1,0:T(8,128)(2,1)}), bf16[16,64,128]{2,1,0:T(8,128)(2,1)S(1)}, u32[]{:S(2)}, u32[]{:S(2)}) %all-to-all-start.4) | async-done | bytes 262176 | tf_op jit(solution)/shard_map/all_to_all | solution.py:542
  (52 shorter events, 16.4 us)
Async XLA Ops:
  2.4 21.5 %copy-start.6 = (bf16[64,1024]{1,0:T(8,128)(2,1)S(1)}, bf16[64,1024]{1,0:T(8,128)(2,1)}, u32[]{:S(2)}) copy-start(bf16[64,1024]{1,0:T(8,128)(2,1)} %param.16) | copy-start | bytes 393220
  2.4 30.1 %all-to-all-start = ((bf16[16,16,1280]{2,1,0:T(8,128)(2,1)}), bf16[16,16,1280]{2,1,0:T(8,128)(2,1)S(1)}, u32[]{:S(2)}, u32[]{:S(2)}) async-start(bf16[16,16,1280]{2,1,0:T(8,128)(2,1)} %get-tuple-element.30), calls=%async_computation | async-start | bytes 1310720 | tf_op jit(solution)/shard_map/all_to_all | solution.py:542
  18.3 6.6 %collective-permute-start = (bf16[2,96,128]{2,1,0:T(8,128)(2,1)S(1)}, bf16[2,96,128]{2,1,0:T(8,128)(2,1)S(1)}, u32[]{:S(2)}, u32[]{:S(2)}) collective-permute-start(bf16[2,96,128]{2,1,0:T(8,128)(2,1)S(1)} %bitcast.19), channel_id=1, source_target_pairs={{0,64},{64,128},{128,192},{192,0},{1,65},{65,129},{129,193},{193,1... | collective-permute-start | bytes 147464 | tf_op jit(solution)/shard_map/ppermute | solution.py:569
  19.8 5.6 %collective-permute-start.1 = (bf16[2,96,128]{2,1,0:T(8,128)(2,1)S(1)}, bf16[2,96,128]{2,1,0:T(8,128)(2,1)S(1)}, u32[]{:S(2)}, u32[]{:S(2)}) collective-permute-start(bf16[2,96,128]{2,1,0:T(8,128)(2,1)S(1)} %bitcast.20), channel_id=1, source_target_pairs={{0,128},{64,192},{128,0},{192,64},{1,129},{65,193},{129,1},{193,65... | collective-permute-start | bytes 147464 | tf_op jit(solution)/shard_map/ppermute | solution.py:569
  22.5 4.1 %collective-permute-start.2 = (bf16[2,96,128]{2,1,0:T(8,128)(2,1)S(1)}, bf16[2,96,128]{2,1,0:T(8,128)(2,1)S(1)}, u32[]{:S(2)}, u32[]{:S(2)}) collective-permute-start(bf16[2,96,128]{2,1,0:T(8,128)(2,1)S(1)} %bitcast.21), channel_id=1, source_target_pairs={{0,192},{64,0},{128,64},{192,128},{1,193},{65,1},{129,65},{193,129... | collective-permute-start | bytes 147464 | tf_op jit(solution)/shard_map/ppermute | solution.py:569
  23.9 5.9 %collective-permute-start.3 = (bf16[64,1024]{1,0:T(8,128)(2,1)S(1)}, bf16[64,1024]{1,0:T(8,128)(2,1)S(1)}, u32[]{:S(2)}, u32[]{:S(2)}) collective-permute-start(bf16[64,1024]{1,0:T(8,128)(2,1)S(1)} %copy-done.6), channel_id=1, source_target_pairs={{0,32},{32,0},{1,33},{33,1},{2,34},{34,2},{3,35},{35,3},{4,36},{36... | collective-permute-start | bytes 393224 | tf_op jit(solution)/shard_map/ppermute | solution.py:573
  37.3 26.9 %all-to-all-start.1 = ((bf16[16,176,128]{2,1,0:T(8,128)(2,1)}), bf16[16,176,128]{2,1,0:T(8,128)(2,1)S(1)}, u32[]{:S(2)}, u32[]{:S(2)}) async-start(bf16[16,176,128]{2,1,0:T(8,128)(2,1)} %get-tuple-element.34), calls=%async_computation.1 | async-start | bytes 1441792 | tf_op jit(solution)/shard_map/all_to_all | solution.py:542
  43.8 17.1 %copy-start.7 = (bf16[1024]{0:T(1024)(128)(2,1)S(1)}, bf16[1024]{0:T(1024)(128)(2,1)}, u32[]{:S(2)}) copy-start(bf16[1024]{0:T(1024)(128)(2,1)} %param.17) | copy-start | bytes 6148
  43.8 20.4 %copy-start.3 = (f32[7,1024]{1,0:T(8,128)S(1)}, f32[7,1024]{1,0:T(8,128)}, u32[]{:S(2)}) copy-start(f32[7,1024]{1,0:T(8,128)} %taps_ref.1) | copy-start | bytes 86020
  43.8 13.1 %collective-permute-start.6 = (bf16[2,64,1024]{2,1,0:T(8,128)(2,1)S(1)}, bf16[2,64,1024]{2,1,0:T(8,128)(2,1)S(1)}, u32[]{:S(2)}, u32[]{:S(2)}) collective-permute-start(bf16[2,64,1024]{2,1,0:T(8,128)(2,1)S(1)} %pad_maximum_fusion.refs_0_), channel_id=1, source_target_pairs={{0,192},{64,0},{128,64},{192,128},{1,193},{65,1},{129,65},{193,129... | collective-permute-start | bytes 786440 | tf_op jit(solution)/shard_map/ppermute | solution.py:582
  46.0 14.3 %collective-permute-start.4 = (bf16[2,64,1024]{2,1,0:T(8,128)(2,1)S(1)}, bf16[2,64,1024]{2,1,0:T(8,128)(2,1)S(1)}, u32[]{:S(2)}, u32[]{:S(2)}) collective-permute-start(bf16[2,64,1024]{2,1,0:T(8,128)(2,1)S(1)} %pad_maximum_fusion.refs_0_), channel_id=1, source_target_pairs={{0,64},{64,128},{128,192},{192,0},{1,65},{65,129},{129,193},{193,1... | collective-permute-start | bytes 786440 | tf_op jit(solution)/shard_map/ppermute | solution.py:582
  46.0 14.3 %collective-permute-start.5 = (bf16[2,64,1024]{2,1,0:T(8,128)(2,1)S(1)}, bf16[2,64,1024]{2,1,0:T(8,128)(2,1)S(1)}, u32[]{:S(2)}, u32[]{:S(2)}) collective-permute-start(bf16[2,64,1024]{2,1,0:T(8,128)(2,1)S(1)} %pad_maximum_fusion.refs_0_), channel_id=1, source_target_pairs={{0,128},{64,192},{128,0},{192,64},{1,129},{65,193},{129,1},{193,65... | collective-permute-start | bytes 786440 | tf_op jit(solution)/shard_map/ppermute | solution.py:582
  48.3 12.6 %collective-permute-start.7 = (bf16[2,64,1024]{2,1,0:T(8,128)(2,1)S(1)}, bf16[2,64,1024]{2,1,0:T(8,128)(2,1)S(1)}, u32[]{:S(2)}, u32[]{:S(2)}) collective-permute-start(bf16[2,64,1024]{2,1,0:T(8,128)(2,1)S(1)} %pad_maximum_fusion.refs_0_), channel_id=1, source_target_pairs={{0,16},{16,0},{1,17},{17,1},{2,18},{18,2},{3,19},{19,3},{4,20},{20... | collective-permute-start | bytes 786440 | tf_op jit(solution)/shard_map/ppermute | solution.py:583
  57.0 3.9 %collective-permute-start.10 = (bf16[2,64,1024]{2,1,0:T(8,128)(2,1)S(1)}, bf16[2,64,1024]{2,1,0:T(8,128)(2,1)S(1)}, u32[]{:S(2)}, u32[]{:S(2)}) collective-permute-start(bf16[2,64,1024]{2,1,0:T(8,128)(2,1)S(1)} %collective-permute-done.6.refs_3_), channel_id=1, source_target_pairs={{0,16},{16,0},{1,17},{17,1},{2,18},{18,2},{3,19},{19,3},{4,20},{20... | collective-permute-start | bytes 786440 | tf_op jit(solution)/shard_map/ppermute | solution.py:583
  60.3 1.5 %collective-permute-start.8 = (bf16[2,64,1024]{2,1,0:T(8,128)(2,1)S(1)}, bf16[2,64,1024]{2,1,0:T(8,128)(2,1)S(1)}, u32[]{:S(2)}, u32[]{:S(2)}) collective-permute-start(bf16[2,64,1024]{2,1,0:T(8,128)(2,1)S(1)} %collective-permute-done.4.refs_1_), channel_id=1, source_target_pairs={{0,16},{16,0},{1,17},{17,1},{2,18},{18,2},{3,19},{19,3},{4,20},{20... | collective-permute-start | bytes 786440 | tf_op jit(solution)/shard_map/ppermute | solution.py:583
  60.3 1.9 %collective-permute-start.9 = (bf16[2,64,1024]{2,1,0:T(8,128)(2,1)S(1)}, bf16[2,64,1024]{2,1,0:T(8,128)(2,1)S(1)}, u32[]{:S(2)}, u32[]{:S(2)}) collective-permute-start(bf16[2,64,1024]{2,1,0:T(8,128)(2,1)S(1)} %collective-permute-done.5.refs_2_), channel_id=1, source_target_pairs={{0,16},{16,0},{1,17},{17,1},{2,18},{18,2},{3,19},{19,3},{4,20},{20... | collective-permute-start | bytes 786440 | tf_op jit(solution)/shard_map/ppermute | solution.py:583
  69.3 19.8 %all-to-all-start.2 = ((bf16[16,64,128]{2,1,0:T(8,128)(2,1)}), bf16[16,64,128]{2,1,0:T(8,128)(2,1)S(1)}, u32[]{:S(2)}, u32[]{:S(2)}) async-start(bf16[16,64,128]{2,1,0:T(8,128)(2,1)} %get-tuple-element.39), calls=%async_computation.2 | async-start | bytes 524288 | tf_op jit(solution)/shard_map/all_to_all | solution.py:542
  77.2 1.9 %collective-permute-start.11 = (bf16[8,192,128]{2,1,0:T(8,128)(2,1)S(1)}, bf16[8,192,128]{2,1,0:T(8,128)(2,1)S(1)}, u32[]{:S(2)}, u32[]{:S(2)}) collective-permute-start(bf16[8,192,128]{2,1,0:T(8,128)(2,1)S(1)} %copy-done.8), channel_id=1, source_target_pairs={{0,16},{16,0},{1,17},{17,1},{2,18},{18,2},{3,19},{19,3},{4,20},{20... | collective-permute-start | bytes 1179656 | tf_op jit(solution)/shard_map/ppermute | solution.py:589
  80.1 16.5 %collective-permute-start.12 = (bf16[2,16,32,128]{3,2,1,0:T(8,128)(2,1)S(1)}, bf16[2,16,32,128]{3,2,1,0:T(8,128)(2,1)}, u32[]{:S(2)}, u32[]{:S(2)}) collective-permute-start(bf16[2,16,32,128]{3,2,1,0:T(8,128)(2,1)S(1)} %get-tuple-element.47), channel_id=1, source_target_pairs={{0,64},{64,128},{128,192},{192,0},{1,65},{65,129},{129,193},{193,1... | collective-permute-start | bytes 786440 | tf_op jit(solution)/shard_map/ppermute | solution.py:592
  80.2 16.4 %collective-permute-start.13 = (bf16[2,16,32,128]{3,2,1,0:T(8,128)(2,1)S(1)}, bf16[2,16,32,128]{3,2,1,0:T(8,128)(2,1)}, u32[]{:S(2)}, u32[]{:S(2)}) collective-permute-start(bf16[2,16,32,128]{3,2,1,0:T(8,128)(2,1)S(1)} %get-tuple-element.48), channel_id=1, source_target_pairs={{0,128},{64,192},{128,0},{192,64},{1,129},{65,193},{129,1},{193,65... | collective-permute-start | bytes 786440 | tf_op jit(solution)/shard_map/ppermute | solution.py:592
  82.3 14.3 %collective-permute-start.14 = (bf16[2,16,32,128]{3,2,1,0:T(8,128)(2,1)S(1)}, bf16[2,16,32,128]{3,2,1,0:T(8,128)(2,1)}, u32[]{:S(2)}, u32[]{:S(2)}) collective-permute-start(bf16[2,16,32,128]{3,2,1,0:T(8,128)(2,1)S(1)} %get-tuple-element.49), channel_id=1, source_target_pairs={{0,192},{64,0},{128,64},{192,128},{1,193},{65,1},{129,65},{193,129... | collective-permute-start | bytes 786440 | tf_op jit(solution)/shard_map/ppermute | solution.py:592
  93.0 13.6 %all-to-all-start.3 = ((bf16[16,96,128]{2,1,0:T(8,128)(2,1)}), bf16[16,96,128]{2,1,0:T(8,128)(2,1)S(1)}, u32[]{:S(2)}, u32[]{:S(2)}) async-start(bf16[16,96,128]{2,1,0:T(8,128)(2,1)} %backward.1), calls=%async_computation.3 | async-start | bytes 786432 | tf_op jit(solution)/shard_map/all_to_all | solution.py:542
  97.7 8.9 %collective-permute-start.15 = (bf16[16,32,128]{2,1,0:T(8,128)(2,1)S(1)}, bf16[16,32,128]{2,1,0:T(8,128)(2,1)S(1)}, u32[]{:S(2)}, u32[]{:S(2)}) collective-permute-start(bf16[16,32,128]{2,1,0:T(8,128)(2,1)S(1)} %fusion), channel_id=1, source_target_pairs={{0,32},{32,0},{1,33},{33,1},{2,34},{34,2},{3,35},{35,3},{4,36},{36... | collective-permute-start | bytes 393224 | tf_op jit(solution)/shard_map/ppermute | solution.py:596
  107.5 18.9 %all-to-all-start.4 = ((bf16[16,64,128]{2,1,0:T(8,128)(2,1)}), bf16[16,64,128]{2,1,0:T(8,128)(2,1)S(1)}, u32[]{:S(2)}, u32[]{:S(2)}) async-start(bf16[16,64,128]{2,1,0:T(8,128)(2,1)} %collect.1), calls=%async_computation.4 | async-start | bytes 524288 | tf_op jit(solution)/shard_map/all_to_all | solution.py:542
  (6 other events, 37.5 us)
